TPU v7x, 128 devices: a whole 4x4x4 slice. The times are simulated.
128 devices in a mesh: row: 16 (over z_lo, y, core), col: 8 (over x, z_hi).
Axes of the slice: x: 4, y: 4, z: 4 (z_hi: 2, z_lo: 2; z = z_hi * 2 + z_lo), core: 2. Of those that a mesh axis runs over, the one named last changes fastest.
Arguments:
- homolog_features: bfloat16 [1024, 128, 256], P('row', 'col'), may hold values from -6 to 6
- pair_input: bfloat16 [128, 128, 128], P('row', 'col'), may hold values from -6 to 6
- cotangent: bfloat16 [128, 128, 128], P('row', 'col'), may hold values from -6 to 6
- homolog_factor_matrix: bfloat16 [256, 64], replicated, may hold values from -0.375 to 0.375
- outer_output_weight: bfloat16 [1024, 128], replicated, may hold values from -6 to 6
- outgoing_input_weight: bfloat16 [128, 640], replicated, may hold values from -0.5 to 0.5
- outgoing_output_weight: bfloat16 [128, 128], replicated, may hold values from -0.5 to 0.5
- incoming_input_weight: bfloat16 [128, 640], replicated, may hold values from -0.5 to 0.5
- incoming_output_weight: bfloat16 [128, 128], replicated, may hold values from -0.5 to 0.5
Outputs:
- pair_output: bfloat16 [128, 128, 128], P('row', 'col')
- pair_input_gradient: float32 [128, 128, 128], P('row', 'col')
- alignment_gradient: float32 [1024, 128, 256], P('row', 'col')
All inputs are finite; a program needn't handle non-finite values.
Results may differ from a plain program's by a relative error of at most 0.025.
Values may be sent and summed in bfloat16 or wider, within the bound.
A program may use at most 64 MiB of HBM per device.

v0:
```python
import math

import jax
import jax.numpy as jnp
from jax import lax
from jax.sharding import PartitionSpec as P

HOMOLOG_TOTAL = 1024


EPSILON = 1e-05


def shortened(array):
    return jax.tree.map(lambda a: a.astype(jnp.bfloat16) if a.dtype == jnp.float32 else a, array)


def broadcast(array, axis, root):
    mine = lax.axis_index(axis) == root
    return lax.psum(jnp.where(mine, array, jnp.zeros_like(array)), axis)


def normalize_layer(inputs):
    average = jnp.mean(inputs, axis=-1, keepdims=True)
    centered = inputs - average
    spread = jnp.mean(centered * centered, axis=-1, keepdims=True)
    return centered * lax.rsqrt(spread + EPSILON)


def norm_backprop(inputs, upstream):
    unused, pullback = jax.vjp(normalize_layer, inputs)
    return pullback(upstream)[0]


def gated_factor(projected_input, channels):
    return (
        jax.nn.sigmoid(projected_input[..., :channels])
        * projected_input[..., channels : 2 * channels]
    ).astype(jnp.bfloat16)


def gated_pairs(projected_input, channels):
    return (
        gated_factor(projected_input, channels),
        gated_factor(projected_input[..., 2 * channels :], channels),
    )


def triangle_inputs(pair_map, weight_in):
    normalized = normalize_layer(pair_map.astype(jnp.float32)).astype(jnp.bfloat16)
    projected_input = jnp.dot(normalized, weight_in, preferred_element_type=jnp.float32)
    return (normalized, projected_input)


def triangle_output(pair_map, projected_input, mixing, weight_out):
    channels = weight_out.shape[1]
    gating = jax.nn.sigmoid(projected_input[..., 4 * channels :])
    mixing_normed = normalize_layer(mixing).astype(jnp.bfloat16)
    update = jnp.dot(mixing_normed, weight_out, preferred_element_type=jnp.float32)
    return (pair_map.astype(jnp.float32) + gating * update).astype(jnp.bfloat16)


def output_pullback(projected_input, mixing, weight_out, upstream):
    channels = weight_out.shape[1]
    gating = jax.nn.sigmoid(projected_input[..., 4 * channels :])
    mixing_normed = normalize_layer(mixing).astype(jnp.bfloat16)
    update = jnp.dot(mixing_normed, weight_out, preferred_element_type=jnp.float32)
    update_cot = (upstream * gating).astype(jnp.bfloat16)
    normalized_gradient = jnp.dot(update_cot, weight_out.T, preferred_element_type=jnp.float32)
    mixing_cot = norm_backprop(mixing, normalized_gradient).astype(jnp.bfloat16)
    gating_cot = upstream * update * gating * (1.0 - gating)
    return (mixing_cot, gating_cot)


def input_pullback(pair_map, projected_input, left_cot, right_cot, gating_cot, weight_in, upstream):
    channels = left_cot.shape[-1]
    left_sigmoid = jax.nn.sigmoid(projected_input[..., :channels])
    right_sigmoid = jax.nn.sigmoid(projected_input[..., 2 * channels : 3 * channels])
    pieces = [
        left_cot
        * projected_input[..., channels : 2 * channels]
        * left_sigmoid
        * (1.0 - left_sigmoid),
        left_cot * left_sigmoid,
        right_cot
        * projected_input[..., 3 * channels : 4 * channels]
        * right_sigmoid
        * (1.0 - right_sigmoid),
        right_cot * right_sigmoid,
        gating_cot,
    ]
    proj_cot = jnp.concatenate(pieces, axis=-1).astype(jnp.bfloat16)
    normalized_gradient = jnp.dot(proj_cot, weight_in.T, preferred_element_type=jnp.float32)
    return upstream + norm_backprop(pair_map.astype(jnp.float32), normalized_gradient)


def homolog_mapped(homolog_features, homolog_factor_matrix):
    hidden_state = homolog_factor_matrix.shape[1] // 2
    normalized = normalize_layer(homolog_features.astype(jnp.float32)).astype(jnp.bfloat16)
    projected_input = jnp.dot(normalized, homolog_factor_matrix, preferred_element_type=jnp.float32)
    return (
        projected_input[..., :hidden_state].astype(jnp.bfloat16),
        projected_input[..., hidden_state:].astype(jnp.bfloat16),
    )


def across_columns(arrays):
    return jax.tree.map(
        lambda part, own: part.astype(own.dtype),
        lax.all_gather(shortened(arrays), "col", axis=1, tiled=True),
        arrays,
    )


def spanning_rows(arrays):
    return jax.tree.map(
        lambda part, own: part.astype(own.dtype),
        lax.all_gather(shortened(arrays), "row", axis=0, tiled=True),
        arrays,
    )


def rows_for_columns(gathered):
    row_ratio = lax.axis_size("row") // lax.axis_size("col")
    first_owner = lax.axis_index("col") * row_ratio
    owned = [
        broadcast(gathered, "row", first_owner + turn_index) for turn_index in range(row_ratio)
    ]
    return jnp.concatenate(owned, axis=0)


def row_column_sets(gathered):
    row_ratio = lax.axis_size("row") // lax.axis_size("col")
    row_index = lax.axis_index("row")
    block_width = gathered.shape[1] // row_ratio
    owned_piece = lax.dynamic_slice_in_dim(
        gathered, row_index % row_ratio * block_width, block_width, 1
    )
    return broadcast(owned_piece, "col", row_index // row_ratio)


def outgoing_forward(pair_map, weight_in, weight_out):
    row_count, column_count, channels = pair_map.shape
    normalized, projected_input = triangle_inputs(pair_map, weight_in)
    left_factor, right_factor = gated_pairs(projected_input, channels)
    gathered = across_columns(
        (
            left_factor.reshape(row_count, column_count * channels),
            right_factor.reshape(row_count, column_count * channels),
        )
    )
    left_row_part = gathered[0].reshape(row_count, -1, channels)
    col_right = rows_for_columns(gathered[1]).reshape(column_count, -1, channels)
    mixing = jnp.einsum(
        "ikc,jkc->ijc", left_row_part, col_right, preferred_element_type=jnp.float32
    )
    return (
        triangle_output(pair_map, projected_input, mixing, weight_out),
        (normalized, projected_input, left_factor, right_factor, mixing),
    )


def incoming_forward(pair_map, weight_in, weight_out):
    row_count, column_count, channels = pair_map.shape
    normalized, projected_input = triangle_inputs(pair_map, weight_in)
    left_factor, right_factor = gated_pairs(projected_input, channels)
    gathered = spanning_rows(
        (
            left_factor.reshape(row_count, column_count * channels),
            right_factor.reshape(row_count, column_count * channels),
        )
    )
    col_left = row_column_sets(gathered[0]).reshape(-1, row_count, channels)
    col_right = gathered[1].reshape(-1, column_count, channels)
    mixing = jnp.einsum("kic,kjc->ijc", col_left, col_right, preferred_element_type=jnp.float32)
    return (
        triangle_output(pair_map, projected_input, mixing, weight_out),
        (normalized, projected_input, left_factor, right_factor, mixing),
    )


def outgoing_backward(pair_map, saved, weight_in, weight_out, upstream):
    row_count, column_count, channels = pair_map.shape
    normalized, projected_input, left_factor, right_factor, mixing = saved
    mixing_cot, gating_cot = output_pullback(projected_input, mixing, weight_out, upstream)
    flat_cot = mixing_cot.reshape(row_count, column_count * channels)
    cot_rows = across_columns(flat_cot).reshape(row_count, -1, channels)
    gathered = spanning_rows(
        (
            flat_cot,
            left_factor.reshape(row_count, column_count * channels),
            right_factor.reshape(row_count, column_count * channels),
        )
    )
    left_all = gathered[1].reshape(-1, column_count, channels)
    right_all = gathered[2].reshape(-1, column_count, channels)
    cot_picked = row_column_sets(gathered[0]).reshape(-1, row_count, channels)
    left_cot = jnp.einsum("ijc,jkc->ikc", cot_rows, right_all, preferred_element_type=jnp.float32)
    right_cot = jnp.einsum("ijc,ikc->jkc", cot_picked, left_all, preferred_element_type=jnp.float32)
    return input_pullback(
        pair_map, projected_input, left_cot, right_cot, gating_cot, weight_in, upstream
    )


def incoming_backward(pair_map, saved, weight_in, weight_out, upstream):
    row_count, column_count, channels = pair_map.shape
    normalized, projected_input, left_factor, right_factor, mixing = saved
    mixing_cot, gating_cot = output_pullback(projected_input, mixing, weight_out, upstream)
    flat_cot = mixing_cot.reshape(row_count, column_count * channels)
    gathered = across_columns(
        (
            flat_cot,
            left_factor.reshape(row_count, column_count * channels),
            right_factor.reshape(row_count, column_count * channels),
        )
    )
    left_all = gathered[1].reshape(row_count, -1, channels)
    right_all = gathered[2].reshape(row_count, -1, channels)
    cot_picked = rows_for_columns(gathered[0]).reshape(column_count, -1, channels)
    cot_cols = spanning_rows(flat_cot).reshape(-1, column_count, channels)
    left_cot = jnp.einsum("ijc,kjc->kic", cot_picked, right_all, preferred_element_type=jnp.float32)
    right_cot = jnp.einsum("ijc,kic->kjc", cot_cols, left_all, preferred_element_type=jnp.float32)
    return input_pullback(
        pair_map, projected_input, left_cot, right_cot, gating_cot, weight_in, upstream
    )


def body(
    homolog_features,
    pair_input,
    cotangent,
    homolog_factor_matrix,
    outer_output_weight,
    outgoing_input_weight,
    outgoing_output_weight,
    incoming_input_weight,
    incoming_output_weight,
):
    local_sequences, column_count, alignment_channels = homolog_features.shape
    row_count, unused_cols, channels = pair_input.shape
    hidden_state = homolog_factor_matrix.shape[1] // 2
    left_alignment, right_alignment = homolog_mapped(homolog_features, homolog_factor_matrix)
    flattened_left = left_alignment.reshape(local_sequences, column_count * hidden_state)
    flattened_right = right_alignment.reshape(local_sequences, column_count * hidden_state)
    alignment_columns = spanning_rows((flattened_left, flattened_right))
    left_row_part = row_column_sets(alignment_columns[0])
    outer_mean = (
        lax.dot_general(
            left_row_part,
            alignment_columns[1],
            (((0,), (0,)), ((), ())),
            preferred_element_type=jnp.float32,
        )
        / HOMOLOG_TOTAL
    )
    outer_mean = outer_mean.reshape(row_count, hidden_state, column_count, hidden_state).transpose(
        0, 2, 1, 3
    )
    outer_mean = outer_mean.reshape(row_count, column_count, hidden_state * hidden_state).astype(
        jnp.bfloat16
    )
    pair_first = (
        pair_input.astype(jnp.float32)
        + jnp.dot(outer_mean, outer_output_weight, preferred_element_type=jnp.float32)
    ).astype(jnp.bfloat16)
    pair_second, saved_out = outgoing_forward(
        pair_first, outgoing_input_weight, outgoing_output_weight
    )
    pair_output, saved_in = incoming_forward(
        pair_second, incoming_input_weight, incoming_output_weight
    )
    upstream = cotangent.astype(jnp.float32)
    second_cot = incoming_backward(
        pair_second, saved_in, incoming_input_weight, incoming_output_weight, upstream
    )
    pair_input_gradient = outgoing_backward(
        pair_first, saved_out, outgoing_input_weight, outgoing_output_weight, second_cot
    )
    pair_gradient_flow = pair_input_gradient.astype(jnp.bfloat16).reshape(
        row_count, column_count * channels
    )
    gathered = across_columns((flattened_left, flattened_right, pair_gradient_flow))
    left_all = gathered[0].reshape(local_sequences, -1, hidden_state)
    right_all = gathered[1].reshape(local_sequences, -1, hidden_state)
    residues = left_all.shape[1]
    cot_rows = rows_for_columns(gathered[2]).reshape(column_count, residues, channels)
    cot_cols = spanning_rows(pair_gradient_flow).reshape(residues, column_count, channels)
    weight_cube = outer_output_weight.reshape(hidden_state, hidden_state, channels)
    left_table = weight_cube.transpose(1, 2, 0).reshape(hidden_state * channels, hidden_state)
    right_table = weight_cube.transpose(0, 2, 1).reshape(hidden_state * channels, hidden_state)
    block_span = math.gcd(column_count, 4)
    count_of_blocks = column_count // block_span

    def block_left_part(row_block):
        mixed_part = jnp.einsum(
            "sjd,ije->side", right_all, row_block, preferred_element_type=jnp.float32
        ).astype(jnp.bfloat16)
        product = jnp.dot(
            mixed_part.reshape(local_sequences * block_span, hidden_state * channels),
            left_table,
            preferred_element_type=jnp.float32,
        )
        return product.reshape(local_sequences, block_span, hidden_state) / HOMOLOG_TOTAL

    def block_right_part(target_tile):
        mixed_part = jnp.einsum(
            "sic,ije->sjce", left_all, target_tile, preferred_element_type=jnp.float32
        ).astype(jnp.bfloat16)
        product = jnp.dot(
            mixed_part.reshape(local_sequences * block_span, hidden_state * channels),
            right_table,
            preferred_element_type=jnp.float32,
        )
        return product.reshape(local_sequences, block_span, hidden_state) / HOMOLOG_TOTAL

    left_alignment_gradient = lax.map(
        block_left_part, cot_rows.reshape(count_of_blocks, block_span, residues, channels)
    )
    left_alignment_gradient = left_alignment_gradient.transpose(1, 0, 2, 3).reshape(
        local_sequences, column_count, hidden_state
    )
    right_alignment_gradient = lax.map(
        block_right_part,
        cot_cols.reshape(residues, count_of_blocks, block_span, channels).transpose(1, 0, 2, 3),
    )
    right_alignment_gradient = right_alignment_gradient.transpose(1, 0, 2, 3).reshape(
        local_sequences, column_count, hidden_state
    )
    alignment_projection_gradient = jnp.concatenate(
        [left_alignment_gradient, right_alignment_gradient], axis=-1
    ).astype(jnp.bfloat16)
    normalized_gradient = jnp.dot(
        alignment_projection_gradient, homolog_factor_matrix.T, preferred_element_type=jnp.float32
    )
    alignment_gradient = norm_backprop(homolog_features.astype(jnp.float32), normalized_gradient)
    return (pair_output, pair_input_gradient, alignment_gradient)


def solution(mesh):
    placed = (
        P("row", "col", None),
        P("row", "col", None),
        P("row", "col", None),
        P(),
        P(),
        P(),
        P(),
        P(),
        P(),
    )
    return jax.shard_map(
        body,
        mesh=mesh,
        in_specs=placed,
        out_specs=(P("row", "col", None), P("row", "col", None), P("row", "col", None)),
        check_vma=False,
    )
```

profile of v0, /device:TPU:1, one launch (start us, length us, event | category | flops | bytes accessed | tf_op | source)
XLA Modules:
  0.0 951.9 jit_solution(17230992144682014722)
XLA Ops:
  15.0 35.1 %all-gather.3.cloned.1.call-done = bf16[1024,512]{1,0:T(8,128)(2,1)} async-done(((bf16[64,512]{1,0:T(8,128)(2,1)}), bf16[1024,512]{1,0:T(8,128)(2,1)}) %all-gather.3.cloned.1.call-update) | async-done | bytes 1048592 | tf_op jit(solution)/shard_map/all_gather | solution.py:118
  52.2 32.6 %all_gather.69 = bf16[64,4096]{0,1:T(8,128)(2,1)S(1)} all-gather(bf16[64,512]{0,1:T(8,128)(2,1)S(1)} %bitcast.351), channel_id=1, replica_groups=mesh['row'=16,'col'=8] {'col'}, dimensions={1}, use_global_device_ids=true | all-gather | bytes 589824 | tf_op jit(solution)/shard_map/all_gather | solution.py:110
  86.7 36.5 %all_gather.71 = bf16[64,4096]{0,1:T(8,128)(2,1)S(1)} all-gather(bf16[64,512]{0,1:T(8,128)(2,1)S(1)} %bitcast.349), channel_id=1, replica_groups=mesh['row'=16,'col'=8] {'col'}, dimensions={1}, use_global_device_ids=true | all-gather | bytes 589824 | tf_op jit(solution)/shard_map/all_gather | solution.py:110
  125.3 47.2 %all-reduce.10.cloned.1.call-done = bf16[1024,256]{1,0:T(8,128)(2,1)} async-done(((bf16[1024,256]{1,0:T(8,128)(2,1)}), bf16[1024,256]{1,0:T(8,128)(2,1)}) %all-reduce.10.cloned.1.call-update) | async-done | bytes 524304 | tf_op jit(solution)/shard_map/psum | solution.py:20
  179.2 28.1 %all_gather.56 = bf16[8,16384]{1,0:T(8,128)(2,1)S(1)} all-gather(bf16[8,2048]{1,0:T(8,128)(2,1)S(1)} %bitcast.369), channel_id=1, replica_groups=mesh['row'=16,'col'=8] {'col'}, dimensions={1}, use_global_device_ids=true | all-gather | bytes 294912 | tf_op jit(solution)/shard_map/all_gather | solution.py:110
  208.3 28.0 %all_gather.57 = bf16[8,16384]{1,0:T(8,128)(2,1)S(1)} all-gather(bf16[8,2048]{1,0:T(8,128)(2,1)S(1)} %bitcast.375), channel_id=1, replica_groups=mesh['row'=16,'col'=8] {'col'}, dimensions={1}, use_global_device_ids=true | all-gather | bytes 294912 | tf_op jit(solution)/shard_map/all_gather | solution.py:110
  236.6 39.0 %all_gather.66 = bf16[128,2048]{1,0:T(8,128)(2,1)S(1)} all-gather(bf16[8,2048]{1,0:T(8,128)(2,1)S(1)} %bitcast.376), channel_id=1, replica_groups=mesh['row'=16,'col'=8] {'row'}, dimensions={0}, use_global_device_ids=true | all-gather | bytes 557056 | tf_op jit(solution)/shard_map/all_gather | solution.py:118
  275.9 17.7 %all_gather.64 = bf16[128,2048]{1,0:T(8,128)(2,1)S(1)} all-gather(bf16[8,2048]{1,0:T(8,128)(2,1)S(1)} %bitcast.370), channel_id=1, replica_groups=mesh['row'=16,'col'=8] {'row'}, dimensions={0}, use_global_device_ids=true | all-gather | bytes 557056 | tf_op jit(solution)/shard_map/all_gather | solution.py:118
  293.9 42.2 %all-reduce.20.cloned.1.call-done = (bf16[8,16384]{1,0:T(8,128)(2,1)}, bf16[8,16384]{1,0:T(8,128)(2,1)}) async-done(((bf16[8,16384]{1,0:T(8,128)(2,1)}, bf16[8,16384]{1,0:T(8,128)(2,1)}), (bf16[8,16384]{1,0:T(8,128)(2,1)}, bf16[8,16384]{1,0:T(8,128)(2,1)})) %all-reduce.20.cloned.1.call-update) | async-done | bytes 524304 | tf_op jit(solution)/shard_map/psum | solution.py:20
  345.4 18.0 %all_gather.59 = bf16[128,2048]{1,0:T(8,128)(2,1)S(1)} all-gather(bf16[8,2048]{1,0:T(8,128)(2,1)S(1)} %bitcast.373), channel_id=1, replica_groups=mesh['row'=16,'col'=8] {'row'}, dimensions={0}, use_global_device_ids=true | all-gather | bytes 557056 | tf_op jit(solution)/shard_map/all_gather | solution.py:118
  366.0 20.9 %all_gather.58 = bf16[128,2048]{1,0:T(8,128)(2,1)} all-gather(bf16[8,2048]{1,0:T(8,128)(2,1)S(1)} %bitcast.367), channel_id=1, replica_groups=mesh['row'=16,'col'=8] {'row'}, dimensions={0}, use_global_device_ids=true | all-gather | bytes 557056 | tf_op jit(solution)/shard_map/all_gather | solution.py:118
  388.2 30.6 %all_gather.62 = bf16[8,16384]{1,0:T(8,128)(2,1)} all-gather(bf16[8,2048]{1,0:T(8,128)(2,1)} %bitcast.374), channel_id=1, replica_groups=mesh['row'=16,'col'=8] {'col'}, dimensions={1}, use_global_device_ids=true | all-gather | bytes 294912 | tf_op jit(solution)/shard_map/all_gather | solution.py:110
  418.9 24.4 %all-reduce.12.cloned.1.call-done = bf16[128,8,128]{0,1,2:T(8,128)(2,1)} async-done(((bf16[128,8,128]{0,1,2:T(8,128)(2,1)}), bf16[128,8,128]{0,1,2:T(8,128)(2,1)}) %all-reduce.12.cloned.1.call-update) | async-done | bytes 262160 | tf_op jit(solution)/shard_map/psum | solution.py:20
  449.0 28.1 %all_gather.61 = bf16[8,16384]{1,0:T(8,128)(2,1)S(1)} all-gather(bf16[8,2048]{1,0:T(8,128)(2,1)S(1)} %bitcast.371), channel_id=1, replica_groups=mesh['row'=16,'col'=8] {'col'}, dimensions={1}, use_global_device_ids=true | all-gather | bytes 294912 | tf_op jit(solution)/shard_map/all_gather | solution.py:110
  478.1 28.3 %all_gather.60 = bf16[8,16384]{1,0:T(8,128)(2,1)S(1)} all-gather(bf16[8,2048]{1,0:T(8,128)(2,1)} %bitcast.368), channel_id=1, replica_groups=mesh['row'=16,'col'=8] {'col'}, dimensions={1}, use_global_device_ids=true | all-gather | bytes 294912 | tf_op jit(solution)/shard_map/all_gather | solution.py:110
  509.8 40.6 %all_gather.63 = bf16[128,2048]{1,0:T(8,128)(2,1)} all-gather(bf16[8,2048]{1,0:T(8,128)(2,1)} %bitcast.372), channel_id=1, replica_groups=mesh['row'=16,'col'=8] {'row'}, dimensions={0}, use_global_device_ids=true | all-gather | bytes 557056 | tf_op jit(solution)/shard_map/all_gather | solution.py:118
  555.7 50.4 %all-reduce.18.cloned.1.call-done = (bf16[8,16384]{1,0:T(8,128)(2,1)}, bf16[8,16384]{1,0:T(8,128)(2,1)}) async-done(((bf16[8,16384]{1,0:T(8,128)(2,1)}, bf16[8,16384]{1,0:T(8,128)(2,1)}), (bf16[8,16384]{1,0:T(8,128)(2,1)}, bf16[8,16384]{1,0:T(8,128)(2,1)})) %all-reduce.18.cloned.1.call-update) | async-done | bytes 524304 | tf_op jit(solution)/shard_map/psum | solution.py:20
  618.5 18.0 %all_gather.67 = bf16[128,2048]{1,0:T(8,128)(2,1)S(1)} all-gather(bf16[8,2048]{1,0:T(8,128)(2,1)S(1)} %bitcast.377), channel_id=1, replica_groups=mesh['row'=16,'col'=8] {'row'}, dimensions={0}, use_global_device_ids=true | all-gather | bytes 557056 | tf_op jit(solution)/shard_map/all_gather | solution.py:118
  636.5 30.5 %all_gather.65 = bf16[8,16384]{1,0:T(8,128)(2,1)} all-gather(bf16[8,2048]{1,0:T(8,128)(2,1)S(1)} %bitcast.378), channel_id=1, replica_groups=mesh['row'=16,'col'=8] {'col'}, dimensions={1}, use_global_device_ids=true | all-gather | bytes 294912 | tf_op jit(solution)/shard_map/all_gather | solution.py:110
  673.4 79.8 %all-reduce.14.cloned.1.call-done = bf16[128,8,128]{0,1,2:T(8,128)(2,1)} async-done(((bf16[128,8,128]{0,1,2:T(8,128)(2,1)}), bf16[128,8,128]{0,1,2:T(8,128)(2,1)}) %all-reduce.14.cloned.1.call-update) | async-done | bytes 262160 | tf_op jit(solution)/shard_map/psum | solution.py:20
  758.1 28.1 %all_gather.68 = bf16[8,16384]{1,0:T(8,128)(2,1)S(1)} all-gather(bf16[8,2048]{1,0:T(8,128)(2,1)S(1)} %bitcast.379), channel_id=1, replica_groups=mesh['row'=16,'col'=8] {'col'}, dimensions={1}, use_global_device_ids=true | all-gather | bytes 294912 | tf_op jit(solution)/shard_map/all_gather | solution.py:110
  786.2 32.8 %all_gather.70 = bf16[128,2048]{1,0:T(8,128)(2,1)S(1)} all-gather(bf16[8,2048]{1,0:T(8,128)(2,1)S(1)} %bitcast.380), channel_id=1, replica_groups=mesh['row'=16,'col'=8] {'row'}, dimensions={0}, use_global_device_ids=true | all-gather | bytes 557056 | tf_op jit(solution)/shard_map/all_gather | solution.py:118
  820.1 7.3 while.21
  827.7 105.9 %all-reduce.16.cloned.1.call-done = (bf16[8,16384]{1,0:T(8,128)(2,1)}, bf16[8,16384]{1,0:T(8,128)(2,1)}) async-done(((bf16[8,16384]{1,0:T(8,128)(2,1)}, bf16[8,16384]{1,0:T(8,128)(2,1)}), (bf16[8,16384]{1,0:T(8,128)(2,1)}, bf16[8,16384]{1,0:T(8,128)(2,1)})) %all-reduce.16.cloned.1.call-update) | async-done | bytes 524304 | tf_op jit(solution)/shard_map/psum | solution.py:20
  (243 shorter events, 100.8 us)
Async XLA Ops:
  7.2 336.7 %copy-start = (bf16[128,640]{1,0:T(8,128)(2,1)S(1)}, bf16[128,640]{1,0:T(8,128)(2,1)}, u32[]{:S(2)}) copy-start(bf16[128,640]{1,0:T(8,128)(2,1)} %param.20) | copy-start | bytes 491524
  7.2 43.0 %all-gather.3.cloned.1.call-start = ((), (), s32[]{:S(2)}) async-start(), calls=%async_computation | async-start | bytes 1114112 | tf_op jit(solution)/shard_map/all_gather | solution.py:118
  13.9 111.4 %all-gather.5.cloned.1.call-start = ((), (), s32[]{:S(2)}) async-start(), calls=%async_computation.2 | async-start | bytes 1114112 | tf_op jit(solution)/shard_map/all_gather | solution.py:118
  14.9 157.5 %all-reduce.10.cloned.1.call-start = ((), (), s32[]{:S(2)}) async-start(), calls=%async_computation.1 | async-start | bytes 1048576 | tf_op jit(solution)/shard_map/psum | solution.py:20
  15.0 70.9 %copy-start.2 = (bf16[1024,128]{1,0:T(8,128)(2,1)S(1)}, bf16[1024,128]{1,0:T(8,128)(2,1)}, u32[]{:S(2)}) copy-start(bf16[1024,128]{1,0:T(8,128)(2,1)} %param.17) | copy-start | bytes 786436
  52.1 284.0 %all-reduce.20.cloned.1.call-start = ((), (), s32[]{:S(2)}) async-start(), calls=%async_computation.7 | async-start | bytes 1048576 | tf_op jit(solution)/shard_map/psum | solution.py:20
  208.3 235.0 %all-reduce.12.cloned.1.call-start = ((), (), s32[]{:S(2)}) async-start(), calls=%async_computation.3 | async-start | bytes 524288 | tf_op jit(solution)/shard_map/psum | solution.py:20
  364.6 241.5 %all-reduce.18.cloned.1.call-start = ((), (), s32[]{:S(2)}) async-start(), calls=%async_computation.6 | async-start | bytes 1048576 | tf_op jit(solution)/shard_map/psum | solution.py:20
  445.4 60.9 %copy-start.7 = (bf16[8,16384]{1,0:T(8,128)(2,1)S(1)}, bf16[8,16384]{1,0:T(8,128)(2,1)}, u32[]{:S(2)}) copy-start(bf16[8,16384]{1,0:T(8,128)(2,1)} %all_gather.62) | copy-start | bytes 786436
  478.0 275.1 %all-reduce.14.cloned.1.call-start = ((), (), s32[]{:S(2)}) async-start(), calls=%async_computation.4 | async-start | bytes 524288 | tf_op jit(solution)/shard_map/psum | solution.py:20
  611.7 6.4 copy-start.34
  611.7 6.4 copy-start.32
  616.8 53.0 %copy-start.5 = (f32[8,16,128]{2,1,0:T(8,128)}, f32[8,16,128]{2,1,0:T(8,128)S(1)}, u32[]{:S(2)}) copy-start(f32[8,16,128]{2,1,0:T(8,128)S(1)} %get-tuple-element.143) | copy-start | bytes 196612
  669.8 263.8 %all-reduce.16.cloned.1.call-start = ((), (), s32[]{:S(2)}) async-start(), calls=%async_computation.5 | async-start | bytes 1048576 | tf_op jit(solution)/shard_map/psum | solution.py:20
  673.2 82.6 %copy-start.12 = (bf16[128,640]{1,0:T(8,128)(2,1)S(1)}, bf16[128,640]{1,0:T(8,128)(2,1)}, u32[]{:S(2)}) copy-start(bf16[128,640]{1,0:T(8,128)(2,1)} %param.18) | copy-start | bytes 491524
  673.2 82.9 %copy-start.30 = (f32[8,16]{1,0:T(8,128)S(1)}, f32[8,16]{1,0:T(8,128)}, u32[]{:S(2)}) copy-start(f32[8,16]{1,0:T(8,128)} %copy-done.29) | copy-start | bytes 1540
  673.2 82.9 %copy-start.25 = (f32[8,16]{1,0:T(8,128)S(1)}, f32[8,16]{1,0:T(8,128)}, u32[]{:S(2)}) copy-start(f32[8,16]{1,0:T(8,128)} %copy-done.24) | copy-start | bytes 1540
  673.2 83.2 %copy-start.6 = (f32[8,16,128]{2,1,0:T(8,128)S(1)}, f32[8,16,128]{2,1,0:T(8,128)}, u32[]{:S(2)}) copy-start(f32[8,16,128]{2,1,0:T(8,128)} %copy-done.5) | copy-start | bytes 196612
  673.3 83.1 %copy-start.23 = (bf16[8,16,128]{2,1,0:T(8,128)(2,1)S(1)}, bf16[8,16,128]{2,1,0:T(8,128)(2,1)}, u32[]{:S(2)}) copy-start(bf16[8,16,128]{2,1,0:T(8,128)(2,1)} %param.15) | copy-start | bytes 98308
  756.1 64.0 %copy-start.21 = (bf16[4,8,32,128]{3,1,2,0:T(8,128)(2,1)S(1)}, bf16[4,8,32,128]{3,1,2,0:T(8,128)(2,1)}, u32[]{:S(2)}) copy-start(bf16[4,8,32,128]{3,1,2,0:T(8,128)(2,1)} %copy.214) | copy-start | bytes 786436
  827.4 107.4 %copy-start.20 = (bf16[4,8,32,128]{3,1,2,0:T(8,128)(2,1)S(1)}, bf16[4,8,32,128]{3,1,2,0:T(8,128)(2,1)}, u32[]{:S(2)}) copy-start(bf16[4,8,32,128]{3,1,2,0:T(8,128)(2,1)} %copy.215) | copy-start | bytes 786436
  934.8 7.5 copy-start.1
  934.8 7.5 copy-start.10
  934.8 7.5 copy-start.37
  (25 other events, 51.0 us)
Sparse Core Ops, SparseCore 0:
  14.0 36.1 all-gather.2
  51.8 34.3 all-gather.4
  89.3 83.0 all-reduce.9
  208.4 127.6 all-reduce.19
  364.7 78.4 all-reduce.11
  478.1 127.9 all-reduce.17
  669.9 83.2 all-reduce.13
  820.2 113.3 all-reduce.15
where the time goes:
time: 953 us; the launch traced here: 952 us
  blocking collectives  458 us (48%)
  waiting for transfers between devices  385 us (40%)
  local copies, waits for them, and re-layouts  37.1 us (4%)
  matrix products  34.5 us (4%)
  other arithmetic  21.5 us (2%)
  between operations  15.2 us (2%)
    psum x6, waiting for transfers between devices, broadcast(): return lax.psum(jnp.where(mine, array, jnp.zeros_like(array)), axis)  350 us
    all_gather x9, blocking collectives, across_columns(): lax.all_gather(shortened(arrays), 'col', axis=1, tiled=True)  271 us
    all_gather x7, blocking collectives, spanning_rows(): lax.all_gather(shortened(arrays), 'row', axis=0, tiled=True)  187 us
    all_gather x2, waiting for transfers between devices, spanning_rows(): lax.all_gather(shortened(arrays), 'row', axis=0, tiled=True)  35.1 us
  transfers between devices with their start and end apart: 8, of which 7 were waited for; matrix products, arithmetic and copies ran while one was open for 3% of the time, Pallas kernels for 0%

commit v1 on v0

v1 whole, which is shorter than its diff:
```python
import jax
import jax.numpy as jnp
from jax import lax
from jax.experimental import pallas as pl
from jax.experimental.pallas import tpu as pltpu
from jax.sharding import PartitionSpec as P

SEQUENCES = 1024
EPSILON = 1e-05
MESH = pl.DeviceIdType.MESH
F32 = jnp.float32
BF16 = jnp.bfloat16
GRID = 8
BLOCK = 16
WIDTH = 128
HIDDEN = 32


def dot(lhs, rhs, dims=((1,), (0,))):
    return lax.dot_general(lhs, rhs, (dims, ((), ())), preferred_element_type=F32)


def layer_norm(inputs):
    centered = inputs - jnp.mean(inputs, axis=-1, keepdims=True)
    spread = jnp.mean(centered * centered, axis=-1, keepdims=True)
    scale = lax.rsqrt(spread + EPSILON)
    return centered * scale, scale


def layer_norm_pullback(normed, scale, upstream):
    along = jnp.mean(upstream * normed, axis=-1, keepdims=True)
    return scale * (upstream - jnp.mean(upstream, axis=-1, keepdims=True) - normed * along)


def pair_kernel(
    left_ic,
    left_ci,
    right_dj,
    pair_input,
    cotangent,
    outer_weight,
    spread_weight_hbm,
    out_in_weight,
    out_out_weight,
    in_in_weight,
    in_out_weight,
    pair_output,
    pair_gradient,
    msa_cots,
    pair_block,
    cot_block,
    relay_left,
    relay_right,
    msa_left,
    msa_right,
    msa_rows,
    o_left,
    o_right,
    o_right_stage,
    i_left,
    i_right,
    i_left_stage,
    ib_right,
    ib_left,
    ib_cot,
    ib_cot_turned,
    ib_cot_stage,
    ob_right,
    ob_left,
    ob_cot_row,
    ob_cot_col,
    ob_cot_stage,
    final_cot,
    spread_weight,
    outer32,
    wide,
    flat,
    proj_out,
    proj_in,
    mixing_out,
    first,
    second,
    upstream32,
    stacked,
    grad_table,
    msa_cot_own,
    msa_cot_got,
    output_stage,
    output_got,
    gradient_stage,
    gradient_got,
    relay_sem,
    block_sem,
    msa_sem,
    rows_sem,
    pair_sem,
    final_sem,
    small_sem,
    send_sem,
    weight_sem,
):
    row, col = lax.axis_index("row"), lax.axis_index("col")
    a, h, b = row // 2, row % 2, col
    other = 1 - h
    own_i = a * other + b * h
    own_j = b * other + a * h
    diagonal = a == b

    def row_chip(n):
        return a * other + n * h, n * other + b * h

    def col_chip(n):
        return n * other + a * h, b * other + n * h

    def remote(src, dst, send, recv, chip, core):
        return pltpu.make_async_remote_copy(
            src_ref=src,
            dst_ref=dst,
            send_sem=send,
            recv_sem=recv,
            device_id=(2 * chip[0] + core, chip[1]),
            device_id_type=MESH,
        )

    def wait_for(ref, sem):
        pltpu.make_async_copy(ref, ref, sem).wait()

    weight_copy = pltpu.make_async_copy(spread_weight_hbm, spread_weight, weight_sem)
    weight_copy.start()

    barrier = pltpu.get_barrier_semaphore()

    def greet(chip, core):
        pl.semaphore_signal(
            barrier, inc=1, device_id=(2 * chip[0] + core, chip[1]), device_id_type=MESH
        )

    def greet_step(k, carry):
        for core in range(2):
            greet(((a + k) % GRID, b), core)
            greet((a, (b + k) % GRID), core)
        return carry

    lax.fori_loop(1, GRID, greet_step, 0)
    greet((a, b), other)

    @pl.when(jnp.logical_not(diagonal))
    def _():
        greet((b, a), 0)
        greet((b, a), 1)
        pl.semaphore_wait(barrier, 31)

    @pl.when(diagonal)
    def _():
        pl.semaphore_wait(barrier, 29)

    for slot, (src, dst) in enumerate(((left_ic, relay_left), (right_dj, relay_right))):

        @pl.when(jnp.logical_not(diagonal))
        def _():
            remote(src, dst, send_sem.at[slot], relay_sem.at[slot], (b, a), h).start()

        @pl.when(diagonal)
        def _():
            pltpu.make_async_copy(src, dst, relay_sem.at[slot]).start()

    def msa_send(src, dst, sems, slot, chips, own, core, send):
        def step(k, carry):
            n = (own + k) % GRID

            @pl.when(jnp.logical_or(k > 0, h != core))
            def _():
                remote(src, dst.at[slot], send, sems.at[slot], chips(n), core).start()

            return carry

        lax.fori_loop(0, GRID, step, 0)

        @pl.when(h == core)
        def _():
            pltpu.make_async_copy(src, dst.at[slot], sems.at[slot]).start()

    def column(n):
        return n, b

    def line(n):
        return a, n

    def msa_sent(src, dst, core, send):
        @pl.when(h == core)
        def _():
            wait_for(dst.at[pl.ds(0, 7)], send)

        @pl.when(h != core)
        def _():
            wait_for(dst.at[pl.ds(0, 8)], send)

    msa_send(right_dj, msa_right, msa_sem.at[1], row, column, a, 0, send_sem.at[2])
    msa_send(left_ic, msa_left, msa_sem.at[0], row, column, a, 1, send_sem.at[3])

    for slot, (src, dst) in enumerate(((pair_input, pair_block), (cotangent, cot_block))):
        half = dst.at[pl.ds(h * 8, 8)]
        sem = block_sem.at[slot, h]

        @pl.when(h == 0)
        def _():
            pltpu.make_async_copy(src, half, sem).start()

        @pl.when(h == 1)
        def _():
            remote(src, half, send_sem.at[4 + slot], sem, (a, b), 0).start()

        @pl.when(jnp.logical_and(h == 1, diagonal))
        def _():
            pltpu.make_async_copy(src, half, sem).start()

        @pl.when(jnp.logical_not(jnp.logical_and(h == 1, diagonal)))
        def _():
            remote(src, half, send_sem.at[6 + slot], sem, (b, a), 1).start()

    def block_sent(slot, src):
        @pl.when(h == 1)
        def _():
            wait_for(src, send_sem.at[4 + slot])

        @pl.when(jnp.logical_not(jnp.logical_and(h == 1, diagonal)))
        def _():
            wait_for(src, send_sem.at[6 + slot])

    relay_slot = 2 * b + h
    wait_for(relay_left, relay_sem.at[0])
    msa_send(relay_left, msa_left, msa_sem.at[0], relay_slot, line, b, 0, send_sem.at[8])
    wait_for(relay_right, relay_sem.at[1])
    msa_send(relay_right, msa_right, msa_sem.at[1], relay_slot, line, b, 1, send_sem.at[9])

    def msa_wait(n, carry):
        wait_for(msa_left.at[n], msa_sem.at[0, n])
        wait_for(msa_right.at[n], msa_sem.at[1, n])
        return carry

    lax.fori_loop(0, 2 * GRID, msa_wait, 0)
    everything = msa_left[...].reshape(SEQUENCES, BLOCK * HIDDEN)
    outer32[...] = dot(
        msa_right[...].reshape(SEQUENCES, BLOCK * HIDDEN), everything, ((0,), (0,))
    ) * (1.0 / SEQUENCES)
    lane_part = lax.broadcasted_iota(jnp.int32, (BLOCK, WIDTH), 1) // HIDDEN

    def project_step(d2, total):
        columns = []
        for part in range(2):
            tile = outer32[pl.ds(pl.multiple_of((2 * d2 + part) * BLOCK, BLOCK), BLOCK), :]
            columns.append(
                jnp.concatenate(
                    [
                        jnp.where(lane_part == q, tile[:, g * WIDTH : (g + 1) * WIDTH], 0.0)
                        for q in range(4)
                        for g in range(4)
                    ],
                    axis=0,
                )
            )
        picked = jnp.concatenate(columns, axis=1).astype(BF16)
        weight = outer_weight[pl.ds(pl.multiple_of(d2 * 2 * WIDTH, 2 * WIDTH), 2 * WIDTH), :]
        return total + dot(picked, weight)

    projected = lax.fori_loop(
        0, HIDDEN // 2, project_step, jnp.zeros((BLOCK * BLOCK, WIDTH), F32)
    )
    for part in range(2):
        wait_for(pair_block.at[pl.ds(part * 8, 8)], block_sem.at[0, part])
        wait_for(cot_block.at[pl.ds(part * 8, 8)], block_sem.at[1, part])
    for i in range(BLOCK):
        start = ((i % 4) * 4 + i // 4) * BLOCK
        first[pl.ds(i * BLOCK, BLOCK), :] = (
            (pair_block[i].astype(F32) + projected[start : start + BLOCK]).astype(BF16).astype(F32)
        )

    def send_same(dst, sems, chips, own, send):
        def step(k, carry):
            remote(
                dst.at[own], dst.at[own], send, sems.at[own], chips((own + k) % GRID), h
            ).start()
            return carry

        lax.fori_loop(1, GRID, step, 0)

    def send_other(src, dst, sems, chips, own, send):
        def step(k, carry):
            remote(
                src, dst.at[own], send, sems.at[own], chips((own + k) % GRID), other
            ).start()
            return carry

        lax.fori_loop(0, GRID, step, 0)

    def contract(left, left_sem, left_own, left_by_column, right, right_sem, right_own, own):
        def arrive(ref, sems, slot, skip):
            if skip is None:
                wait_for(ref.at[slot], sems.at[slot])
            else:

                @pl.when(slot != skip)
                def _():
                    wait_for(ref.at[slot], sems.at[slot])

        def block_step(k, totals):
            slot = (own + k) % GRID
            arrive(left, left_sem, slot, left_own)
            arrive(right, right_sem, slot, right_own)
            wide[...] = left[slot].astype(F32)

            def inner(group, totals):
                totals = list(totals)
                for u in range(4):
                    t = group * 4 + u
                    across = right[slot, t].astype(F32)
                    for p in range(BLOCK):
                        if left_by_column:
                            one = wide[t, pl.ds(p, 1), :]
                        else:
                            one = wide[p, pl.ds(t, 1), :]
                        totals[p] = totals[p] + one * across
                return tuple(totals)

            return lax.fori_loop(0, BLOCK // 4, inner, totals)

        zeros = tuple(jnp.zeros((BLOCK, WIDTH), F32) for _ in range(BLOCK))
        totals = lax.fori_loop(0, GRID, block_step, zeros)
        return jnp.concatenate(totals, axis=0)

    def turned(value, store):
        flat[...] = value
        for j in range(BLOCK):
            store(j, flat[pl.ds(j, BLOCK, stride=BLOCK), :].astype(BF16))

    def blocked(value):
        return value.astype(BF16).reshape(BLOCK, BLOCK, WIDTH)

    def gates(projected, at):
        return jax.nn.sigmoid(projected[:, at * WIDTH : (at + 1) * WIDTH])

    def channels(projected, at):
        return projected[:, at * WIDTH : (at + 1) * WIDTH]

    normed, unused = layer_norm(first[...])
    projected = dot(normed.astype(BF16), out_in_weight[...])
    proj_out[...] = projected
    o_left[own_j] = blocked(gates(projected, 0) * channels(projected, 1))
    send_same(o_left, pair_sem.at[0], row_chip, own_j, send_sem.at[10])
    right = gates(projected, 2) * channels(projected, 3)

    def store_right(j, value):
        o_right_stage[j] = value

    turned(right, store_right)
    send_other(o_right_stage, o_right, pair_sem.at[1], row_chip, own_j, send_sem.at[11])
    ob_left[own_i] = o_left[own_j]
    ob_right[own_i] = blocked(right)
    send_same(ob_left, pair_sem.at[2], col_chip, own_i, send_sem.at[12])
    send_same(ob_right, pair_sem.at[3], col_chip, own_i, send_sem.at[13])
    mixing = contract(
        o_left, pair_sem.at[0], own_j, False, o_right, pair_sem.at[1], None, own_j
    )
    mixing_out[...] = mixing
    normed, unused = layer_norm(mixing)
    update = dot(normed.astype(BF16), out_out_weight[...])
    second[...] = (first[...] + gates(proj_out[...], 4) * update).astype(BF16).astype(F32)

    normed, unused = layer_norm(second[...])
    projected = dot(normed.astype(BF16), in_in_weight[...])
    proj_in[...] = projected
    i_right[own_i] = blocked(gates(projected, 2) * channels(projected, 3))
    send_same(i_right, pair_sem.at[4], col_chip, own_i, send_sem.at[14])
    i_left_stage[...] = blocked(gates(projected, 0) * channels(projected, 1))
    send_other(i_left_stage, i_left, pair_sem.at[5], col_chip, own_i, send_sem.at[15])
    ib_right[own_j] = i_right[own_i]
    ib_left[own_j] = i_left_stage[...]
    send_same(ib_right, pair_sem.at[6], row_chip, own_j, send_sem.at[16])
    send_same(ib_left, pair_sem.at[7], row_chip, own_j, send_sem.at[17])
    mixing = contract(
        i_left, pair_sem.at[5], None, True, i_right, pair_sem.at[4], own_i, own_i
    )
    normed, scale = layer_norm(mixing)
    update = dot(normed.astype(BF16), in_out_weight[...])
    gating = gates(proj_in[...], 4)
    result = (second[...] + gating * update).astype(BF16)

    def output_pullback(normed, scale, update, gating, weight, upstream):
        update_cot = (upstream * gating).astype(BF16)
        normed_cot = dot(update_cot, weight[...], ((1,), (1,)))
        mixing_cot = layer_norm_pullback(normed, scale, normed_cot)
        return mixing_cot, upstream * update * gating * (1.0 - gating)

    def input_pullback(projected, left_cot, right_cot, gating_cot, weight, inputs, upstream):
        left_gate, right_gate = gates(projected, 0), gates(projected, 2)
        left_part, right_part = left_cot * left_gate, right_cot * right_gate
        pieces = [
            left_part * channels(projected, 1) * (1.0 - left_gate),
            left_part,
            right_part * channels(projected, 3) * (1.0 - right_gate),
            right_part,
            gating_cot,
        ]
        proj_cot = jnp.concatenate([piece.astype(BF16) for piece in pieces], axis=1)
        normed_cot = dot(proj_cot, weight[...], ((1,), (1,)))
        normed, scale = layer_norm(inputs)
        return upstream + layer_norm_pullback(normed, scale, normed_cot)

    upstream = cot_block[...].reshape(BLOCK * BLOCK, WIDTH).astype(F32)
    mixing_cot, gating_cot = output_pullback(
        normed, scale, update, gating, in_out_weight, upstream
    )
    ib_cot[own_i] = blocked(mixing_cot)
    send_same(ib_cot, pair_sem.at[8], col_chip, own_i, send_sem.at[18])

    def store_cot(j, value):
        ib_cot_stage[j] = value

    turned(mixing_cot, store_cot)
    send_other(ib_cot_stage, ib_cot_turned, pair_sem.at[9], row_chip, own_j, send_sem.at[19])

    @pl.when(h == 0)
    def _():
        pair_output[...] = result[: BLOCK * BLOCK // 2].reshape(8, BLOCK, WIDTH)
        output_stage[...] = result[BLOCK * BLOCK // 2 :].reshape(8, BLOCK, WIDTH)
        remote(output_stage, output_got, send_sem.at[20], small_sem.at[0], (a, b), 1).start()

    line_slot = b

    def rows_send(src, core, send):
        target = msa_rows.at[line_slot, pl.ds(pl.multiple_of(h * 64, 64), 64)]

        def step(k, carry):
            @pl.when(jnp.logical_or(k > 0, h != core))
            def _():
                remote(
                    src, target, send, rows_sem.at[line_slot, h], (a, (b + k) % GRID), core
                ).start()

            return carry

        lax.fori_loop(0, GRID, step, 0)

        @pl.when(h == core)
        def _():
            pltpu.make_async_copy(src, target, rows_sem.at[line_slot, h]).start()

    rows_send(left_ci, 0, send_sem.at[21])

    left_cot = contract(
        ib_right,
        pair_sem.at[6],
        own_j,
        False,
        ib_cot_turned,
        pair_sem.at[9],
        None,
        own_j,
    )
    upstream32[...] = left_cot
    right_cot = contract(
        ib_left, pair_sem.at[7], own_j, False, ib_cot, pair_sem.at[8], own_i, own_j
    )
    second_cot = input_pullback(
        proj_in[...],
        upstream32[...],
        right_cot,
        gating_cot,
        in_in_weight,
        second[...],
        upstream,
    )
    upstream32[...] = second_cot

    normed, scale = layer_norm(mixing_out[...])
    update = dot(normed.astype(BF16), out_out_weight[...])
    mixing_cot, gating_cot = output_pullback(
        normed, scale, update, gates(proj_out[...], 4), out_out_weight, second_cot
    )
    ob_cot_row[own_j] = blocked(mixing_cot)
    send_same(ob_cot_row, pair_sem.at[10], row_chip, own_j, send_sem.at[22])
    ob_cot_stage[...] = blocked(mixing_cot)
    send_other(ob_cot_stage, ob_cot_col, pair_sem.at[11], col_chip, own_i, send_sem.at[23])
    rows_send(right_dj, 1, send_sem.at[24])
    left_cot = contract(
        ob_cot_row, pair_sem.at[10], own_j, False, ob_right, pair_sem.at[3], own_i, own_j
    )
    flat[...] = left_cot
    right_cot = contract(
        ob_cot_col, pair_sem.at[11], None, True, ob_left, pair_sem.at[2], own_i, own_i
    )
    gradient = input_pullback(
        proj_out[...],
        flat[...],
        right_cot,
        gating_cot,
        out_in_weight,
        first[...],
        upstream32[...],
    )

    @pl.when(h == 0)
    def _():
        pair_gradient[...] = gradient[: BLOCK * BLOCK // 2].reshape(8, BLOCK, WIDTH)
        gradient_stage[...] = gradient[BLOCK * BLOCK // 2 :].reshape(8, BLOCK, WIDTH)
        remote(
            gradient_stage, gradient_got, send_sem.at[25], small_sem.at[1], (a, b), 1
        ).start()
        flat[...] = gradient
        for j in range(BLOCK):
            final_cot[a, j] = flat[pl.ds(j, BLOCK, stride=BLOCK), :].astype(BF16)

    @pl.when(h == 1)
    def _():
        final_cot[a] = blocked(gradient)

    send_same(final_cot, final_sem, column, a, send_sem.at[26])

    weight_copy.wait()

    def final_wait(k, carry):
        slot = (a + k) % GRID
        wait_for(final_cot.at[slot], final_sem.at[slot])
        return carry

    lax.fori_loop(1, GRID, final_wait, 0)
    for g in range(4):
        for q in range(4):
            stacked[g * WIDTH : (g + 1) * WIDTH, q * WIDTH : (q + 1) * WIDTH] = final_cot[
                :, 4 * g + q
            ].reshape(WIDTH, WIDTH)

    def table_step(x2, carry):
        at = pl.multiple_of(x2 * 2 * WIDTH, 2 * WIDTH)
        chunk = dot(stacked[...], spread_weight[:, pl.ds(at, 2 * WIDTH)]).astype(BF16)
        for part in range(2):
            start = pl.multiple_of((2 * x2 + part) * BLOCK, BLOCK)
            for g in range(4):
                grad_table[:, pl.ds(start, BLOCK), g * WIDTH : (g + 1) * WIDTH] = chunk[
                    g * WIDTH : (g + 1) * WIDTH, part * WIDTH : (part + 1) * WIDTH
                ].reshape(GRID, BLOCK, WIDTH)
        return carry

    lax.fori_loop(0, HIDDEN // 2, table_step, 0)

    def rows_wait(n, carry):
        for part in range(2):
            wait_for(msa_rows.at[n, pl.ds(part * 64, 64)], rows_sem.at[n, part])
        return carry

    lax.fori_loop(0, GRID, rows_wait, 0)

    def cot_step(n, total):
        return total + dot(msa_rows[n], grad_table[n])

    total = lax.fori_loop(0, GRID, cot_step, jnp.zeros((128, BLOCK * HIDDEN), F32))
    msa_cot_own[...] = (total * (1.0 / SEQUENCES)).astype(BF16)
    remote(
        msa_cot_own.at[pl.ds(pl.multiple_of(other * 64, 64), 64)],
        msa_cot_got,
        send_sem.at[27],
        small_sem.at[2],
        (a, b),
        other,
    ).start()
    msa_cots[other] = msa_cot_own[pl.ds(pl.multiple_of(h * 64, 64), 64), :]
    wait_for(msa_cot_got, small_sem.at[2])
    msa_cots[h] = msa_cot_got[...]

    @pl.when(h == 1)
    def _():
        wait_for(output_got, small_sem.at[0])
        pair_output[...] = output_got[...]
        wait_for(gradient_got, small_sem.at[1])
        pair_gradient[...] = gradient_got[...]

    @pl.when(jnp.logical_not(diagonal))
    def _():
        wait_for(relay_left, send_sem.at[0])
        wait_for(relay_right, send_sem.at[1])

    msa_sent(right_dj, msa_right, 0, send_sem.at[2])
    msa_sent(left_ic, msa_left, 1, send_sem.at[3])
    block_sent(0, pair_input)
    block_sent(1, cotangent)
    msa_sent(relay_left, msa_left, 0, send_sem.at[8])
    msa_sent(relay_right, msa_right, 1, send_sem.at[9])
    for at in (10, 12, 13, 14, 16, 17, 18, 22, 26):
        wait_for(o_left.at[pl.ds(0, 7)], send_sem.at[at])
    for at in (11, 15, 19, 23):
        wait_for(o_left, send_sem.at[at])
    msa_sent(left_ci, msa_left, 0, send_sem.at[21])
    msa_sent(right_dj, msa_left, 1, send_sem.at[24])
    wait_for(msa_cot_got, send_sem.at[27])

    @pl.when(h == 0)
    def _():
        wait_for(output_stage, send_sem.at[20])
        wait_for(gradient_stage, send_sem.at[25])


def pair_updates(left_ic, left_ci, right_dj, pair_input, cotangent, outer_weight, spread, weights):
    gathered = pltpu.VMEM((GRID, BLOCK, BLOCK, WIDTH), BF16)
    block = pltpu.VMEM((BLOCK, BLOCK, WIDTH), BF16)
    flat = pltpu.VMEM((BLOCK * BLOCK, WIDTH), F32)
    shares = pltpu.VMEM((64, BLOCK * HIDDEN), BF16)
    all_sequences = pltpu.VMEM((2 * GRID, 64, BLOCK * HIDDEN), BF16)
    half_block = pltpu.VMEM((8, BLOCK, WIDTH), BF16)
    half_wide = pltpu.VMEM((8, BLOCK, WIDTH), F32)
    projected = pltpu.VMEM((BLOCK * BLOCK, 5 * WIDTH), F32)
    dma = pltpu.SemaphoreType.DMA
    vmem = pl.BlockSpec(memory_space=pltpu.VMEM)
    return pl.pallas_call(
        pair_kernel,
        out_shape=(
            jax.ShapeDtypeStruct((8, BLOCK, WIDTH), BF16),
            jax.ShapeDtypeStruct((8, BLOCK, WIDTH), F32),
            jax.ShapeDtypeStruct((2, 64, BLOCK * HIDDEN), BF16),
        ),
        in_specs=[vmem] * 6 + [pl.BlockSpec(memory_space=pl.ANY)] + [vmem] * 4,
        out_specs=(vmem, vmem, vmem),
        scratch_shapes=[
            block,
            block,
            shares,
            shares,
            all_sequences,
            all_sequences,
            pltpu.VMEM((GRID, 128, BLOCK * HIDDEN), BF16),
            gathered,
            gathered,
            block,
            gathered,
            gathered,
            block,
            gathered,
            gathered,
            gathered,
            gathered,
            block,
            gathered,
            gathered,
            gathered,
            gathered,
            block,
            gathered,
            pltpu.VMEM((4 * WIDTH, HIDDEN * WIDTH), BF16),
            pltpu.VMEM((BLOCK * HIDDEN, BLOCK * HIDDEN), F32),
            pltpu.VMEM((BLOCK, BLOCK, WIDTH), F32),
            flat,
            projected,
            projected,
            flat,
            flat,
            flat,
            flat,
            pltpu.VMEM((4 * WIDTH, 4 * WIDTH), BF16),
            pltpu.VMEM((GRID, BLOCK * HIDDEN, BLOCK * HIDDEN), BF16),
            pltpu.VMEM((128, BLOCK * HIDDEN), BF16),
            shares,
            half_block,
            half_block,
            half_wide,
            half_wide,
            dma((2,)),
            dma((2, 2)),
            dma((2, 2 * GRID)),
            dma((GRID, 2)),
            dma((12, GRID)),
            dma((GRID,)),
            dma((3,)),
            dma((28,)),
            dma(()),
        ],
        compiler_params=pltpu.CompilerParams(
            collective_id=1, has_side_effects=True, vmem_limit_bytes=48 << 20
        ),
        name="pair_updates",
    )(left_ic, left_ci, right_dj, pair_input, cotangent, outer_weight, spread, *weights)


def body(
    homolog_features,
    pair_input,
    cotangent,
    homolog_factor_matrix,
    outer_output_weight,
    outgoing_input_weight,
    outgoing_output_weight,
    incoming_input_weight,
    incoming_output_weight,
):
    sequences, residues, depth = homolog_features.shape
    core = lax.axis_index("row") % 2
    normed, scale = layer_norm(homolog_features.astype(F32))
    projected = jnp.dot(
        normed.astype(BF16), homolog_factor_matrix, preferred_element_type=F32
    ).astype(BF16)
    left, right = projected[..., :HIDDEN], projected[..., HIDDEN:]
    left_ic = left.reshape(sequences, residues * HIDDEN)
    left_ci = left.transpose(0, 2, 1).reshape(sequences, residues * HIDDEN)
    right_dj = right.transpose(0, 2, 1).reshape(sequences, residues * HIDDEN)
    cube = outer_output_weight.reshape(HIDDEN, HIDDEN, WIDTH)
    outer_weight = jnp.broadcast_to(
        cube.transpose(1, 0, 2)[:, None], (HIDDEN, 4, HIDDEN, WIDTH)
    ).reshape(4 * HIDDEN * HIDDEN, WIDTH)
    picked = jnp.where(core == 0, cube.transpose(2, 0, 1), cube.transpose(2, 1, 0))
    spread = (
        jnp.eye(4, dtype=BF16)[:, None, None, :, None] * picked[None, :, :, None, :]
    ).reshape(4 * WIDTH, HIDDEN * WIDTH)
    pair_output, pair_gradient, cots = pair_updates(
        left_ic,
        left_ci,
        right_dj,
        pair_input,
        cotangent,
        outer_weight,
        spread,
        (
            outgoing_input_weight,
            outgoing_output_weight,
            incoming_input_weight,
            incoming_output_weight,
        ),
    )
    cots = cots.reshape(2, sequences, residues, HIDDEN)
    projection_cot = jnp.concatenate([cots[0], cots[1]], axis=-1)
    normed_cot = jnp.dot(
        projection_cot, homolog_factor_matrix.T, preferred_element_type=F32
    )
    normed, scale = layer_norm(homolog_features.astype(F32))
    alignment_gradient = layer_norm_pullback(normed, scale, normed_cot)
    return pair_output, pair_gradient, alignment_gradient


def solution(mesh):
    split = P("row", "col", None)
    return jax.shard_map(
        body,
        mesh=mesh,
        in_specs=(split, split, split, P(), P(), P(), P(), P(), P()),
        out_specs=(split, split, split),
        check_vma=False,
    )
```

time: 953 us -> 166 us (0.17)
  blocking collectives: 458 us -> 0 us
  waiting for transfers between devices: 385 us -> 0 us
  Pallas kernels: 0 us -> 143 us
  matrix products: 34.5 us -> 1.4 us
  local copies, waits for them, and re-layouts: 37.1 us -> 15.1 us
  other arithmetic: 21.5 us -> 4.88 us
  between operations: 15.2 us -> 0.93 us
    all_gather x16 -> x0, blocking collectives: 458 us -> none  [the longest x9 271 us: across_columns(): lax.all_gather(shortened(arrays), 'col', axis=1, tiled=True)]
    psum x6 -> x0, waiting for transfers between devices: 350 us -> none  [broadcast(): return lax.psum(jnp.where(mine, array, jnp.zeros_like(array)), axis)]
    pallas_call x0 -> x1, Pallas kernels: none -> 143 us  [pair_updates(): pl.pallas_call(pair_kernel, out_shape=(jax.ShapeDtypeStruct((8, BLOCK, WI...]
    all_gather x2 -> x0, waiting for transfers between devices: 35.1 us -> none  [spanning_rows(): lax.all_gather(shortened(arrays), 'row', axis=0, tiled=True)]
    dot_general x34 -> x2, matrix products: 34.5 us -> 1.4 us  [the longest x1 0.95 us: body(): jnp.dot(projection_cot, homolog_factor_matrix.T, preferred_element_type=F32)]
    reshape x11 -> x3, local copies, waits for them, and re-layouts: 10 us -> 0.3 us  [the longest x1 0.1 us: body(): left_ic = left.reshape(sequences, residues * HIDDEN)]
  transfers between devices with their start and end apart: 8 -> 0, of which waited for: 7 -> 0; matrix products, arithmetic and copies ran while one was open for 3% -> 0% of each run, Pallas kernels for 0% -> 0%
where the time goes in v1:
time: 166 us; the launch traced here: 165 us
  Pallas kernels  143 us (86%)
  local copies, waits for them, and re-layouts  15.1 us (9%)
  other arithmetic  4.88 us (3%)
    pallas_call x1, Pallas kernels, pair_updates(): pl.pallas_call(pair_kernel, out_shape=(jax.ShapeDtypeStruct((8, BLOCK, WI...  143 us
    mul x1, local copies, waits for them, and re-layouts, body(): jnp.eye(4, dtype=BF16)[:, None, None, :, None] * picked[None, :, :, None, :]  6.51 us
    unnamed x23, local copies, waits for them, and re-layouts  6.14 us

profile of v1, /device:TPU:1, one launch (start us, length us, event | category | flops | bytes accessed | tf_op | source)
XLA Modules:
  0.0 165.3 jit_solution(510392060533709553)
XLA Ops:
  0.7 1.1 bitcast_select_fusion
  1.8 0.1 copy.22
  1.9 1.6 broadcast_multiply_fusion
  3.6 2.7 %copy.34 = bf16[512,8,4,128]{3,1,2,0:T(8,128)(2,1)} copy(bf16[512,8,4,128]{3,2,1,0:T(4,128)(2,1)S(1)} %bitcast.32) | data formatting | bytes 8388608
  6.2 6.5 %copy.26.spread_weight_hbm = bf16[512,4096]{1,0:T(8,128)(2,1)} copy(bf16[512,4096]{0,1:T(8,128)(2,1)} %bitcast.33) | data formatting | bytes 8388608 | tf_op jit(solution)/shard_map/mul | solution.py:709
  12.8 0.2 convert_reduce_fusion
  13.0 0.4 fusion.8
  13.4 0.5 convolution_convert_fusion
  13.9 0.2 slice_bitcast_fusion
  14.1 0.3 copy.17
  14.4 0.3 copy.18
  14.9 0.3 copy.19
  15.3 0.1 copy.20
  15.4 0.2 broadcast_in_dim.2
  15.7 2.2 %copy-done.1 = bf16[512,4096]{1,0:T(8,128)(2,1)S(1)} copy-done((bf16[512,4096]{1,0:T(8,128)(2,1)S(1)}, bf16[512,4096]{1,0:T(8,128)(2,1)}, u32[]{:S(2)}) %copy-start.1) | copy-done | bytes 4194328
  17.8 142.9 %pair_updates.1 = (bf16[8,16,128]{2,1,0:T(8,128)(2,1)S(1)}, f32[8,16,128]{2,1,0:T(8,128)S(1)}, bf16[2,64,512]{2,1,0:T(8,128)(2,1)S(1)}) custom-call(bf16[64,512]{1,0:T(8,128)(2,1)S(1)} %copy.23.left_ic, bf16[64,512]{1,0:T(8,128)(2,1)S(1)} %copy.24.left_ci, bf16[64,512]{1,0:T(8,128)(2,1)S(1)} %copy.25.right_dj, bf16[8,16,128]{2,1,0:T(8,128)(2,1)S(1)} %copy-done.4, ...), custom_call_target="tpu_custom_call" | custom-call | tf_op jit(solution)/shard_map/pair_updates/pallas_call | solution.py:613
  160.8 0.1 copy.27
  160.9 0.3 copy.29
  161.2 0.1 copy.28
  161.3 0.3 copy.30
  161.6 0.9 fusion.20
  162.5 1.5 fusion.7
  164.0 0.6 copy.37
  164.6 0.6 copy.38
  (27 shorter events, 0.4 us)
Async XLA Ops:
  0.6 12.8 %copy-start = (bf16[256,64]{0,1:T(8,128)(2,1)S(1)}, bf16[256,64]{0,1:T(8,128)(2,1)}, u32[]{:S(2)}) copy-start(bf16[256,64]{0,1:T(8,128)(2,1)} %param.12) | copy-start | bytes 98308
  6.2 6.5 %copy-start.8 = (bf16[64,16,256]{2,1,0:T(8,128)(2,1)S(1)}, bf16[64,16,256]{2,1,0:T(8,128)(2,1)}, u32[]{:S(2)}) copy-start(bf16[64,16,256]{2,1,0:T(8,128)(2,1)} %param.9) | copy-start | bytes 1572868
  12.8 2.5 %copy-start.9 = (bf16[1024,128]{1,0:T(8,128)(2,1)S(1)}, bf16[1024,128]{1,0:T(8,128)(2,1)}, u32[]{:S(2)}) copy-start(bf16[1024,128]{1,0:T(8,128)(2,1)} %param.13) | copy-start | bytes 786436
  12.8 2.8 %copy-start.2 = (bf16[128,640]{1,0:T(8,128)(2,1)S(1)}, bf16[128,640]{1,0:T(8,128)(2,1)}, u32[]{:S(2)}) copy-start(bf16[128,640]{1,0:T(8,128)(2,1)} %out_in_weight.1) | copy-start | bytes 491524
  12.8 2.8 %copy-start.3 = (bf16[128,640]{1,0:T(8,128)(2,1)S(1)}, bf16[128,640]{1,0:T(8,128)(2,1)}, u32[]{:S(2)}) copy-start(bf16[128,640]{1,0:T(8,128)(2,1)} %in_in_weight.1) | copy-start | bytes 491524
  12.8 2.8 %copy-start.4 = (bf16[8,16,128]{2,1,0:T(8,128)(2,1)S(1)}, bf16[8,16,128]{2,1,0:T(8,128)(2,1)}, u32[]{:S(2)}) copy-start(bf16[8,16,128]{2,1,0:T(8,128)(2,1)} %pair_input.1) | copy-start | bytes 98308
  12.8 2.8 %copy-start.5 = (bf16[8,16,128]{2,1,0:T(8,128)(2,1)S(1)}, bf16[8,16,128]{2,1,0:T(8,128)(2,1)}, u32[]{:S(2)}) copy-start(bf16[8,16,128]{2,1,0:T(8,128)(2,1)} %cotangent.1) | copy-start | bytes 98308
  12.8 2.8 %copy-start.6 = (bf16[128,128]{1,0:T(8,128)(2,1)S(1)}, bf16[128,128]{1,0:T(8,128)(2,1)}, u32[]{:S(2)}) copy-start(bf16[128,128]{1,0:T(8,128)(2,1)} %out_out_weight.1) | copy-start | bytes 98308
  12.8 2.8 %copy-start.7 = (bf16[128,128]{1,0:T(8,128)(2,1)S(1)}, bf16[128,128]{1,0:T(8,128)(2,1)}, u32[]{:S(2)}) copy-start(bf16[128,128]{1,0:T(8,128)(2,1)} %in_out_weight.1) | copy-start | bytes 98308
  15.6 2.2 %copy-start.1 = (bf16[512,4096]{1,0:T(8,128)(2,1)S(1)}, bf16[512,4096]{1,0:T(8,128)(2,1)}, u32[]{:S(2)}) copy-start(bf16[512,4096]{1,0:T(8,128)(2,1)} %copy.26.spread_weight_hbm) | copy-start | bytes 12582916

commit v2 on v1

--- a/solution.py
+++ b/solution.py
@@ -39,7 +39,6 @@
     pair_input,
     cotangent,
     outer_weight,
-    spread_weight_hbm,
     out_in_weight,
     out_out_weight,
     in_in_weight,
@@ -62,18 +61,20 @@
     i_left_stage,
     ib_right,
     ib_left,
-    ib_cot,
-    ib_cot_turned,
-    ib_cot_stage,
     ob_right,
     ob_left,
-    ob_cot_row,
-    ob_cot_col,
-    ob_cot_stage,
+    left_parts,
+    right_parts,
+    left_parts2,
+    right_parts2,
     final_cot,
+    wide_weight,
+    table_weight,
     spread_weight,
     outer32,
     wide,
+    cot_wide,
+    cot_turned,
     flat,
     proj_out,
     proj_in,
@@ -97,20 +98,32 @@
     final_sem,
     small_sem,
     send_sem,
-    weight_sem,
+    output_sem,
+    gradient_sem,
 ):
     row, col = lax.axis_index("row"), lax.axis_index("col")
     a, h, b = row // 2, row % 2, col
     other = 1 - h
-    own_i = a * other + b * h
-    own_j = b * other + a * h
-    diagonal = a == b
+    odd = b % 2
+    at = (a + 4 * odd) % GRID
+    own_i = at * other + b * h
+    own_j = b * other + at * h
+    stays = jnp.logical_and(a == b, odd == 0)
+
+    def chip_at(i, j):
+        return (i + 4 * (j % 2)) % GRID, j
 
     def row_chip(n):
-        return a * other + n * h, n * other + b * h
+        return chip_at(at * other + n * h, n * other + b * h)
 
     def col_chip(n):
-        return n * other + a * h, b * other + n * h
+        return chip_at(n * other + at * h, b * other + n * h)
+
+    def column(n):
+        return n, b
+
+    def line(n):
+        return chip_at(at, n)
 
     def remote(src, dst, send, recv, chip, core):
         return pltpu.make_async_remote_copy(
@@ -125,9 +138,6 @@
     def wait_for(ref, sem):
         pltpu.make_async_copy(ref, ref, sem).wait()
 
-    weight_copy = pltpu.make_async_copy(spread_weight_hbm, spread_weight, weight_sem)
-    weight_copy.start()
-
     barrier = pltpu.get_barrier_semaphore()
 
     def greet(chip, core):
@@ -137,30 +147,66 @@
 
     def greet_step(k, carry):
         for core in range(2):
-            greet(((a + k) % GRID, b), core)
-            greet((a, (b + k) % GRID), core)
+            greet(column((a + k) % GRID), core)
+            greet(line((b + k) % GRID), core)
         return carry
 
+    def greet_across(k, carry):
+        for core in range(2):
+            greet((a, 2 * k + 1 - odd), core)
+        return carry
+
     lax.fori_loop(1, GRID, greet_step, 0)
+    lax.fori_loop(0, GRID // 2, greet_across, 0)
     greet((a, b), other)
 
-    @pl.when(jnp.logical_not(diagonal))
-    def _():
-        greet((b, a), 0)
-        greet((b, a), 1)
-        pl.semaphore_wait(barrier, 31)
-
-    @pl.when(diagonal)
-    def _():
-        pl.semaphore_wait(barrier, 29)
+    @pl.when(jnp.logical_not(stays))
+    def _():
+        greet((b, at), 0)
+        greet((b, at), 1)
+
+    wide_weight[...] = outer_weight[...].astype(F32)
+    spread_weight[...] = jnp.zeros(spread_weight.shape, BF16)
+
+    def weight_step(n, carry):
+        by_d = wide_weight[pl.ds(n, HIDDEN, stride=HIDDEN), :].astype(BF16)
+        start = pl.multiple_of(n * WIDTH, WIDTH)
+        for q in range(4):
+            table_weight[pl.ds(start + q * HIDDEN, HIDDEN), :] = by_d
+
+        def spread(piece):
+            for q in range(4):
+                spread_weight[
+                    pl.ds(start + q * HIDDEN, HIDDEN), q * WIDTH : (q + 1) * WIDTH
+                ] = piece
+
+        @pl.when(h == 0)
+        def _():
+            spread(outer_weight[pl.ds(pl.multiple_of(n * HIDDEN, HIDDEN), HIDDEN), :])
+
+        @pl.when(h == 1)
+        def _():
+            spread(by_d)
+
+        return carry
+
+    lax.fori_loop(0, HIDDEN, weight_step, 0)
+
+    @pl.when(jnp.logical_not(stays))
+    def _():
+        pl.semaphore_wait(barrier, 39)
+
+    @pl.when(stays)
+    def _():
+        pl.semaphore_wait(barrier, 37)
 
     for slot, (src, dst) in enumerate(((left_ic, relay_left), (right_dj, relay_right))):
 
-        @pl.when(jnp.logical_not(diagonal))
-        def _():
-            remote(src, dst, send_sem.at[slot], relay_sem.at[slot], (b, a), h).start()
-
-        @pl.when(diagonal)
+        @pl.when(jnp.logical_not(stays))
+        def _():
+            remote(src, dst, send_sem.at[slot], relay_sem.at[slot], chip_at(b, a), h).start()
+
+        @pl.when(stays)
         def _():
             pltpu.make_async_copy(src, dst, relay_sem.at[slot]).start()
 
@@ -180,12 +226,6 @@
         def _():
             pltpu.make_async_copy(src, dst.at[slot], sems.at[slot]).start()
 
-    def column(n):
-        return n, b
-
-    def line(n):
-        return a, n
-
     def msa_sent(src, dst, core, send):
         @pl.when(h == core)
         def _():
@@ -198,32 +238,34 @@
     msa_send(right_dj, msa_right, msa_sem.at[1], row, column, a, 0, send_sem.at[2])
     msa_send(left_ic, msa_left, msa_sem.at[0], row, column, a, 1, send_sem.at[3])
 
+    keeps_first = jnp.logical_and(h == 0, odd == 0)
+    keeps_second = jnp.logical_and(h == 1, stays)
     for slot, (src, dst) in enumerate(((pair_input, pair_block), (cotangent, cot_block))):
         half = dst.at[pl.ds(h * 8, 8)]
         sem = block_sem.at[slot, h]
 
-        @pl.when(h == 0)
+        @pl.when(keeps_first)
         def _():
             pltpu.make_async_copy(src, half, sem).start()
 
-        @pl.when(h == 1)
-        def _():
-            remote(src, half, send_sem.at[4 + slot], sem, (a, b), 0).start()
-
-        @pl.when(jnp.logical_and(h == 1, diagonal))
+        @pl.when(jnp.logical_not(keeps_first))
+        def _():
+            remote(src, half, send_sem.at[4 + slot], sem, chip_at(a, b), 0).start()
+
+        @pl.when(keeps_second)
         def _():
             pltpu.make_async_copy(src, half, sem).start()
 
-        @pl.when(jnp.logical_not(jnp.logical_and(h == 1, diagonal)))
-        def _():
-            remote(src, half, send_sem.at[6 + slot], sem, (b, a), 1).start()
+        @pl.when(jnp.logical_not(keeps_second))
+        def _():
+            remote(src, half, send_sem.at[6 + slot], sem, chip_at(b, a), 1).start()
 
     def block_sent(slot, src):
-        @pl.when(h == 1)
+        @pl.when(jnp.logical_not(keeps_first))
         def _():
             wait_for(src, send_sem.at[4 + slot])
 
-        @pl.when(jnp.logical_not(jnp.logical_and(h == 1, diagonal)))
+        @pl.when(jnp.logical_not(keeps_second))
         def _():
             wait_for(src, send_sem.at[6 + slot])
 
@@ -260,7 +302,7 @@
                 )
             )
         picked = jnp.concatenate(columns, axis=1).astype(BF16)
-        weight = outer_weight[pl.ds(pl.multiple_of(d2 * 2 * WIDTH, 2 * WIDTH), 2 * WIDTH), :]
+        weight = table_weight[pl.ds(pl.multiple_of(d2 * 2 * WIDTH, 2 * WIDTH), 2 * WIDTH), :]
         return total + dot(picked, weight)
 
     projected = lax.fori_loop(
@@ -275,6 +317,26 @@
             (pair_block[i].astype(F32) + projected[start : start + BLOCK]).astype(BF16).astype(F32)
         )
 
+    def rows_send(src, core, send, first_step, last_step):
+        target = msa_rows.at[b, pl.ds(pl.multiple_of(h * 64, 64), 64)]
+
+        def step(k, carry):
+            @pl.when(jnp.logical_or(k > 0, h != core))
+            def _():
+                remote(
+                    src, target, send, rows_sem.at[b, h], (a, (b + k) % GRID), core
+                ).start()
+
+            return carry
+
+        lax.fori_loop(first_step, last_step, step, 0)
+
+        if first_step == 0:
+
+            @pl.when(h == core)
+            def _():
+                pltpu.make_async_copy(src, target, rows_sem.at[b, h]).start()
+
     def send_same(dst, sems, chips, own, send):
         def step(k, carry):
             remote(
@@ -293,7 +355,23 @@
 
         lax.fori_loop(0, GRID, step, 0)
 
-    def contract(left, left_sem, left_own, left_by_column, right, right_sem, right_own, own):
+    def block_product(totals, left, by_column, right):
+        def inner(group, totals):
+            totals = list(totals)
+            for u in range(4):
+                t = group * 4 + u
+                across = right(t)
+                for p in range(BLOCK):
+                    one = left[t, pl.ds(p, 1), :] if by_column else left[p, pl.ds(t, 1), :]
+                    totals[p] = totals[p] + one * across
+            return tuple(totals)
+
+        return lax.fori_loop(0, BLOCK // 4, inner, totals)
+
+    def no_totals():
+        return tuple(jnp.zeros((BLOCK, WIDTH), F32) for _ in range(BLOCK))
+
+    def contract(left, left_sem, left_own, by_column, right, right_sem, right_own, own):
         def arrive(ref, sems, slot, skip):
             if skip is None:
                 wait_for(ref.at[slot], sems.at[slot])
@@ -308,30 +386,44 @@
             arrive(left, left_sem, slot, left_own)
             arrive(right, right_sem, slot, right_own)
             wide[...] = left[slot].astype(F32)
-
-            def inner(group, totals):
-                totals = list(totals)
-                for u in range(4):
-                    t = group * 4 + u
-                    across = right[slot, t].astype(F32)
-                    for p in range(BLOCK):
-                        if left_by_column:
-                            one = wide[t, pl.ds(p, 1), :]
-                        else:
-                            one = wide[p, pl.ds(t, 1), :]
-                        totals[p] = totals[p] + one * across
-                return tuple(totals)
-
-            return lax.fori_loop(0, BLOCK // 4, inner, totals)
-
-        zeros = tuple(jnp.zeros((BLOCK, WIDTH), F32) for _ in range(BLOCK))
-        totals = lax.fori_loop(0, GRID, block_step, zeros)
+            return block_product(totals, wide, by_column, lambda t: right[slot, t].astype(F32))
+
+        totals = lax.fori_loop(0, GRID, block_step, no_totals())
         return jnp.concatenate(totals, axis=0)
+
+    def partial(part, n, totals):
+        for p in range(BLOCK):
+            part[n, p] = totals[p].astype(BF16)
+
+    def sum_of(parts, sems, skip, own):
+        def step(k, total):
+            slot = (own + k) % GRID
+            if skip is None:
+                wait_for(parts.at[slot], sems.at[slot])
+            else:
+
+                @pl.when(slot != skip)
+                def _():
+                    wait_for(parts.at[slot], sems.at[slot])
+
+            return total + parts[slot].reshape(BLOCK * BLOCK, WIDTH).astype(F32)
+
+        return lax.fori_loop(0, GRID, step, jnp.zeros((BLOCK * BLOCK, WIDTH), F32))
+
+    def send_part(part, n, dst, slot, sems, chips, core, send):
+        remote(part.at[n], dst.at[slot], send, sems.at[slot], chips(n), core).start()
 
     def turned(value, store):
         flat[...] = value
         for j in range(BLOCK):
             store(j, flat[pl.ds(j, BLOCK, stride=BLOCK), :].astype(BF16))
+
+    def turn_cot(value):
+        rounded = value.astype(BF16).astype(F32)
+        cot_wide[...] = rounded.reshape(BLOCK, BLOCK, WIDTH)
+        flat[...] = rounded
+        for j in range(BLOCK):
+            cot_turned[j] = flat[pl.ds(j, BLOCK, stride=BLOCK), :]
 
     def blocked(value):
         return value.astype(BF16).reshape(BLOCK, BLOCK, WIDTH)
@@ -354,10 +446,7 @@
 
     turned(right, store_right)
     send_other(o_right_stage, o_right, pair_sem.at[1], row_chip, own_j, send_sem.at[11])
-    ob_left[own_i] = o_left[own_j]
-    ob_right[own_i] = blocked(right)
-    send_same(ob_left, pair_sem.at[2], col_chip, own_i, send_sem.at[12])
-    send_same(ob_right, pair_sem.at[3], col_chip, own_i, send_sem.at[13])
+    rows_send(left_ci, 0, send_sem.at[21], 0, 4)
     mixing = contract(
         o_left, pair_sem.at[0], own_j, False, o_right, pair_sem.at[1], None, own_j
     )
@@ -373,10 +462,7 @@
     send_same(i_right, pair_sem.at[4], col_chip, own_i, send_sem.at[14])
     i_left_stage[...] = blocked(gates(projected, 0) * channels(projected, 1))
     send_other(i_left_stage, i_left, pair_sem.at[5], col_chip, own_i, send_sem.at[15])
-    ib_right[own_j] = i_right[own_i]
-    ib_left[own_j] = i_left_stage[...]
-    send_same(ib_right, pair_sem.at[6], row_chip, own_j, send_sem.at[16])
-    send_same(ib_left, pair_sem.at[7], row_chip, own_j, send_sem.at[17])
+    rows_send(left_ci, 0, send_sem.at[21], 4, 8)
     mixing = contract(
         i_left, pair_sem.at[5], None, True, i_right, pair_sem.at[4], own_i, own_i
     )
@@ -410,57 +496,50 @@
     mixing_cot, gating_cot = output_pullback(
         normed, scale, update, gating, in_out_weight, upstream
     )
-    ib_cot[own_i] = blocked(mixing_cot)
-    send_same(ib_cot, pair_sem.at[8], col_chip, own_i, send_sem.at[18])
-
-    def store_cot(j, value):
-        ib_cot_stage[j] = value
-
-    turned(mixing_cot, store_cot)
-    send_other(ib_cot_stage, ib_cot_turned, pair_sem.at[9], row_chip, own_j, send_sem.at[19])
+    turn_cot(mixing_cot)
+
+    def incoming_step(k, carry):
+        n = (own_i + 1 + k) % GRID
+        wide[...] = i_right[n].astype(F32)
+        totals = block_product(no_totals(), wide, False, lambda t: cot_turned[t])
+        partial(left_parts, n, totals)
+        send_part(
+            left_parts, n, ib_left, own_j, pair_sem.at[2], row_chip, other, send_sem.at[12]
+        )
+        wide[...] = i_left[n].astype(F32)
+        totals = block_product(no_totals(), wide, False, lambda t: cot_wide[t])
+
+        @pl.when(n != own_i)
+        def _():
+            partial(right_parts, n, totals)
+            send_part(
+                right_parts, n, ib_right, own_i, pair_sem.at[3], col_chip, h, send_sem.at[13]
+            )
+
+        @pl.when(n == own_i)
+        def _():
+            partial(ib_right, n, totals)
+
+        return carry
+
+    lax.fori_loop(0, GRID, incoming_step, 0)
+    rows_send(right_dj, 1, send_sem.at[24], 0, 4)
+
+    def hand_over(value, stage, got, sem, send):
+        stage[...] = value.reshape(2, 8, BLOCK, WIDTH)
+        for part in range(2):
+            order = remote(stage.at[part], got, send.at[part], sem, (at, b), part)
+            if part == 0:
+                pl.when(odd == 1)(order.start)
+            else:
+                order.start()
 
     @pl.when(h == 0)
     def _():
-        pair_output[...] = result[: BLOCK * BLOCK // 2].reshape(8, BLOCK, WIDTH)
-        output_stage[...] = result[BLOCK * BLOCK // 2 :].reshape(8, BLOCK, WIDTH)
-        remote(output_stage, output_got, send_sem.at[20], small_sem.at[0], (a, b), 1).start()
-
-    line_slot = b
-
-    def rows_send(src, core, send):
-        target = msa_rows.at[line_slot, pl.ds(pl.multiple_of(h * 64, 64), 64)]
-
-        def step(k, carry):
-            @pl.when(jnp.logical_or(k > 0, h != core))
-            def _():
-                remote(
-                    src, target, send, rows_sem.at[line_slot, h], (a, (b + k) % GRID), core
-                ).start()
-
-            return carry
-
-        lax.fori_loop(0, GRID, step, 0)
-
-        @pl.when(h == core)
-        def _():
-            pltpu.make_async_copy(src, target, rows_sem.at[line_slot, h]).start()
-
-    rows_send(left_ci, 0, send_sem.at[21])
-
-    left_cot = contract(
-        ib_right,
-        pair_sem.at[6],
-        own_j,
-        False,
-        ib_cot_turned,
-        pair_sem.at[9],
-        None,
-        own_j,
-    )
-    upstream32[...] = left_cot
-    right_cot = contract(
-        ib_left, pair_sem.at[7], own_j, False, ib_cot, pair_sem.at[8], own_i, own_j
-    )
+        hand_over(result, output_stage, output_got, small_sem.at[0], output_sem)
+
+    upstream32[...] = sum_of(ib_left, pair_sem.at[2], None, own_j)
+    right_cot = sum_of(ib_right, pair_sem.at[3], own_i, own_i)
     second_cot = input_pullback(
         proj_in[...],
         upstream32[...],
@@ -477,21 +556,43 @@
     mixing_cot, gating_cot = output_pullback(
         normed, scale, update, gates(proj_out[...], 4), out_out_weight, second_cot
     )
-    ob_cot_row[own_j] = blocked(mixing_cot)
-    send_same(ob_cot_row, pair_sem.at[10], row_chip, own_j, send_sem.at[22])
-    ob_cot_stage[...] = blocked(mixing_cot)
-    send_other(ob_cot_stage, ob_cot_col, pair_sem.at[11], col_chip, own_i, send_sem.at[23])
-    rows_send(right_dj, 1, send_sem.at[24])
-    left_cot = contract(
-        ob_cot_row, pair_sem.at[10], own_j, False, ob_right, pair_sem.at[3], own_i, own_j
-    )
-    flat[...] = left_cot
-    right_cot = contract(
-        ob_cot_col, pair_sem.at[11], None, True, ob_left, pair_sem.at[2], own_i, own_i
-    )
+    turn_cot(mixing_cot)
+
+    def outgoing_step(k, carry):
+        n = (own_j + 1 + k) % GRID
+        wide[...] = o_right[n].astype(F32)
+        totals = block_product(no_totals(), wide, False, lambda t: cot_turned[t])
+
+        @pl.when(n != own_j)
+        def _():
+            partial(left_parts2, n, totals)
+            send_part(
+                left_parts2, n, ob_left, own_j, pair_sem.at[6], row_chip, h, send_sem.at[16]
+            )
+
+        @pl.when(n == own_j)
+        def _():
+            partial(ob_left, n, totals)
+
+        totals = block_product(
+            no_totals(), cot_wide, True, lambda t: o_left[n, t].astype(F32)
+        )
+        partial(right_parts2, n, totals)
+        send_part(
+            right_parts2, n, ob_right, own_i, pair_sem.at[7], col_chip, other, send_sem.at[17]
+        )
+        return carry
+
+    lax.fori_loop(0, GRID, outgoing_step, 0)
+    rows_send(right_dj, 1, send_sem.at[24], 4, 8)
+    left_turned = sum_of(ob_left, pair_sem.at[6], own_j, own_j)
+    right_cot = sum_of(ob_right, pair_sem.at[7], None, own_i)
+    flat[...] = left_turned
+    for j in range(BLOCK):
+        mixing_out[pl.ds(j * BLOCK, BLOCK), :] = flat[pl.ds(j, BLOCK, stride=BLOCK), :]
     gradient = input_pullback(
         proj_out[...],
-        flat[...],
+        mixing_out[...],
         right_cot,
         gating_cot,
         out_in_weight,
@@ -501,25 +602,22 @@
 
     @pl.when(h == 0)
     def _():
-        pair_gradient[...] = gradient[: BLOCK * BLOCK // 2].reshape(8, BLOCK, WIDTH)
-        gradient_stage[...] = gradient[BLOCK * BLOCK // 2 :].reshape(8, BLOCK, WIDTH)
-        remote(
-            gradient_stage, gradient_got, send_sem.at[25], small_sem.at[1], (a, b), 1
-        ).start()
+        hand_over(gradient, gradient_stage, gradient_got, small_sem.at[1], gradient_sem)
         flat[...] = gradient
         for j in range(BLOCK):
-            final_cot[a, j] = flat[pl.ds(j, BLOCK, stride=BLOCK), :].astype(BF16)
+            final_cot[at, j] = flat[pl.ds(j, BLOCK, stride=BLOCK), :].astype(BF16)
 
     @pl.when(h == 1)
     def _():
-        final_cot[a] = blocked(gradient)
-
-    send_same(final_cot, final_sem, column, a, send_sem.at[26])
-
-    weight_copy.wait()
+        final_cot[at] = blocked(gradient)
+
+    def final_chip(n):
+        return chip_at(n, b)
+
+    send_same(final_cot, final_sem, final_chip, at, send_sem.at[26])
 
     def final_wait(k, carry):
-        slot = (a + k) % GRID
+        slot = (at + k) % GRID
         wait_for(final_cot.at[slot], final_sem.at[slot])
         return carry
 
@@ -531,8 +629,10 @@
             ].reshape(WIDTH, WIDTH)
 
     def table_step(x2, carry):
-        at = pl.multiple_of(x2 * 2 * WIDTH, 2 * WIDTH)
-        chunk = dot(stacked[...], spread_weight[:, pl.ds(at, 2 * WIDTH)]).astype(BF16)
+        begin = pl.multiple_of(x2 * 2 * WIDTH, 2 * WIDTH)
+        chunk = dot(
+            stacked[...], spread_weight[pl.ds(begin, 2 * WIDTH), :], ((1,), (1,))
+        ).astype(BF16)
         for part in range(2):
             start = pl.multiple_of((2 * x2 + part) * BLOCK, BLOCK)
             for g in range(4):
@@ -567,14 +667,19 @@
     wait_for(msa_cot_got, small_sem.at[2])
     msa_cots[h] = msa_cot_got[...]
 
-    @pl.when(h == 1)
+    @pl.when(keeps_first)
+    def _():
+        pair_output[...] = output_stage[0]
+        pair_gradient[...] = gradient_stage[0]
+
+    @pl.when(jnp.logical_not(keeps_first))
     def _():
         wait_for(output_got, small_sem.at[0])
         pair_output[...] = output_got[...]
         wait_for(gradient_got, small_sem.at[1])
         pair_gradient[...] = gradient_got[...]
 
-    @pl.when(jnp.logical_not(diagonal))
+    @pl.when(jnp.logical_not(stays))
     def _():
         wait_for(relay_left, send_sem.at[0])
         wait_for(relay_right, send_sem.at[1])
@@ -585,27 +690,33 @@
     block_sent(1, cotangent)
     msa_sent(relay_left, msa_left, 0, send_sem.at[8])
     msa_sent(relay_right, msa_right, 1, send_sem.at[9])
-    for at in (10, 12, 13, 14, 16, 17, 18, 22, 26):
-        wait_for(o_left.at[pl.ds(0, 7)], send_sem.at[at])
-    for at in (11, 15, 19, 23):
-        wait_for(o_left, send_sem.at[at])
+    for number in (10, 13, 14, 16, 26):
+        wait_for(o_left.at[pl.ds(0, 7)], send_sem.at[number])
+    for number in (11, 12, 15, 17):
+        wait_for(o_left, send_sem.at[number])
     msa_sent(left_ci, msa_left, 0, send_sem.at[21])
     msa_sent(right_dj, msa_left, 1, send_sem.at[24])
     wait_for(msa_cot_got, send_sem.at[27])
 
     @pl.when(h == 0)
     def _():
-        wait_for(output_stage, send_sem.at[20])
-        wait_for(gradient_stage, send_sem.at[25])
-
-
-def pair_updates(left_ic, left_ci, right_dj, pair_input, cotangent, outer_weight, spread, weights):
+        wait_for(output_got, output_sem.at[1])
+        wait_for(gradient_got, gradient_sem.at[1])
+
+        @pl.when(odd == 1)
+        def _():
+            wait_for(output_got, output_sem.at[0])
+            wait_for(gradient_got, gradient_sem.at[0])
+
+
+def pair_updates(left_ic, left_ci, right_dj, pair_input, cotangent, weights):
     gathered = pltpu.VMEM((GRID, BLOCK, BLOCK, WIDTH), BF16)
     block = pltpu.VMEM((BLOCK, BLOCK, WIDTH), BF16)
     flat = pltpu.VMEM((BLOCK * BLOCK, WIDTH), F32)
     shares = pltpu.VMEM((64, BLOCK * HIDDEN), BF16)
     all_sequences = pltpu.VMEM((2 * GRID, 64, BLOCK * HIDDEN), BF16)
     half_block = pltpu.VMEM((8, BLOCK, WIDTH), BF16)
+    wide_block = pltpu.VMEM((BLOCK, BLOCK, WIDTH), F32)
     half_wide = pltpu.VMEM((8, BLOCK, WIDTH), F32)
     projected = pltpu.VMEM((BLOCK * BLOCK, 5 * WIDTH), F32)
     dma = pltpu.SemaphoreType.DMA
@@ -617,7 +728,7 @@
             jax.ShapeDtypeStruct((8, BLOCK, WIDTH), F32),
             jax.ShapeDtypeStruct((2, 64, BLOCK * HIDDEN), BF16),
         ),
-        in_specs=[vmem] * 6 + [pl.BlockSpec(memory_space=pl.ANY)] + [vmem] * 4,
+        in_specs=[vmem] * 10,
         out_specs=(vmem, vmem, vmem),
         scratch_shapes=[
             block,
@@ -637,16 +748,18 @@
             gathered,
             gathered,
             gathered,
-            block,
-            gathered,
-            gathered,
-            gathered,
-            gathered,
-            block,
-            gathered,
-            pltpu.VMEM((4 * WIDTH, HIDDEN * WIDTH), BF16),
+            gathered,
+            gathered,
+            gathered,
+            gathered,
+            gathered,
+            pltpu.VMEM((HIDDEN * HIDDEN, WIDTH), F32),
+            pltpu.VMEM((HIDDEN * WIDTH, WIDTH), BF16),
+            pltpu.VMEM((HIDDEN * WIDTH, 4 * WIDTH), BF16),
             pltpu.VMEM((BLOCK * HIDDEN, BLOCK * HIDDEN), F32),
-            pltpu.VMEM((BLOCK, BLOCK, WIDTH), F32),
+            wide_block,
+            wide_block,
+            wide_block,
             flat,
             projected,
             projected,
@@ -658,25 +771,26 @@
             pltpu.VMEM((GRID, BLOCK * HIDDEN, BLOCK * HIDDEN), BF16),
             pltpu.VMEM((128, BLOCK * HIDDEN), BF16),
             shares,
+            pltpu.VMEM((2, 8, BLOCK, WIDTH), BF16),
             half_block,
-            half_block,
-            half_wide,
+            pltpu.VMEM((2, 8, BLOCK, WIDTH), F32),
             half_wide,
             dma((2,)),
             dma((2, 2)),
             dma((2, 2 * GRID)),
             dma((GRID, 2)),
-            dma((12, GRID)),
+            dma((8, GRID)),
             dma((GRID,)),
             dma((3,)),
             dma((28,)),
-            dma(()),
+            dma((2,)),
+            dma((2,)),
         ],
         compiler_params=pltpu.CompilerParams(
             collective_id=1, has_side_effects=True, vmem_limit_bytes=48 << 20
         ),
         name="pair_updates",
-    )(left_ic, left_ci, right_dj, pair_input, cotangent, outer_weight, spread, *weights)
+    )(left_ic, left_ci, right_dj, pair_input, cotangent, *weights)
 
 
 def body(
@@ -691,7 +805,6 @@
     incoming_output_weight,
 ):
     sequences, residues, depth = homolog_features.shape
-    core = lax.axis_index("row") % 2
     normed, scale = layer_norm(homolog_features.astype(F32))
     projected = jnp.dot(
         normed.astype(BF16), homolog_factor_matrix, preferred_element_type=F32
@@ -700,23 +813,14 @@
     left_ic = left.reshape(sequences, residues * HIDDEN)
     left_ci = left.transpose(0, 2, 1).reshape(sequences, residues * HIDDEN)
     right_dj = right.transpose(0, 2, 1).reshape(sequences, residues * HIDDEN)
-    cube = outer_output_weight.reshape(HIDDEN, HIDDEN, WIDTH)
-    outer_weight = jnp.broadcast_to(
-        cube.transpose(1, 0, 2)[:, None], (HIDDEN, 4, HIDDEN, WIDTH)
-    ).reshape(4 * HIDDEN * HIDDEN, WIDTH)
-    picked = jnp.where(core == 0, cube.transpose(2, 0, 1), cube.transpose(2, 1, 0))
-    spread = (
-        jnp.eye(4, dtype=BF16)[:, None, None, :, None] * picked[None, :, :, None, :]
-    ).reshape(4 * WIDTH, HIDDEN * WIDTH)
     pair_output, pair_gradient, cots = pair_updates(
         left_ic,
         left_ci,
         right_dj,
         pair_input,
         cotangent,
-        outer_weight,
-        spread,
         (
+            outer_output_weight,
             outgoing_input_weight,
             outgoing_output_weight,
             incoming_input_weight,

time: 166 us -> 114 us (0.69)
  Pallas kernels: 143 us -> 104 us
  local copies, waits for them, and re-layouts: 15.1 us -> 4.26 us
  other arithmetic: 4.88 us -> 3.2 us
    pallas_call x1, Pallas kernels: 143 us -> 104 us  [pair_updates(): pl.pallas_call(pair_kernel, out_shape=(jax.ShapeDtypeStruct((8, BLOCK, WI...]
    mul x1 -> x0, local copies, waits for them, and re-layouts: 6.51 us -> none  [body(): jnp.eye(4, dtype=BF16)[:, None, None, :, None] * picked[None, :, :, None, :]]
    unnamed x23 -> x20, local copies, waits for them, and re-layouts: 6.14 us -> 2.14 us
where the time goes in v2:
time: 114 us
  Pallas kernels  104 us (91%)
  local copies, waits for them, and re-layouts  4.26 us (4%)
  other arithmetic  3.2 us (3%)
  matrix products  1.4 us (1%)
    pallas_call x1, Pallas kernels, pair_updates(): pl.pallas_call(pair_kernel, out_shape=(jax.ShapeDtypeStruct((8, BLOCK, WI...  104 us

profile of v2, /device:TPU:1, one launch (start us, length us, event | category | flops | bytes accessed | tf_op | source)
XLA Modules:
  0.0 113.6 jit_solution(6353391476123589224)
XLA Ops:
  0.7 1.3 %convert_reduce_fusion = f32[64,16]{1,0:T(8,128)S(1)} fusion(bf16[64,16,256]{2,1,0:T(8,128)(2,1)} %param.9), kind=kLoop, calls=%fused_computation.1 | loop fusion | flops 523264 | bytes 528384 | tf_op jit(solution)/shard_map/reduce_sum | solution.py:24
  2.0 0.4 fusion.8
  2.4 0.5 convolution_convert_fusion
  2.9 0.2 slice_bitcast_fusion
  3.0 0.3 copy.16
  3.3 0.1 copy.19.right_dj
  3.4 0.3 copy.15
  3.8 0.1 copy.18.left_ci
  3.9 0.3 copy.14
  4.2 0.1 copy.17.left_ic
  4.3 0.2 copy-done.4
  4.5 0.0 copy-done.5
  4.6 0.3 copy-done.1
  4.9 0.0 copy-done.3
  4.9 0.3 copy-done.2
  5.2 103.9 %pair_updates.1 = (bf16[8,16,128]{2,1,0:T(8,128)(2,1)S(1)}, f32[8,16,128]{2,1,0:T(8,128)S(1)}, bf16[2,64,512]{2,1,0:T(8,128)(2,1)S(1)}) custom-call(bf16[64,512]{1,0:T(8,128)(2,1)S(1)} %copy.17.left_ic, bf16[64,512]{1,0:T(8,128)(2,1)S(1)} %copy.18.left_ci, bf16[64,512]{1,0:T(8,128)(2,1)S(1)} %copy.19.right_dj, bf16[8,16,128]{2,1,0:T(8,128)(2,1)S(1)} %copy-done.4, ...), custom_call_target="tpu_custom_call" | custom-call | tf_op jit(solution)/shard_map/pair_updates/pallas_call | solution.py:724
  109.1 0.1 copy.20
  109.3 0.3 copy.22
  109.5 0.1 copy.21
  109.6 0.3 copy.23
  109.9 0.9 fusion.19
  110.9 1.5 %fusion.7 = f32[64,16,256]{2,1,0:T(8,128)} fusion(bf16[64,16,256]{2,1,0:T(8,128)(2,1)S(1)} %copy-done.8, f32[64,16,256]{2,1,0:T(8,128)S(1)} %get-tuple-element.16, f32[64,16]{1,0:T(8,128)S(1)} %get-tuple-element.17, f32[64,16]{1,0:T(8,128)S(1)} %get-tuple-element.18, f32[64,16]{1,0:T(8,128)S(1)} %add_rsqrt_fusion, f32[64,16]{1,0:T(8,128)S(1)} %broadcast_multiply_fusion.2), kind=kLoop, calls=%fused_computation.10 | loop fusion | flops 1835008 | bytes 2637824 | tf_op jit(solution)/shard_map/mul | solution.py:32
  112.4 0.6 copy.26
  113.0 0.6 copy.27
  (17 shorter events, 0.1 us)
Async XLA Ops:
  0.6 1.8 %copy-start = (bf16[256,64]{0,1:T(8,128)(2,1)S(1)}, bf16[256,64]{0,1:T(8,128)(2,1)}, u32[]{:S(2)}) copy-start(bf16[256,64]{0,1:T(8,128)(2,1)} %param.12) | copy-start | bytes 98308
  0.6 1.3 %copy-start.8 = (bf16[64,16,256]{2,1,0:T(8,128)(2,1)S(1)}, bf16[64,16,256]{2,1,0:T(8,128)(2,1)}, u32[]{:S(2)}) copy-start(bf16[64,16,256]{2,1,0:T(8,128)(2,1)} %param.9) | copy-start | bytes 1572868
  3.8 0.8 copy-start.4
  3.8 0.8 copy-start.5
  3.8 0.8 copy-start.6
  3.8 0.8 copy-start.7
  3.9 1.0 copy-start.1
  3.9 1.0 copy-start.3
  4.2 1.0 copy-start.2

commit v3 on v2

v3 whole, which is shorter than its diff:
```python
import jax
import jax.numpy as jnp
from jax import lax
from jax.experimental import pallas as pl
from jax.experimental.pallas import tpu as pltpu
from jax.sharding import PartitionSpec as P

SEQUENCES = 1024
EPSILON = 1e-05
MESH = pl.DeviceIdType.MESH
F32 = jnp.float32
BF16 = jnp.bfloat16
GRID = 8
BLOCK = 16
WIDTH = 128
HIDDEN = 32
ROWS_AT = 2


def dot(lhs, rhs, dims=((1,), (0,))):
    return lax.dot_general(lhs, rhs, (dims, ((), ())), preferred_element_type=F32)


def layer_norm(inputs):
    centered = inputs - jnp.mean(inputs, axis=-1, keepdims=True)
    spread = jnp.mean(centered * centered, axis=-1, keepdims=True)
    scale = lax.rsqrt(spread + EPSILON)
    return centered * scale, scale


def layer_norm_pullback(normed, scale, upstream):
    along = jnp.mean(upstream * normed, axis=-1, keepdims=True)
    return scale * (upstream - jnp.mean(upstream, axis=-1, keepdims=True) - normed * along)


def repeat_factor(factor_weight, spread_factor):
    hidden_row = lax.broadcasted_iota(jnp.int32, (2 * HIDDEN, 2 * WIDTH), 0)
    hidden_lane = lax.broadcasted_iota(jnp.int32, (2 * HIDDEN, 2 * WIDTH), 1)
    repeats = (hidden_lane % HIDDEN + HIDDEN * (hidden_lane // WIDTH) == hidden_row).astype(F32)
    repeated = dot(factor_weight[...], repeats.astype(BF16), ((0,), (0,)))
    lane_quarter = lax.broadcasted_iota(jnp.int32, (2 * WIDTH, 2 * WIDTH), 1) % WIDTH // HIDDEN
    for q in range(4):
        spread_factor[q * 2 * WIDTH : (q + 1) * 2 * WIDTH, :] = jnp.where(
            lane_quarter == q, repeated, 0.0
        ).astype(BF16)


def pair_kernel(
    homolog_hbm,
    factor_weight_hbm,
    pair_input,
    cotangent,
    outer_weight_hbm,
    out_in_weight_hbm,
    out_out_weight_hbm,
    in_in_weight_hbm,
    in_out_weight_hbm,
    pair_output,
    pair_gradient,
    msa_cots,
    homolog,
    factor_weight,
    outer_weight,
    out_in_weight,
    out_out_weight,
    in_in_weight,
    in_out_weight,
    normed_msa,
    spread_factor,
    left_ic,
    left_ci,
    right_dj,
    pair_block,
    cot_block,
    relay_left,
    relay_right,
    msa_left,
    msa_right,
    msa_rows,
    o_left,
    o_right,
    o_right_stage,
    i_left,
    i_right,
    i_left_stage,
    ib_right,
    ib_left,
    ob_right,
    ob_left,
    left_parts,
    right_parts,
    left_parts2,
    right_parts2,
    final_cot,
    wide_weight,
    table_weight,
    spread_weight,
    turned_weight,
    out_in_turned,
    out_out_turned,
    in_in_turned,
    in_out_turned,
    outer32,
    wide,
    cot_wide,
    cot_turned,
    flat,
    out_kept,
    in_kept,
    first,
    upstream32,
    stacked,
    grad_table,
    msa_cot_own,
    msa_cot_got,
    output_stage,
    output_got,
    gradient_stage,
    gradient_got,
    relay_sem,
    relay_send_sem,
    block_sem,
    msa_sem,
    rows_sem,
    pair_sem,
    final_sem,
    small_sem,
    send_sem,
    output_sem,
    gradient_sem,
    input_sem,
):
    row, col = lax.axis_index("row"), lax.axis_index("col")
    a, h, b = row // 2, row % 2, col
    other = 1 - h
    odd = b % 2
    at = (a + 4 * odd) % GRID
    own_i = at * other + b * h
    own_j = b * other + at * h
    stays = jnp.logical_and(a == b, odd == 0)

    def chip_at(i, j):
        return (i + 4 * (j % 2)) % GRID, j

    def row_chip(n):
        return chip_at(at * other + n * h, n * other + b * h)

    def col_chip(n):
        return chip_at(n * other + at * h, b * other + n * h)

    def apart(k):
        m = k // 2
        return m + (m // 2) * (5 - 2 * m), k % 2

    def along_rows(own, k):
        dm, dv = apart(k)
        return (own // 4 + dv) % 2 * 4 + (own % 4 + dm) % 4

    def along_columns(own, k):
        dm, dv = apart(k)
        return (own // 2 + dm) % 4 * 2 + (own % 2 + dv) % 2

    def step_i(k):
        return along_rows(at, k) * other + along_columns(b, k) * h

    def step_j(k):
        return along_columns(b, k) * other + along_rows(at, k) * h

    relay_column = (a % 4 + b // 2 + 2 * (b % 4)) % 4 * 2 + a // 4
    relay_chip = chip_at(b, relay_column)
    source_row = b % 2 * 4 + (b // 2 + 16 - at // 2 - 2 * (at % 4)) % 4
    relay_stays = jnp.logical_and(relay_column == b, relay_chip[0] == a)

    def column(n):
        return n, b

    def line(n):
        return chip_at(at, n)

    def remote(src, dst, send, recv, chip, core):
        return pltpu.make_async_remote_copy(
            src_ref=src,
            dst_ref=dst,
            send_sem=send,
            recv_sem=recv,
            device_id=(2 * chip[0] + core, chip[1]),
            device_id_type=MESH,
        )

    def wait_for(ref, sem):
        pltpu.make_async_copy(ref, ref, sem).wait()

    barrier = pltpu.get_barrier_semaphore()

    def greet(chip, core):
        pl.semaphore_signal(
            barrier, inc=1, device_id=(2 * chip[0] + core, chip[1]), device_id_type=MESH
        )

    def greet_step(k, carry):
        for core in range(2):
            greet(column(along_rows(a, GRID - k)), core)
            greet(line(along_columns(b, GRID - k)), core)
        return carry

    def greet_across(k, carry):
        for core in range(2):
            greet((a, 2 * k + 1 - odd), core)
        return carry

    @pl.when(jnp.logical_not(relay_stays))
    def _():
        greet((source_row, at), h)

    @pl.when(h == 1)
    def _():
        greet((b, at), 0)

    @pl.when(jnp.logical_and(h == 1, jnp.logical_not(stays)))
    def _():
        greet((b, at), 1)

    lax.fori_loop(0, GRID // 2, greet_across, 0)
    lax.fori_loop(1, GRID, greet_step, 0)
    greet((a, b), other)
    inputs = (
        (homolog_hbm, homolog),
        (factor_weight_hbm, factor_weight),
        (outer_weight_hbm, outer_weight),
        (out_in_weight_hbm, out_in_weight),
        (out_out_weight_hbm, out_out_weight),
        (in_in_weight_hbm, in_in_weight),
        (in_out_weight_hbm, in_out_weight),
    )
    copies = [
        pltpu.make_async_copy(src, dst, input_sem.at[number])
        for number, (src, dst) in enumerate(inputs)
    ]
    for copy in copies:
        copy.start()
    copies[0].wait()
    copies[1].wait()

    def normalize_step(n, carry):
        rows = pl.ds(pl.multiple_of(n * 256, 256), 256)
        normed, unused = layer_norm(homolog[rows, :].astype(F32))
        normed_msa[0][rows, :] = normed[:, :WIDTH]
        normed_msa[1][rows, :] = normed[:, WIDTH:]
        return carry

    lax.fori_loop(0, 4, normalize_step, 0)
    repeat_factor(factor_weight, spread_factor)
    groups = []
    for g in range(4):
        pieces = [
            normed_msa[part][pl.ds(4 * g + q, 64, stride=BLOCK), :].astype(BF16)
            for q in range(4)
            for part in range(2)
        ]
        groups.append(jnp.concatenate(pieces, axis=1))
    factors = dot(jnp.concatenate(groups, axis=0), spread_factor[...]).astype(BF16)
    left_value = jnp.concatenate(
        [factors[g * 64 : (g + 1) * 64, :WIDTH] for g in range(4)], axis=1
    )
    right_value = jnp.concatenate(
        [factors[g * 64 : (g + 1) * 64, WIDTH:] for g in range(4)], axis=1
    )
    left_ic[...] = left_value
    before = lax.broadcasted_iota(jnp.int32, (BLOCK * HIDDEN, BLOCK * HIDDEN), 0)
    after = lax.broadcasted_iota(jnp.int32, (BLOCK * HIDDEN, BLOCK * HIDDEN), 1)
    moved = (before == after % BLOCK * HIDDEN + after // BLOCK).astype(F32).astype(BF16)
    turned_factors = dot(jnp.concatenate([left_value, right_value], axis=0), moved).astype(BF16)
    left_ci[...] = turned_factors[:64]
    right_dj[...] = turned_factors[64:]

    for copy in copies[2:]:
        copy.wait()
    keeps_first = jnp.logical_and(h == 0, odd == 0)
    keeps_second = jnp.logical_and(h == 1, stays)
    pl.semaphore_wait(barrier, 39 - relay_stays.astype(jnp.int32) - keeps_second.astype(jnp.int32))

    for slot in range(4):
        src, dst = ((left_ic, relay_left), (right_dj, relay_right))[slot // 2]
        half = pl.ds(slot % 2 * 32, 32)

        @pl.when(jnp.logical_not(relay_stays))
        def _():
            remote(
                src.at[half],
                dst.at[half],
                relay_send_sem.at[slot],
                relay_sem.at[slot],
                relay_chip,
                h,
            ).start()

        @pl.when(relay_stays)
        def _():
            pltpu.make_async_copy(src.at[half], dst.at[half], relay_sem.at[slot]).start()

    def msa_send(src, dst, sems, slot, chip_of, core, send, half=None):
        whole = half is None
        source = src if whole else src.at[pl.ds(half * 32, 32)]
        target = dst.at[slot] if whole else dst.at[slot, pl.ds(half * 32, 32)]

        def step(k, carry):
            place = (GRID - 1 - k) * other + k * h

            @pl.when(jnp.logical_or(place > 0, h != core))
            def _():
                remote(source, target, send, sems.at[slot], chip_of(place), core).start()

            return carry

        lax.fori_loop(0, GRID, step, 0)

        @pl.when(h == core)
        def _():
            pltpu.make_async_copy(source, target, sems.at[slot]).start()

    def column_step(k):
        return column(along_rows(a, k))

    def line_step(k):
        return line(along_columns(b, k))

    def msa_sent(src, dst, core, send):
        @pl.when(h == core)
        def _():
            wait_for(dst.at[pl.ds(0, 7)], send)

        @pl.when(h != core)
        def _():
            wait_for(dst.at[pl.ds(0, 8)], send)

    msa_send(right_dj, msa_right, msa_sem.at[1], row, column_step, 0, send_sem.at[2])
    msa_send(left_ic, msa_left, msa_sem.at[0], row, column_step, 1, send_sem.at[3])

    for slot, (src, dst) in enumerate(((pair_input, pair_block), (cotangent, cot_block))):
        half = dst.at[pl.ds(h * 8, 8)]
        sem = block_sem.at[slot, h]

        @pl.when(keeps_first)
        def _():
            pltpu.make_async_copy(src, half, sem).start()

        @pl.when(jnp.logical_not(keeps_first))
        def _():
            remote(src, half, send_sem.at[4 + slot], sem, chip_at(a, b), 0).start()

        @pl.when(keeps_second)
        def _():
            pltpu.make_async_copy(src, half, sem).start()

        @pl.when(jnp.logical_not(keeps_second))
        def _():
            remote(src, half, send_sem.at[6 + slot], sem, chip_at(b, a), 1).start()

    def block_sent(slot, src):
        @pl.when(jnp.logical_not(keeps_first))
        def _():
            wait_for(src, send_sem.at[4 + slot])

        @pl.when(jnp.logical_not(keeps_second))
        def _():
            wait_for(src, send_sem.at[6 + slot])

    wide_weight[...] = outer_weight[...].astype(F32)
    spread_weight[...] = jnp.zeros(spread_weight.shape, BF16)

    def weight_step(n, carry):
        by_d = wide_weight[pl.ds(n, HIDDEN, stride=HIDDEN), :].astype(BF16)
        start = pl.multiple_of(n * WIDTH, WIDTH)
        for q in range(4):
            table_weight[pl.ds(start + q * HIDDEN, HIDDEN), :] = by_d

        def spread(piece):
            for q in range(4):
                spread_weight[
                    pl.ds(start + q * HIDDEN, HIDDEN), q * WIDTH : (q + 1) * WIDTH
                ] = piece

        @pl.when(h == 0)
        def _():
            spread(outer_weight[pl.ds(pl.multiple_of(n * HIDDEN, HIDDEN), HIDDEN), :])

        @pl.when(h == 1)
        def _():
            spread(by_d)

        return carry

    lax.fori_loop(0, HIDDEN, weight_step, 0)

    relay_slot = 2 * source_row + h
    for slot in range(4):
        half = slot % 2
        src, dst = ((relay_left, msa_left), (relay_right, msa_right))[slot // 2]
        wait_for(src.at[pl.ds(half * 32, 32)], relay_sem.at[slot])
        kind = slot // 2
        msa_send(
            src, dst, msa_sem.at[kind], relay_slot, line_step, kind, send_sem.at[8 + kind], half
        )

    def turn_step(n, carry):
        rows = pl.ds(pl.multiple_of(n * 2 * WIDTH, 2 * WIDTH), 2 * WIDTH)
        turned_weight[:, rows] = spread_weight[rows, :].T
        return carry

    lax.fori_loop(0, HIDDEN // 2, turn_step, 0)
    for weight, turned_one in (
        (out_in_weight, out_in_turned),
        (out_out_weight, out_out_turned),
        (in_in_weight, in_in_turned),
        (in_out_weight, in_out_turned),
    ):
        turned_one[...] = weight[...].T

    def outer_step(k, carry):
        n = (b // 2 + k) % 4

        def msa_wait(part, carry):
            slot = 4 * n + part
            wait_for(msa_left.at[slot], msa_sem.at[0, slot])
            wait_for(msa_right.at[slot], msa_sem.at[1, slot])
            return carry

        lax.fori_loop(0, 4, msa_wait, 0)
        four = pl.ds(4 * n, 4)
        outer32[...] += dot(
            msa_right[four].reshape(256, BLOCK * HIDDEN),
            msa_left[four].reshape(256, BLOCK * HIDDEN),
            ((0,), (0,)),
        )
        return carry

    outer32[...] = jnp.zeros(outer32.shape, F32)
    lax.fori_loop(0, 4, outer_step, 0)
    lane_part = lax.broadcasted_iota(jnp.int32, (BLOCK, WIDTH), 1) // HIDDEN

    def project_step(d8, total):
        columns = []
        for part in range(8):
            tile = outer32[pl.ds(pl.multiple_of((8 * d8 + part) * BLOCK, BLOCK), BLOCK), :]
            columns.append(
                jnp.concatenate(
                    [
                        jnp.where(lane_part == q, tile[:, g * WIDTH : (g + 1) * WIDTH], 0.0)
                        for q in range(4)
                        for g in range(4)
                    ],
                    axis=0,
                )
            )
        picked = (jnp.concatenate(columns, axis=1) * (1.0 / SEQUENCES)).astype(BF16)
        weight = table_weight[pl.ds(pl.multiple_of(d8 * 8 * WIDTH, 8 * WIDTH), 8 * WIDTH), :]
        return total + dot(picked, weight)

    projected = lax.fori_loop(
        0, HIDDEN // 8, project_step, jnp.zeros((BLOCK * BLOCK, WIDTH), F32)
    )
    for part in range(2):
        wait_for(pair_block.at[pl.ds(part * 8, 8)], block_sem.at[0, part])
        wait_for(cot_block.at[pl.ds(part * 8, 8)], block_sem.at[1, part])
    for i in range(BLOCK):
        start = ((i % 4) * 4 + i // 4) * BLOCK
        first[pl.ds(i * BLOCK, BLOCK), :] = (
            (pair_block[i].astype(F32) + projected[start : start + BLOCK]).astype(BF16).astype(F32)
        )

    def rows_send(src, core, send, first_step, last_step):
        target = msa_rows.at[b, pl.ds(pl.multiple_of(h * 64, 64), 64)]

        def step(k, carry):
            @pl.when(jnp.logical_or(k > 0, h != core))
            def _():
                remote(
                    src, target, send, rows_sem.at[b, h], (a, along_columns(b, k)), core
                ).start()

            return carry

        lax.fori_loop(first_step, last_step, step, 0)

        if first_step == 0:

            @pl.when(h == core)
            def _():
                pltpu.make_async_copy(src, target, rows_sem.at[b, h]).start()

    def send_same(dst, sems, chips, steps, send):
        own = steps(0)

        def step(k, carry):
            chip = chips(steps(GRID - k))
            remote(dst.at[own], dst.at[own], send, sems.at[own], chip, h).start()
            return carry

        lax.fori_loop(1, GRID, step, 0)

    def send_other(src, dst, sems, chips, steps, send):
        own = steps(0)

        def step(k, carry):
            chip = chips(steps(GRID - 1 - k))
            remote(src, dst.at[own], send, sems.at[own], chip, other).start()
            return carry

        lax.fori_loop(0, GRID, step, 0)

    def block_product(totals, left, by_column, right):
        def inner(group, totals):
            totals = list(totals)
            for u in range(4):
                t = group * 4 + u
                across = right(t)
                for p in range(BLOCK):
                    one = left[t, pl.ds(p, 1), :] if by_column else left[p, pl.ds(t, 1), :]
                    totals[p] = totals[p] + one * across
            return tuple(totals)

        return lax.fori_loop(0, BLOCK // 4, inner, totals)

    def no_totals():
        return tuple(jnp.zeros((BLOCK, WIDTH), F32) for _ in range(BLOCK))

    def send_rows_at(k, rows):
        @pl.when(k == ROWS_AT)
        def _():
            rows_send(*rows)

    def contract(left, left_sem, left_own, by_column, right, right_sem, right_own, steps, rows):
        def arrive(ref, sems, slot, skip):
            if skip is None:
                wait_for(ref.at[slot], sems.at[slot])
            else:

                @pl.when(slot != skip)
                def _():
                    wait_for(ref.at[slot], sems.at[slot])

        def block_step(k, totals):
            slot = steps(k)
            send_rows_at(k, rows)
            arrive(left, left_sem, slot, left_own)
            arrive(right, right_sem, slot, right_own)
            wide[...] = left[slot].astype(F32)
            return block_product(totals, wide, by_column, lambda t: right[slot, t].astype(F32))

        totals = lax.fori_loop(0, GRID, block_step, no_totals())
        return jnp.concatenate(totals, axis=0)

    def partial(part, n, totals):
        for p in range(BLOCK):
            part[n, p] = totals[p].astype(BF16)

    def sum_of(parts, sems, skip, steps, rows=None):
        def step(k, total):
            slot = steps(k)
            if rows is not None:
                send_rows_at(k, rows)
            if skip is None:
                wait_for(parts.at[slot], sems.at[slot])
            else:

                @pl.when(slot != skip)
                def _():
                    wait_for(parts.at[slot], sems.at[slot])

            return total + parts[slot].reshape(BLOCK * BLOCK, WIDTH).astype(F32)

        return lax.fori_loop(0, GRID, step, jnp.zeros((BLOCK * BLOCK, WIDTH), F32))

    def send_part(part, n, dst, slot, sems, chips, core, send):
        remote(part.at[n], dst.at[slot], send, sems.at[slot], chips(n), core).start()

    def turned(value, store):
        flat[...] = value
        for j in range(BLOCK):
            store(j, flat[pl.ds(j, BLOCK, stride=BLOCK), :].astype(BF16))

    def turn_cot(value):
        rounded = value.astype(BF16).astype(F32)
        cot_wide[...] = rounded.reshape(BLOCK, BLOCK, WIDTH)
        flat[...] = rounded
        for j in range(BLOCK):
            cot_turned[j] = flat[pl.ds(j, BLOCK, stride=BLOCK), :]

    def blocked(value):
        return value.astype(BF16).reshape(BLOCK, BLOCK, WIDTH)

    def gated(normed, weight, at):
        projected = dot(normed, weight[:, at * WIDTH : (at + 2) * WIDTH])
        gate, value = jax.nn.sigmoid(projected[:, :WIDTH]), projected[:, WIDTH:]
        return gate, value

    def keep_gated(ref, first_at, gate, value):
        ref[first_at] = value * gate * (1.0 - gate)
        ref[first_at + 1] = gate

    def keep_norm(ref, first_at, normed, scale):
        ref[first_at] = normed
        ref[first_at + 1] = jnp.broadcast_to(scale, normed.shape)

    normed, scale = layer_norm(first[...])
    rounded = normed.astype(BF16)
    left_gate, left_value = gated(rounded, out_in_weight, 0)
    o_left[own_j] = blocked(left_gate * left_value)
    send_same(o_left, pair_sem.at[0], row_chip, step_j, send_sem.at[10])
    right_gate, right_value = gated(rounded, out_in_weight, 2)

    def store_right(j, value):
        o_right_stage[j] = value

    turned(right_gate * right_value, store_right)
    send_other(o_right_stage, o_right, pair_sem.at[1], row_chip, step_j, send_sem.at[11])
    keep_gated(out_kept, 0, left_gate, left_value)
    keep_gated(out_kept, 2, right_gate, right_value)
    keep_norm(out_kept, 4, normed, scale)
    out_kept[6] = jax.nn.sigmoid(dot(rounded, out_in_weight[:, 4 * WIDTH :]))
    mixing = contract(
        o_left,
        pair_sem.at[0],
        own_j,
        False,
        o_right,
        pair_sem.at[1],
        None,
        step_j,
        (left_ci, 0, send_sem.at[21], 0, 4),
    )
    mixing_normed, mixing_scale = layer_norm(mixing)
    update = dot(mixing_normed.astype(BF16), out_out_weight[...])
    second = (first[...] + out_kept[6] * update).astype(BF16).astype(F32)

    normed, scale = layer_norm(second)
    rounded = normed.astype(BF16)
    right_gate, right_value = gated(rounded, in_in_weight, 2)
    i_right[own_i] = blocked(right_gate * right_value)
    send_same(i_right, pair_sem.at[4], col_chip, step_i, send_sem.at[14])
    left_gate, left_value = gated(rounded, in_in_weight, 0)
    i_left_stage[...] = blocked(left_gate * left_value)
    send_other(i_left_stage, i_left, pair_sem.at[5], col_chip, step_i, send_sem.at[15])
    keep_norm(out_kept, 7, mixing_normed, mixing_scale)
    out_kept[9] = update
    keep_gated(in_kept, 0, left_gate, left_value)
    keep_gated(in_kept, 2, right_gate, right_value)
    keep_norm(in_kept, 4, normed, scale)
    gating = jax.nn.sigmoid(dot(rounded, in_in_weight[:, 4 * WIDTH :]))
    in_kept[6] = gating
    in_kept[7] = second
    upstream = cot_block[...].reshape(BLOCK * BLOCK, WIDTH).astype(F32)
    upstream32[...] = upstream
    in_kept[8] = dot((upstream * gating).astype(BF16), in_out_turned[...])
    mixing = contract(
        i_left,
        pair_sem.at[5],
        None,
        True,
        i_right,
        pair_sem.at[4],
        own_i,
        step_i,
        (left_ci, 0, send_sem.at[21], 4, 8),
    )

    def input_pullback(kept, left_cot, right_cot, gating_part, weight, upstream):
        pieces = [
            (left_cot * kept[0]).astype(BF16),
            (left_cot * kept[1]).astype(BF16),
            (right_cot * kept[2]).astype(BF16),
            (right_cot * kept[3]).astype(BF16),
        ]
        normed_cot = gating_part + dot(
            jnp.concatenate(pieces, axis=1), weight[: 4 * WIDTH, :]
        )
        return upstream + layer_norm_pullback(kept[4], kept[5], normed_cot)

    normed, scale = layer_norm(mixing)
    turn_cot(layer_norm_pullback(normed, scale, in_kept[8]))

    def incoming_step(k, carry):
        n = step_i(GRID - 1 - k)
        wide[...] = i_right[n].astype(F32)
        totals = block_product(no_totals(), wide, False, lambda t: cot_turned[t])
        partial(left_parts, n, totals)
        send_part(
            left_parts, n, ib_left, own_j, pair_sem.at[2], row_chip, other, send_sem.at[12]
        )
        wide[...] = i_left[n].astype(F32)
        totals = block_product(no_totals(), wide, False, lambda t: cot_wide[t])

        @pl.when(n != own_i)
        def _():
            partial(right_parts, n, totals)
            send_part(
                right_parts, n, ib_right, own_i, pair_sem.at[3], col_chip, h, send_sem.at[13]
            )

        @pl.when(n == own_i)
        def _():
            partial(ib_right, n, totals)

        return carry

    lax.fori_loop(0, GRID, incoming_step, 0)
    gating = in_kept[6]
    update = dot(normed.astype(BF16), in_out_weight[...])
    result = (in_kept[7] + gating * update).astype(BF16)
    gating_cot = upstream32[...] * update * gating * (1.0 - gating)
    gating_part = dot(gating_cot.astype(BF16), in_in_turned[4 * WIDTH :, :])

    def hand_over(value, stage, got, sem, send):
        stage[...] = value.reshape(2, 8, BLOCK, WIDTH)
        for part in range(2):
            order = remote(stage.at[part], got, send.at[part], sem, (at, b), part)
            if part == 0:
                pl.when(odd == 1)(order.start)
            else:
                order.start()

    @pl.when(h == 0)
    def _():
        hand_over(result, output_stage, output_got, small_sem.at[0], output_sem)

    left_cot = sum_of(
        ib_left, pair_sem.at[2], None, step_j, (right_dj, 1, send_sem.at[24], 0, 4)
    )
    right_cot = sum_of(ib_right, pair_sem.at[3], own_i, step_i)
    second_cot = input_pullback(
        in_kept, left_cot, right_cot, gating_part, in_in_turned, upstream32[...]
    )

    normed_cot = dot((second_cot * out_kept[6]).astype(BF16), out_out_turned[...])
    turn_cot(layer_norm_pullback(out_kept[7], out_kept[8], normed_cot))

    def outgoing_step(k, carry):
        n = step_j(GRID - 1 - k)
        wide[...] = o_right[n].astype(F32)
        totals = block_product(no_totals(), wide, False, lambda t: cot_turned[t])

        @pl.when(n != own_j)
        def _():
            partial(left_parts2, n, totals)
            send_part(
                left_parts2, n, ob_left, own_j, pair_sem.at[6], row_chip, h, send_sem.at[16]
            )

        @pl.when(n == own_j)
        def _():
            partial(ob_left, n, totals)

        totals = block_product(
            no_totals(), cot_wide, True, lambda t: o_left[n, t].astype(F32)
        )
        partial(right_parts2, n, totals)
        send_part(
            right_parts2, n, ob_right, own_i, pair_sem.at[7], col_chip, other, send_sem.at[17]
        )
        return carry

    lax.fori_loop(0, GRID, outgoing_step, 0)
    gating = out_kept[6]
    gating_cot = second_cot * out_kept[9] * gating * (1.0 - gating)
    gating_part = dot(gating_cot.astype(BF16), out_in_turned[4 * WIDTH :, :])
    flat[...] = sum_of(
        ob_left, pair_sem.at[6], own_j, step_j, (right_dj, 1, send_sem.at[24], 4, 8)
    )
    left_cot = jnp.concatenate(
        [flat[pl.ds(j, BLOCK, stride=BLOCK), :] for j in range(BLOCK)], axis=0
    )
    right_cot = sum_of(ob_right, pair_sem.at[7], None, step_i)
    gradient = input_pullback(
        out_kept, left_cot, right_cot, gating_part, out_in_turned, second_cot
    )

    @pl.when(h == 0)
    def _():
        hand_over(gradient, gradient_stage, gradient_got, small_sem.at[1], gradient_sem)
        flat[...] = gradient
        for j in range(BLOCK):
            final_cot[at, j] = flat[pl.ds(j, BLOCK, stride=BLOCK), :].astype(BF16)

    @pl.when(h == 1)
    def _():
        final_cot[at] = blocked(gradient)

    def final_chip(n):
        return chip_at(n, b)

    def final_step(k):
        return along_rows(at, k)

    send_same(final_cot, final_sem, final_chip, final_step, send_sem.at[26])

    def final_half(part, total):
        def stack_step(k, carry):
            slot = final_step(4 * part + k)

            @pl.when(slot != at)
            def _():
                wait_for(final_cot.at[slot], final_sem.at[slot])

            for g in range(4):
                rows = pl.ds(pl.multiple_of(g * 64 + k * BLOCK, BLOCK), BLOCK)
                for q in range(4):
                    stacked[rows, q * WIDTH : (q + 1) * WIDTH] = final_cot[slot, 4 * g + q]
            return carry

        lax.fori_loop(0, 4, stack_step, 0)

        def table_step(x8, carry):
            begin = pl.multiple_of(x8 * 8 * WIDTH, 8 * WIDTH)
            chunk = dot(stacked[...], turned_weight[:, pl.ds(begin, 8 * WIDTH)]).astype(BF16)
            for piece in range(8):
                start = pl.multiple_of((8 * x8 + piece) * BLOCK, BLOCK)
                for g in range(4):
                    for k in range(4):
                        row = g * 64 + k * BLOCK
                        grad_table[k, pl.ds(start, BLOCK), g * WIDTH : (g + 1) * WIDTH] = chunk[
                            row : row + BLOCK, piece * WIDTH : (piece + 1) * WIDTH
                        ]
            return carry

        lax.fori_loop(0, HIDDEN // 8, table_step, 0)
        sequences = []
        for k in range(4):
            slot = final_step(4 * part + k)
            for piece in range(2):
                wait_for(msa_rows.at[slot, pl.ds(piece * 64, 64)], rows_sem.at[slot, piece])
            sequences.append(msa_rows[slot])
        return total + dot(
            jnp.concatenate(sequences, axis=1),
            grad_table[...].reshape(4 * BLOCK * HIDDEN, BLOCK * HIDDEN),
        )

    total = lax.fori_loop(0, 2, final_half, jnp.zeros((128, BLOCK * HIDDEN), F32))
    msa_cot_own[...] = (total * (1.0 / SEQUENCES)).astype(BF16)
    remote(
        msa_cot_own.at[pl.ds(pl.multiple_of(other * 64, 64), 64)],
        msa_cot_got,
        send_sem.at[27],
        small_sem.at[2],
        (a, b),
        other,
    ).start()
    msa_cots[other] = msa_cot_own[pl.ds(pl.multiple_of(h * 64, 64), 64), :]
    wait_for(msa_cot_got, small_sem.at[2])
    msa_cots[h] = msa_cot_got[...]

    @pl.when(keeps_first)
    def _():
        pair_output[...] = output_stage[0]
        pair_gradient[...] = gradient_stage[0]

    @pl.when(jnp.logical_not(keeps_first))
    def _():
        wait_for(output_got, small_sem.at[0])
        pair_output[...] = output_got[...]
        wait_for(gradient_got, small_sem.at[1])
        pair_gradient[...] = gradient_got[...]

    @pl.when(jnp.logical_not(relay_stays))
    def _():
        for slot in range(4):
            wait_for(relay_left.at[pl.ds(0, 32)], relay_send_sem.at[slot])

    msa_sent(right_dj, msa_right, 0, send_sem.at[2])
    msa_sent(left_ic, msa_left, 1, send_sem.at[3])
    block_sent(0, pair_input)
    block_sent(1, cotangent)
    msa_sent(relay_left, msa_left, 0, send_sem.at[8])
    msa_sent(relay_right, msa_right, 1, send_sem.at[9])
    for number in (10, 13, 14, 16, 26):
        wait_for(o_left.at[pl.ds(0, 7)], send_sem.at[number])
    for number in (11, 12, 15, 17):
        wait_for(o_left, send_sem.at[number])
    msa_sent(left_ci, msa_left, 0, send_sem.at[21])
    msa_sent(right_dj, msa_left, 1, send_sem.at[24])
    wait_for(msa_cot_got, send_sem.at[27])

    @pl.when(h == 0)
    def _():
        wait_for(output_got, output_sem.at[1])
        wait_for(gradient_got, gradient_sem.at[1])

        @pl.when(odd == 1)
        def _():
            wait_for(output_got, output_sem.at[0])
            wait_for(gradient_got, gradient_sem.at[0])


def pair_updates(homolog, factor_weight, pair_input, cotangent, weights):
    gathered = pltpu.VMEM((GRID, BLOCK, BLOCK, WIDTH), BF16)
    block = pltpu.VMEM((BLOCK, BLOCK, WIDTH), BF16)
    flat = pltpu.VMEM((BLOCK * BLOCK, WIDTH), F32)
    shares = pltpu.VMEM((64, BLOCK * HIDDEN), BF16)
    all_sequences = pltpu.VMEM((2 * GRID, 64, BLOCK * HIDDEN), BF16)
    half_block = pltpu.VMEM((8, BLOCK, WIDTH), BF16)
    wide_block = pltpu.VMEM((BLOCK, BLOCK, WIDTH), F32)
    half_wide = pltpu.VMEM((8, BLOCK, WIDTH), F32)
    dma = pltpu.SemaphoreType.DMA
    vmem = pl.BlockSpec(memory_space=pltpu.VMEM)
    return pl.pallas_call(
        pair_kernel,
        out_shape=(
            jax.ShapeDtypeStruct((8, BLOCK, WIDTH), BF16),
            jax.ShapeDtypeStruct((8, BLOCK, WIDTH), F32),
            jax.ShapeDtypeStruct((2, 64, BLOCK * HIDDEN), BF16),
        ),
        in_specs=[pl.BlockSpec(memory_space=pl.ANY)] * 9,
        out_specs=(vmem, vmem, vmem),
        scratch_shapes=[
            pltpu.VMEM((64 * BLOCK, 2 * WIDTH), BF16),
            pltpu.VMEM((2 * HIDDEN, 2 * WIDTH), BF16),
            pltpu.VMEM((HIDDEN * HIDDEN, WIDTH), BF16),
            pltpu.VMEM((WIDTH, 5 * WIDTH), BF16),
            pltpu.VMEM((WIDTH, WIDTH), BF16),
            pltpu.VMEM((WIDTH, 5 * WIDTH), BF16),
            pltpu.VMEM((WIDTH, WIDTH), BF16),
            [pltpu.VMEM((64 * BLOCK, WIDTH), F32)] * 2,
            pltpu.VMEM((8 * WIDTH, 2 * WIDTH), BF16),
            shares,
            shares,
            shares,
            block,
            block,
            shares,
            shares,
            all_sequences,
            all_sequences,
            pltpu.VMEM((GRID, 128, BLOCK * HIDDEN), BF16),
            gathered,
            gathered,
            block,
            gathered,
            gathered,
            block,
            gathered,
            gathered,
            gathered,
            gathered,
            gathered,
            gathered,
            gathered,
            gathered,
            gathered,
            pltpu.VMEM((HIDDEN * HIDDEN, WIDTH), F32),
            pltpu.VMEM((HIDDEN * WIDTH, WIDTH), BF16),
            pltpu.VMEM((HIDDEN * WIDTH, 4 * WIDTH), BF16),
            pltpu.VMEM((4 * WIDTH, HIDDEN * WIDTH), BF16),
            pltpu.VMEM((5 * WIDTH, WIDTH), BF16),
            pltpu.VMEM((WIDTH, WIDTH), BF16),
            pltpu.VMEM((5 * WIDTH, WIDTH), BF16),
            pltpu.VMEM((WIDTH, WIDTH), BF16),
            pltpu.VMEM((BLOCK * HIDDEN, BLOCK * HIDDEN), F32),
            wide_block,
            wide_block,
            wide_block,
            flat,
            pltpu.VMEM((10, BLOCK * BLOCK, WIDTH), F32),
            pltpu.VMEM((9, BLOCK * BLOCK, WIDTH), F32),
            flat,
            flat,
            pltpu.VMEM((2 * WIDTH, 4 * WIDTH), BF16),
            pltpu.VMEM((4, BLOCK * HIDDEN, BLOCK * HIDDEN), BF16),
            pltpu.VMEM((128, BLOCK * HIDDEN), BF16),
            shares,
            pltpu.VMEM((2, 8, BLOCK, WIDTH), BF16),
            half_block,
            pltpu.VMEM((2, 8, BLOCK, WIDTH), F32),
            half_wide,
            dma((4,)),
            dma((4,)),
            dma((2, 2)),
            dma((2, 2 * GRID)),
            dma((GRID, 2)),
            dma((8, GRID)),
            dma((GRID,)),
            dma((3,)),
            dma((28,)),
            dma((2,)),
            dma((2,)),
            dma((7,)),
        ],
        compiler_params=pltpu.CompilerParams(
            collective_id=1, has_side_effects=True, vmem_limit_bytes=62 << 20
        ),
        name="pair_updates",
    )(homolog, factor_weight, pair_input, cotangent, *weights)


def finish_kernel(
    homolog_hbm,
    factor_weight_hbm,
    msa_cots_hbm,
    pair_output,
    pair_gradient,
    pair_output_out,
    pair_gradient_out,
    alignment_gradient,
    homolog,
    factor_weight,
    msa_cots,
    wide,
    result,
    spread_factor,
    copy_sem,
):
    copies = [
        pltpu.make_async_copy(src, dst, copy_sem.at[number])
        for number, (src, dst) in enumerate(
            (
                (homolog_hbm, homolog),
                (factor_weight_hbm, factor_weight),
                (msa_cots_hbm, msa_cots),
                (pair_gradient, pair_gradient_out),
                (pair_output, pair_output_out),
            )
        )
    ]
    for copy in copies:
        copy.start()
    copies[0].wait()
    copies[1].wait()
    for part in range(2):
        wide[part][...] = homolog[:, part * WIDTH : (part + 1) * WIDTH].astype(F32)
    repeat_factor(factor_weight, spread_factor)
    copies[2].wait()
    cots = jnp.concatenate(
        [
            jnp.concatenate(
                [msa_cots[kind, :, g * WIDTH : (g + 1) * WIDTH] for kind in range(2)], axis=1
            )
            for g in range(4)
        ],
        axis=0,
    )
    for q in range(4):
        normed_cots = dot(
            cots, spread_factor[q * 2 * WIDTH : (q + 1) * 2 * WIDTH, :], ((1,), (1,))
        )
        for g in range(4):
            rows = pl.ds(4 * g + q, 64, stride=BLOCK)
            normed, scale = layer_norm(
                jnp.concatenate([wide[0][rows, :], wide[1][rows, :]], axis=1)
            )
            value = layer_norm_pullback(normed, scale, normed_cots[g * 64 : (g + 1) * 64])
            for part in range(2):
                result[part][rows, :] = value[:, part * WIDTH : (part + 1) * WIDTH]
    for part in range(2):
        alignment_gradient[:, part * WIDTH : (part + 1) * WIDTH] = result[part][...]
    copies[3].wait()
    copies[4].wait()


def body(
    homolog_features,
    pair_input,
    cotangent,
    homolog_factor_matrix,
    outer_output_weight,
    outgoing_input_weight,
    outgoing_output_weight,
    incoming_input_weight,
    incoming_output_weight,
):
    sequences, residues, depth = homolog_features.shape
    homolog = homolog_features.reshape(sequences * residues, depth)
    factor_weight = homolog_factor_matrix.T
    pair_output, pair_gradient, cots = pair_updates(
        homolog,
        factor_weight,
        pair_input,
        cotangent,
        (
            outer_output_weight,
            outgoing_input_weight,
            outgoing_output_weight,
            incoming_input_weight,
            incoming_output_weight,
        ),
    )
    vmem = pl.BlockSpec(memory_space=pltpu.VMEM)
    anywhere = pl.BlockSpec(memory_space=pl.ANY)
    pair_output, pair_gradient, alignment_gradient = pl.pallas_call(
        finish_kernel,
        out_shape=(
            jax.ShapeDtypeStruct(pair_output.shape, BF16),
            jax.ShapeDtypeStruct(pair_gradient.shape, F32),
            jax.ShapeDtypeStruct((sequences * residues, depth), F32),
        ),
        in_specs=[anywhere] * 5,
        out_specs=(anywhere, anywhere, vmem),
        scratch_shapes=[
            pltpu.VMEM((sequences * residues, depth), BF16),
            pltpu.VMEM((2 * HIDDEN, depth), BF16),
            pltpu.VMEM((2, sequences, residues * HIDDEN), BF16),
            [pltpu.VMEM((64 * BLOCK, WIDTH), F32)] * 2,
            [pltpu.VMEM((64 * BLOCK, WIDTH), F32)] * 2,
            pltpu.VMEM((8 * WIDTH, 2 * WIDTH), BF16),
            pltpu.SemaphoreType.DMA((5,)),
        ],
        compiler_params=pltpu.CompilerParams(vmem_limit_bytes=62 << 20),
        name="finish",
    )(homolog, factor_weight, cots, pair_output, pair_gradient)
    return pair_output, pair_gradient, alignment_gradient.reshape(sequences, residues, depth)


def solution(mesh):
    split = P("row", "col", None)
    return jax.shard_map(
        body,
        mesh=mesh,
        in_specs=(split, split, split, P(), P(), P(), P(), P(), P()),
        out_specs=(split, split, split),
        check_vma=False,
    )
```

time: 114 us -> 101 us (0.89)
  local copies, waits for them, and re-layouts: 4.26 us -> 0 us
  Pallas kernels: 104 us -> 99.8 us
  other arithmetic: 3.2 us -> 0 us
  matrix products: 1.4 us -> 0 us
    pallas_call x1, Pallas kernels: 104 us -> 94.7 us  [pair_updates(): pl.pallas_call(pair_kernel, out_shape=(jax.ShapeDtypeStruct((8, BLOCK, WI...]
    pallas_call x0 -> x1, Pallas kernels: none -> 5.1 us  [body(): pl.pallas_call(finish_kernel, out_shape=(jax.ShapeDtypeStruct(pair_output...]
    unnamed x20 -> x0, local copies, waits for them, and re-layouts: 2.14 us -> none
    reduce_sum x2 -> x0, other arithmetic: 1.67 us -> none  [the longest x1 1.31 us: layer_norm(): centered = inputs - jnp.mean(inputs, axis=-1, keepdims=True)]
    mul x1 -> x0, other arithmetic: 1.5 us -> none  [layer_norm_pullback(): scale * (upstream - jnp.mean(upstream, axis=-1, keepdims=True) - normed *...]
    dot_general x2 -> x0, matrix products: 1.4 us -> none  [the longest x1 0.95 us: body(): jnp.dot(projection_cot, homolog_factor_matrix.T, preferred_element_type=F32)]
where the time goes in v3:
time: 101 us; the launch traced here: 100 us
  Pallas kernels  99.8 us (99%)
    pallas_call x1, Pallas kernels, pair_updates(): pl.pallas_call(pair_kernel, out_shape=(jax.ShapeDtypeStruct((8, BLOCK, WI...  94.7 us
    pallas_call x1, Pallas kernels, body(): pl.pallas_call(finish_kernel, out_shape=(jax.ShapeDtypeStruct(pair_output...  5.1 us

profile of v3, /device:TPU:1, one launch (start us, length us, event | category | flops | bytes accessed | tf_op | source)
XLA Modules:
  0.0 100.5 jit_solution(16277638266067248319)
XLA Ops:
  0.6 94.7 %pair_updates.1 = (bf16[8,16,128]{2,1,0:T(8,128)(2,1)}, f32[8,16,128]{2,1,0:T(8,128)}, bf16[2,64,512]{2,1,0:T(8,128)(2,1)}) custom-call(bf16[1024,256]{1,0:T(8,128)(2,1)} %bitcast.3, bf16[64,256]{1,0:T(8,128)(2,1)} %bitcast.5, bf16[8,16,128]{2,1,0:T(8,128)(2,1)} %pair_input.1, bf16[8,16,128]{2,1,0:T(8,128)(2,1)} %cotangent.1, ...), custom_call_target="tpu_custom_call" | custom-call | tf_op jit(solution)/shard_map/pair_updates/pallas_call | solution.py:904
  95.4 5.1 %finish.1 = (bf16[8,16,128]{2,1,0:T(8,128)(2,1)}, f32[8,16,128]{2,1,0:T(8,128)}, f32[1024,256]{1,0:T(8,128)}) custom-call(bf16[1024,256]{1,0:T(8,128)(2,1)} %bitcast.4, bf16[64,256]{1,0:T(8,128)(2,1)} %bitcast.6, bf16[2,64,512]{2,1,0:T(8,128)(2,1)} %get-tuple-element.9.msa_cots_hbm, bf16[8,16,128]{2,1,0:T(8,128)(2,1)} %get-tuple-element.10.pair_output, ...), custom_call_target="tpu_custom_call" | custom-call | tf_op jit(solution)/shard_map/finish/pallas_call | solution.py:1086

commit v4 on v3

--- a/solution.py
+++ b/solution.py
@@ -15,6 +15,7 @@
 WIDTH = 128
 HIDDEN = 32
 ROWS_AT = 2
+ROWS_PARTS = ((), (), (0, 7), (6, 5), (4, 3), (2, 1))
 
 
 def dot(lhs, rhs, dims=((1,), (0,))):
@@ -57,7 +58,7 @@
     in_out_weight_hbm,
     pair_output,
     pair_gradient,
-    msa_cots,
+    alignment_gradient,
     homolog,
     factor_weight,
     outer_weight,
@@ -66,6 +67,8 @@
     in_in_weight,
     in_out_weight,
     normed_msa,
+    msa_scale,
+    alignment,
     spread_factor,
     left_ic,
     left_ci,
@@ -111,6 +114,7 @@
     upstream32,
     stacked,
     grad_table,
+    msa_cots,
     msa_cot_own,
     msa_cot_got,
     output_stage,
@@ -129,6 +133,7 @@
     output_sem,
     gradient_sem,
     input_sem,
+    alignment_sem,
 ):
     row, col = lax.axis_index("row"), lax.axis_index("col")
     a, h, b = row // 2, row % 2, col
@@ -243,7 +248,8 @@
 
     def normalize_step(n, carry):
         rows = pl.ds(pl.multiple_of(n * 256, 256), 256)
-        normed, unused = layer_norm(homolog[rows, :].astype(F32))
+        normed, scale = layer_norm(homolog[rows, :].astype(F32))
+        msa_scale[rows, :] = jnp.broadcast_to(scale, (256, WIDTH))
         normed_msa[0][rows, :] = normed[:, :WIDTH]
         normed_msa[1][rows, :] = normed[:, WIDTH:]
         return carry
@@ -324,6 +330,27 @@
     def line_step(k):
         return line(along_columns(b, k))
 
+    def rows_send(src, core, send, steps):
+        target = msa_rows.at[b, pl.ds(pl.multiple_of(h * 64, 64), 64)]
+        sem = rows_sem.at[b, h]
+        for k in steps:
+            if k == 0:
+
+                @pl.when(h == core)
+                def _():
+                    pltpu.make_async_copy(src, target, sem).start()
+
+                @pl.when(h != core)
+                def _():
+                    remote(src, target, send, sem, (a, b), core).start()
+
+            else:
+                remote(src, target, send, sem, (a, along_columns(b, k)), core).start()
+
+    def rows_pair(steps):
+        rows_send(left_ci, 0, send_sem.at[21], steps)
+        rows_send(right_dj, 1, send_sem.at[24], steps)
+
     def msa_sent(src, dst, core, send):
         @pl.when(h == core)
         def _():
@@ -335,6 +362,8 @@
 
     msa_send(right_dj, msa_right, msa_sem.at[1], row, column_step, 0, send_sem.at[2])
     msa_send(left_ic, msa_left, msa_sem.at[0], row, column_step, 1, send_sem.at[3])
+
+    rows_pair(ROWS_PARTS[0])
 
     for slot, (src, dst) in enumerate(((pair_input, pair_block), (cotangent, cot_block))):
         half = dst.at[pl.ds(h * 8, 8)]
@@ -364,33 +393,6 @@
         @pl.when(jnp.logical_not(keeps_second))
         def _():
             wait_for(src, send_sem.at[6 + slot])
-
-    wide_weight[...] = outer_weight[...].astype(F32)
-    spread_weight[...] = jnp.zeros(spread_weight.shape, BF16)
-
-    def weight_step(n, carry):
-        by_d = wide_weight[pl.ds(n, HIDDEN, stride=HIDDEN), :].astype(BF16)
-        start = pl.multiple_of(n * WIDTH, WIDTH)
-        for q in range(4):
-            table_weight[pl.ds(start + q * HIDDEN, HIDDEN), :] = by_d
-
-        def spread(piece):
-            for q in range(4):
-                spread_weight[
-                    pl.ds(start + q * HIDDEN, HIDDEN), q * WIDTH : (q + 1) * WIDTH
-                ] = piece
-
-        @pl.when(h == 0)
-        def _():
-            spread(outer_weight[pl.ds(pl.multiple_of(n * HIDDEN, HIDDEN), HIDDEN), :])
-
-        @pl.when(h == 1)
-        def _():
-            spread(by_d)
-
-        return carry
-
-    lax.fori_loop(0, HIDDEN, weight_step, 0)
 
     relay_slot = 2 * source_row + h
     for slot in range(4):
@@ -401,6 +403,35 @@
         msa_send(
             src, dst, msa_sem.at[kind], relay_slot, line_step, kind, send_sem.at[8 + kind], half
         )
+
+    wide_weight[...] = outer_weight[...].astype(F32)
+    spread_weight[...] = jnp.zeros(spread_weight.shape, BF16)
+
+    def weight_step(n, carry):
+        by_d = wide_weight[pl.ds(n, HIDDEN, stride=HIDDEN), :].astype(BF16)
+        start = pl.multiple_of(n * WIDTH, WIDTH)
+        for q in range(4):
+            table_weight[pl.ds(start + q * HIDDEN, HIDDEN), :] = by_d
+
+        def spread(piece):
+            for q in range(4):
+                spread_weight[
+                    pl.ds(start + q * HIDDEN, HIDDEN), q * WIDTH : (q + 1) * WIDTH
+                ] = piece
+
+        @pl.when(h == 0)
+        def _():
+            spread(outer_weight[pl.ds(pl.multiple_of(n * HIDDEN, HIDDEN), HIDDEN), :])
+
+        @pl.when(h == 1)
+        def _():
+            spread(by_d)
+
+        return carry
+
+    lax.fori_loop(0, HIDDEN, weight_step, 0)
+
+    rows_pair(ROWS_PARTS[1])
 
     def turn_step(n, carry):
         rows = pl.ds(pl.multiple_of(n * 2 * WIDTH, 2 * WIDTH), 2 * WIDTH)
@@ -468,26 +499,6 @@
             (pair_block[i].astype(F32) + projected[start : start + BLOCK]).astype(BF16).astype(F32)
         )
 
-    def rows_send(src, core, send, first_step, last_step):
-        target = msa_rows.at[b, pl.ds(pl.multiple_of(h * 64, 64), 64)]
-
-        def step(k, carry):
-            @pl.when(jnp.logical_or(k > 0, h != core))
-            def _():
-                remote(
-                    src, target, send, rows_sem.at[b, h], (a, along_columns(b, k)), core
-                ).start()
-
-            return carry
-
-        lax.fori_loop(first_step, last_step, step, 0)
-
-        if first_step == 0:
-
-            @pl.when(h == core)
-            def _():
-                pltpu.make_async_copy(src, target, rows_sem.at[b, h]).start()
-
     def send_same(dst, sems, chips, steps, send):
         own = steps(0)
 
@@ -527,7 +538,7 @@
     def send_rows_at(k, rows):
         @pl.when(k == ROWS_AT)
         def _():
-            rows_send(*rows)
+            rows_pair(rows)
 
     def contract(left, left_sem, left_own, by_column, right, right_sem, right_own, steps, rows):
         def arrive(ref, sems, slot, skip):
@@ -627,7 +638,7 @@
         pair_sem.at[1],
         None,
         step_j,
-        (left_ci, 0, send_sem.at[21], 0, 4),
+        ROWS_PARTS[2],
     )
     mixing_normed, mixing_scale = layer_norm(mixing)
     update = dot(mixing_normed.astype(BF16), out_out_weight[...])
@@ -661,7 +672,7 @@
         pair_sem.at[4],
         own_i,
         step_i,
-        (left_ci, 0, send_sem.at[21], 4, 8),
+        ROWS_PARTS[3],
     )
 
     def input_pullback(kept, left_cot, right_cot, gating_part, weight, upstream):
@@ -724,7 +735,7 @@
         hand_over(result, output_stage, output_got, small_sem.at[0], output_sem)
 
     left_cot = sum_of(
-        ib_left, pair_sem.at[2], None, step_j, (right_dj, 1, send_sem.at[24], 0, 4)
+        ib_left, pair_sem.at[2], None, step_j, ROWS_PARTS[4]
     )
     right_cot = sum_of(ib_right, pair_sem.at[3], own_i, step_i)
     second_cot = input_pullback(
@@ -764,7 +775,7 @@
     gating_cot = second_cot * out_kept[9] * gating * (1.0 - gating)
     gating_part = dot(gating_cot.astype(BF16), out_in_turned[4 * WIDTH :, :])
     flat[...] = sum_of(
-        ob_left, pair_sem.at[6], own_j, step_j, (right_dj, 1, send_sem.at[24], 4, 8)
+        ob_left, pair_sem.at[6], own_j, step_j, ROWS_PARTS[5]
     )
     left_cot = jnp.concatenate(
         [flat[pl.ds(j, BLOCK, stride=BLOCK), :] for j in range(BLOCK)], axis=0
@@ -848,6 +859,39 @@
     wait_for(msa_cot_got, small_sem.at[2])
     msa_cots[h] = msa_cot_got[...]
 
+    cots = jnp.concatenate(
+        [
+            jnp.concatenate(
+                [msa_cots[kind, :, g * WIDTH : (g + 1) * WIDTH] for kind in range(2)], axis=1
+            )
+            for g in range(4)
+        ],
+        axis=0,
+    )
+    for q in range(4):
+        normed_cots = dot(
+            cots, spread_factor[q * 2 * WIDTH : (q + 1) * 2 * WIDTH, :], ((1,), (1,))
+        )
+        for g in range(4):
+            rows = pl.ds(4 * g + q, 64, stride=BLOCK)
+            value = layer_norm_pullback(
+                jnp.concatenate([normed_msa[0][rows, :], normed_msa[1][rows, :]], axis=1),
+                msa_scale[rows, :1],
+                normed_cots[g * 64 : (g + 1) * 64],
+            )
+            for part in range(2):
+                alignment[part][rows, :] = value[:, part * WIDTH : (part + 1) * WIDTH]
+    alignment_copies = [
+        pltpu.make_async_copy(
+            alignment[part],
+            alignment_gradient.at[:, pl.ds(part * WIDTH, WIDTH)],
+            alignment_sem.at[part],
+        )
+        for part in range(2)
+    ]
+    for copy in alignment_copies:
+        copy.start()
+
     @pl.when(keeps_first)
     def _():
         pair_output[...] = output_stage[0]
@@ -888,6 +932,9 @@
         def _():
             wait_for(output_got, output_sem.at[0])
             wait_for(gradient_got, gradient_sem.at[0])
+
+    for copy in alignment_copies:
+        copy.wait()
 
 
 def pair_updates(homolog, factor_weight, pair_input, cotangent, weights):
@@ -906,10 +953,10 @@
         out_shape=(
             jax.ShapeDtypeStruct((8, BLOCK, WIDTH), BF16),
             jax.ShapeDtypeStruct((8, BLOCK, WIDTH), F32),
-            jax.ShapeDtypeStruct((2, 64, BLOCK * HIDDEN), BF16),
+            jax.ShapeDtypeStruct((64 * BLOCK, 2 * WIDTH), F32),
         ),
         in_specs=[pl.BlockSpec(memory_space=pl.ANY)] * 9,
-        out_specs=(vmem, vmem, vmem),
+        out_specs=(vmem, vmem, pl.BlockSpec(memory_space=pl.ANY)),
         scratch_shapes=[
             pltpu.VMEM((64 * BLOCK, 2 * WIDTH), BF16),
             pltpu.VMEM((2 * HIDDEN, 2 * WIDTH), BF16),
@@ -918,6 +965,8 @@
             pltpu.VMEM((WIDTH, WIDTH), BF16),
             pltpu.VMEM((WIDTH, 5 * WIDTH), BF16),
             pltpu.VMEM((WIDTH, WIDTH), BF16),
+            [pltpu.VMEM((64 * BLOCK, WIDTH), F32)] * 2,
+            pltpu.VMEM((64 * BLOCK, WIDTH), F32),
             [pltpu.VMEM((64 * BLOCK, WIDTH), F32)] * 2,
             pltpu.VMEM((8 * WIDTH, 2 * WIDTH), BF16),
             shares,
@@ -964,6 +1013,7 @@
             flat,
             pltpu.VMEM((2 * WIDTH, 4 * WIDTH), BF16),
             pltpu.VMEM((4, BLOCK * HIDDEN, BLOCK * HIDDEN), BF16),
+            pltpu.VMEM((2, 64, BLOCK * HIDDEN), BF16),
             pltpu.VMEM((128, BLOCK * HIDDEN), BF16),
             shares,
             pltpu.VMEM((2, 8, BLOCK, WIDTH), BF16),
@@ -982,6 +1032,7 @@
             dma((2,)),
             dma((2,)),
             dma((7,)),
+            dma((2,)),
         ],
         compiler_params=pltpu.CompilerParams(
             collective_id=1, has_side_effects=True, vmem_limit_bytes=62 << 20
@@ -990,68 +1041,29 @@
     )(homolog, factor_weight, pair_input, cotangent, *weights)
 
 
-def finish_kernel(
-    homolog_hbm,
-    factor_weight_hbm,
-    msa_cots_hbm,
-    pair_output,
-    pair_gradient,
-    pair_output_out,
-    pair_gradient_out,
-    alignment_gradient,
-    homolog,
-    factor_weight,
-    msa_cots,
-    wide,
-    result,
-    spread_factor,
-    copy_sem,
-):
-    copies = [
-        pltpu.make_async_copy(src, dst, copy_sem.at[number])
-        for number, (src, dst) in enumerate(
-            (
-                (homolog_hbm, homolog),
-                (factor_weight_hbm, factor_weight),
-                (msa_cots_hbm, msa_cots),
-                (pair_gradient, pair_gradient_out),
-                (pair_output, pair_output_out),
+def hand_out_kernel(*refs):
+    sources, targets, held = refs[:3], refs[3:6], refs[6:9]
+    read_sem, write_sem = refs[9:]
+    reads, writes = [], []
+    for src, dst, buffer in zip(sources, targets, held):
+        parts = 4 if src.shape[0] > 8 else 1
+        rows = src.shape[0] // parts
+        for part in range(parts):
+            some = pl.ds(part * rows, rows)
+            number = len(reads)
+            reads.append(
+                pltpu.make_async_copy(src.at[some], buffer.at[some], read_sem.at[number])
             )
-        )
-    ]
-    for copy in copies:
+            writes.append(
+                pltpu.make_async_copy(buffer.at[some], dst.at[some], write_sem.at[number])
+            )
+    for copy in reads:
         copy.start()
-    copies[0].wait()
-    copies[1].wait()
-    for part in range(2):
-        wide[part][...] = homolog[:, part * WIDTH : (part + 1) * WIDTH].astype(F32)
-    repeat_factor(factor_weight, spread_factor)
-    copies[2].wait()
-    cots = jnp.concatenate(
-        [
-            jnp.concatenate(
-                [msa_cots[kind, :, g * WIDTH : (g + 1) * WIDTH] for kind in range(2)], axis=1
-            )
-            for g in range(4)
-        ],
-        axis=0,
-    )
-    for q in range(4):
-        normed_cots = dot(
-            cots, spread_factor[q * 2 * WIDTH : (q + 1) * 2 * WIDTH, :], ((1,), (1,))
-        )
-        for g in range(4):
-            rows = pl.ds(4 * g + q, 64, stride=BLOCK)
-            normed, scale = layer_norm(
-                jnp.concatenate([wide[0][rows, :], wide[1][rows, :]], axis=1)
-            )
-            value = layer_norm_pullback(normed, scale, normed_cots[g * 64 : (g + 1) * 64])
-            for part in range(2):
-                result[part][rows, :] = value[:, part * WIDTH : (part + 1) * WIDTH]
-    for part in range(2):
-        alignment_gradient[:, part * WIDTH : (part + 1) * WIDTH] = result[part][...]
-    copies[3].wait()
-    copies[4].wait()
+    for read, write in zip(reads, writes):
+        read.wait()
+        write.start()
+    for copy in writes:
+        copy.wait()
 
 
 def body(
@@ -1068,7 +1080,7 @@
     sequences, residues, depth = homolog_features.shape
     homolog = homolog_features.reshape(sequences * residues, depth)
     factor_weight = homolog_factor_matrix.T
-    pair_output, pair_gradient, cots = pair_updates(
+    results = pair_updates(
         homolog,
         factor_weight,
         pair_input,
@@ -1081,29 +1093,17 @@
             incoming_output_weight,
         ),
     )
-    vmem = pl.BlockSpec(memory_space=pltpu.VMEM)
     anywhere = pl.BlockSpec(memory_space=pl.ANY)
     pair_output, pair_gradient, alignment_gradient = pl.pallas_call(
-        finish_kernel,
-        out_shape=(
-            jax.ShapeDtypeStruct(pair_output.shape, BF16),
-            jax.ShapeDtypeStruct(pair_gradient.shape, F32),
-            jax.ShapeDtypeStruct((sequences * residues, depth), F32),
-        ),
-        in_specs=[anywhere] * 5,
-        out_specs=(anywhere, anywhere, vmem),
-        scratch_shapes=[
-            pltpu.VMEM((sequences * residues, depth), BF16),
-            pltpu.VMEM((2 * HIDDEN, depth), BF16),
-            pltpu.VMEM((2, sequences, residues * HIDDEN), BF16),
-            [pltpu.VMEM((64 * BLOCK, WIDTH), F32)] * 2,
-            [pltpu.VMEM((64 * BLOCK, WIDTH), F32)] * 2,
-            pltpu.VMEM((8 * WIDTH, 2 * WIDTH), BF16),
-            pltpu.SemaphoreType.DMA((5,)),
-        ],
+        hand_out_kernel,
+        out_shape=tuple(jax.ShapeDtypeStruct(one.shape, one.dtype) for one in results),
+        in_specs=[anywhere] * 3,
+        out_specs=(anywhere,) * 3,
+        scratch_shapes=[pltpu.VMEM(one.shape, one.dtype) for one in results]
+        + [pltpu.SemaphoreType.DMA((6,))] * 2,
         compiler_params=pltpu.CompilerParams(vmem_limit_bytes=62 << 20),
-        name="finish",
-    )(homolog, factor_weight, cots, pair_output, pair_gradient)
+        name="hand_out",
+    )(*results)
     return pair_output, pair_gradient, alignment_gradient.reshape(sequences, residues, depth)
 
 

time: 101 us -> 98.6 us (0.976)
  Pallas kernels: 99.8 us -> 97.8 us
    pallas_call x1, Pallas kernels: 5.1 us -> 2.07 us  [body(): pl.pallas_call(hand_out_kernel, out_shape=tuple((jax.ShapeDtypeStruct(one...]
where the time goes in v4:
time: 98.6 us; the launch traced here: 98.4 us
  Pallas kernels  97.8 us (99%)
    pallas_call x1, Pallas kernels, pair_updates(): pl.pallas_call(pair_kernel, out_shape=(jax.ShapeDtypeStruct((8, BLOCK, WI...  95.7 us
    pallas_call x1, Pallas kernels, body(): pl.pallas_call(hand_out_kernel, out_shape=tuple((jax.ShapeDtypeStruct(one...  2.07 us

profile of v4, /device:TPU:1, one launch (start us, length us, event | category | flops | bytes accessed | tf_op | source)
XLA Modules:
  0.0 98.4 jit_solution(13978708868458597796)
XLA Ops:
  0.6 95.7 %pair_updates.1 = (bf16[8,16,128]{2,1,0:T(8,128)(2,1)}, f32[8,16,128]{2,1,0:T(8,128)}, f32[1024,256]{1,0:T(8,128)}) custom-call(bf16[1024,256]{1,0:T(8,128)(2,1)} %bitcast.3, bf16[64,256]{1,0:T(8,128)(2,1)} %bitcast.4, bf16[8,16,128]{2,1,0:T(8,128)(2,1)} %pair_input.1, bf16[8,16,128]{2,1,0:T(8,128)(2,1)} %cotangent.1, bf16[1024,128]{1,0:T(8,128)(2,1)} %outer_weight_hbm.1, ...), custom_call_target="tpu_custom_call" | custom-call | tf_op jit(solution)/shard_map/pair_updates/pallas_call | solution.py:951
  96.3 2.1 %hand_out.1 = (bf16[8,16,128]{2,1,0:T(8,128)(2,1)}, f32[8,16,128]{2,1,0:T(8,128)}, f32[1024,256]{1,0:T(8,128)}) custom-call(bf16[8,16,128]{2,1,0:T(8,128)(2,1)} %get-tuple-element.9.refs_0_, f32[8,16,128]{2,1,0:T(8,128)} %get-tuple-element.10.refs_1_, f32[1024,256]{1,0:T(8,128)} %get-tuple-element.11.refs_2_), custom_call_target="tpu_custom_call" | custom-call | tf_op jit(solution)/shard_map/hand_out/pallas_call | solution.py:1097

commit v5 on v4

--- a/solution.py
+++ b/solution.py
@@ -14,8 +14,6 @@
 BLOCK = 16
 WIDTH = 128
 HIDDEN = 32
-ROWS_AT = 2
-ROWS_PARTS = ((), (), (0, 7), (6, 5), (4, 3), (2, 1))
 
 
 def dot(lhs, rhs, dims=((1,), (0,))):
@@ -73,13 +71,13 @@
     left_ic,
     left_ci,
     right_dj,
+    right_jd,
     pair_block,
     cot_block,
     relay_left,
     relay_right,
-    msa_left,
-    msa_right,
-    msa_rows,
+    msa_relayed,
+    msa_direct,
     o_left,
     o_right,
     o_right_stage,
@@ -94,7 +92,6 @@
     right_parts,
     left_parts2,
     right_parts2,
-    final_cot,
     wide_weight,
     table_weight,
     spread_weight,
@@ -115,8 +112,8 @@
     stacked,
     grad_table,
     msa_cots,
-    msa_cot_own,
-    msa_cot_got,
+    cot_parts,
+    cot_got,
     output_stage,
     output_got,
     gradient_stage,
@@ -125,9 +122,8 @@
     relay_send_sem,
     block_sem,
     msa_sem,
-    rows_sem,
     pair_sem,
-    final_sem,
+    cot_sem,
     small_sem,
     send_sem,
     output_sem,
@@ -208,11 +204,6 @@
             greet(line(along_columns(b, GRID - k)), core)
         return carry
 
-    def greet_across(k, carry):
-        for core in range(2):
-            greet((a, 2 * k + 1 - odd), core)
-        return carry
-
     @pl.when(jnp.logical_not(relay_stays))
     def _():
         greet((source_row, at), h)
@@ -225,7 +216,6 @@
     def _():
         greet((b, at), 1)
 
-    lax.fori_loop(0, GRID // 2, greet_across, 0)
     lax.fori_loop(1, GRID, greet_step, 0)
     greet((a, b), other)
     inputs = (
@@ -272,6 +262,7 @@
         [factors[g * 64 : (g + 1) * 64, WIDTH:] for g in range(4)], axis=1
     )
     left_ic[...] = left_value
+    right_jd[...] = right_value
     before = lax.broadcasted_iota(jnp.int32, (BLOCK * HIDDEN, BLOCK * HIDDEN), 0)
     after = lax.broadcasted_iota(jnp.int32, (BLOCK * HIDDEN, BLOCK * HIDDEN), 1)
     moved = (before == after % BLOCK * HIDDEN + after // BLOCK).astype(F32).astype(BF16)
@@ -283,10 +274,10 @@
         copy.wait()
     keeps_first = jnp.logical_and(h == 0, odd == 0)
     keeps_second = jnp.logical_and(h == 1, stays)
-    pl.semaphore_wait(barrier, 39 - relay_stays.astype(jnp.int32) - keeps_second.astype(jnp.int32))
+    pl.semaphore_wait(barrier, 31 - relay_stays.astype(jnp.int32) - keeps_second.astype(jnp.int32))
 
     for slot in range(4):
-        src, dst = ((left_ic, relay_left), (right_dj, relay_right))[slot // 2]
+        src, dst = ((left_ci, relay_left), (right_dj, relay_right))[slot // 2]
         half = pl.ds(slot % 2 * 32, 32)
 
         @pl.when(jnp.logical_not(relay_stays))
@@ -330,27 +321,6 @@
     def line_step(k):
         return line(along_columns(b, k))
 
-    def rows_send(src, core, send, steps):
-        target = msa_rows.at[b, pl.ds(pl.multiple_of(h * 64, 64), 64)]
-        sem = rows_sem.at[b, h]
-        for k in steps:
-            if k == 0:
-
-                @pl.when(h == core)
-                def _():
-                    pltpu.make_async_copy(src, target, sem).start()
-
-                @pl.when(h != core)
-                def _():
-                    remote(src, target, send, sem, (a, b), core).start()
-
-            else:
-                remote(src, target, send, sem, (a, along_columns(b, k)), core).start()
-
-    def rows_pair(steps):
-        rows_send(left_ci, 0, send_sem.at[21], steps)
-        rows_send(right_dj, 1, send_sem.at[24], steps)
-
     def msa_sent(src, dst, core, send):
         @pl.when(h == core)
         def _():
@@ -360,10 +330,8 @@
         def _():
             wait_for(dst.at[pl.ds(0, 8)], send)
 
-    msa_send(right_dj, msa_right, msa_sem.at[1], row, column_step, 0, send_sem.at[2])
-    msa_send(left_ic, msa_left, msa_sem.at[0], row, column_step, 1, send_sem.at[3])
-
-    rows_pair(ROWS_PARTS[0])
+    msa_send(right_jd, msa_direct, msa_sem.at[1], row, column_step, 0, send_sem.at[2])
+    msa_send(left_ic, msa_direct, msa_sem.at[1], row, column_step, 1, send_sem.at[3])
 
     for slot, (src, dst) in enumerate(((pair_input, pair_block), (cotangent, cot_block))):
         half = dst.at[pl.ds(h * 8, 8)]
@@ -397,41 +365,36 @@
     relay_slot = 2 * source_row + h
     for slot in range(4):
         half = slot % 2
-        src, dst = ((relay_left, msa_left), (relay_right, msa_right))[slot // 2]
+        src = (relay_left, relay_right)[slot // 2]
         wait_for(src.at[pl.ds(half * 32, 32)], relay_sem.at[slot])
         kind = slot // 2
         msa_send(
-            src, dst, msa_sem.at[kind], relay_slot, line_step, kind, send_sem.at[8 + kind], half
+            src, msa_relayed, msa_sem.at[0], relay_slot, line_step, kind, send_sem.at[8 + kind], half
         )
 
     wide_weight[...] = outer_weight[...].astype(F32)
     spread_weight[...] = jnp.zeros(spread_weight.shape, BF16)
 
     def weight_step(n, carry):
-        by_d = wide_weight[pl.ds(n, HIDDEN, stride=HIDDEN), :].astype(BF16)
         start = pl.multiple_of(n * WIDTH, WIDTH)
-        for q in range(4):
-            table_weight[pl.ds(start + q * HIDDEN, HIDDEN), :] = by_d
-
-        def spread(piece):
+
+        def lay_out(piece):
             for q in range(4):
-                spread_weight[
-                    pl.ds(start + q * HIDDEN, HIDDEN), q * WIDTH : (q + 1) * WIDTH
-                ] = piece
+                some = pl.ds(start + q * HIDDEN, HIDDEN)
+                table_weight[some, :] = piece
+                spread_weight[some, q * WIDTH : (q + 1) * WIDTH] = piece
 
         @pl.when(h == 0)
         def _():
-            spread(outer_weight[pl.ds(pl.multiple_of(n * HIDDEN, HIDDEN), HIDDEN), :])
+            lay_out(outer_weight[pl.ds(pl.multiple_of(n * HIDDEN, HIDDEN), HIDDEN), :])
 
         @pl.when(h == 1)
         def _():
-            spread(by_d)
+            lay_out(wide_weight[pl.ds(n, HIDDEN, stride=HIDDEN), :].astype(BF16))
 
         return carry
 
     lax.fori_loop(0, HIDDEN, weight_step, 0)
-
-    rows_pair(ROWS_PARTS[1])
 
     def turn_step(n, carry):
         rows = pl.ds(pl.multiple_of(n * 2 * WIDTH, 2 * WIDTH), 2 * WIDTH)
@@ -452,15 +415,15 @@
 
         def msa_wait(part, carry):
             slot = 4 * n + part
-            wait_for(msa_left.at[slot], msa_sem.at[0, slot])
-            wait_for(msa_right.at[slot], msa_sem.at[1, slot])
+            wait_for(msa_relayed.at[slot], msa_sem.at[0, slot])
+            wait_for(msa_direct.at[slot], msa_sem.at[1, slot])
             return carry
 
         lax.fori_loop(0, 4, msa_wait, 0)
         four = pl.ds(4 * n, 4)
         outer32[...] += dot(
-            msa_right[four].reshape(256, BLOCK * HIDDEN),
-            msa_left[four].reshape(256, BLOCK * HIDDEN),
+            msa_relayed[four].reshape(256, BLOCK * HIDDEN),
+            msa_direct[four].reshape(256, BLOCK * HIDDEN),
             ((0,), (0,)),
         )
         return carry
@@ -493,11 +456,24 @@
     for part in range(2):
         wait_for(pair_block.at[pl.ds(part * 8, 8)], block_sem.at[0, part])
         wait_for(cot_block.at[pl.ds(part * 8, 8)], block_sem.at[1, part])
-    for i in range(BLOCK):
-        start = ((i % 4) * 4 + i // 4) * BLOCK
+    for r in range(BLOCK):
+        start = ((r % 4) * 4 + r // 4) * BLOCK
+        flat[pl.ds(r * BLOCK, BLOCK), :] = projected[start : start + BLOCK]
+
+    def add_rows(i, value):
         first[pl.ds(i * BLOCK, BLOCK), :] = (
-            (pair_block[i].astype(F32) + projected[start : start + BLOCK]).astype(BF16).astype(F32)
-        )
+            (pair_block[i].astype(F32) + value).astype(BF16).astype(F32)
+        )
+
+    @pl.when(h == 0)
+    def _():
+        for i in range(BLOCK):
+            add_rows(i, flat[pl.ds(i, BLOCK, stride=BLOCK), :])
+
+    @pl.when(h == 1)
+    def _():
+        for i in range(BLOCK):
+            add_rows(i, flat[pl.ds(i * BLOCK, BLOCK), :])
 
     def send_same(dst, sems, chips, steps, send):
         own = steps(0)
@@ -535,12 +511,7 @@
     def no_totals():
         return tuple(jnp.zeros((BLOCK, WIDTH), F32) for _ in range(BLOCK))
 
-    def send_rows_at(k, rows):
-        @pl.when(k == ROWS_AT)
-        def _():
-            rows_pair(rows)
-
-    def contract(left, left_sem, left_own, by_column, right, right_sem, right_own, steps, rows):
+    def contract(left, left_sem, left_own, by_column, right, right_sem, right_own, steps):
         def arrive(ref, sems, slot, skip):
             if skip is None:
                 wait_for(ref.at[slot], sems.at[slot])
@@ -552,7 +523,6 @@
 
         def block_step(k, totals):
             slot = steps(k)
-            send_rows_at(k, rows)
             arrive(left, left_sem, slot, left_own)
             arrive(right, right_sem, slot, right_own)
             wide[...] = left[slot].astype(F32)
@@ -565,11 +535,9 @@
         for p in range(BLOCK):
             part[n, p] = totals[p].astype(BF16)
 
-    def sum_of(parts, sems, skip, steps, rows=None):
+    def sum_of(parts, sems, skip, steps):
         def step(k, total):
             slot = steps(k)
-            if rows is not None:
-                send_rows_at(k, rows)
             if skip is None:
                 wait_for(parts.at[slot], sems.at[slot])
             else:
@@ -638,7 +606,6 @@
         pair_sem.at[1],
         None,
         step_j,
-        ROWS_PARTS[2],
     )
     mixing_normed, mixing_scale = layer_norm(mixing)
     update = dot(mixing_normed.astype(BF16), out_out_weight[...])
@@ -672,7 +639,6 @@
         pair_sem.at[4],
         own_i,
         step_i,
-        ROWS_PARTS[3],
     )
 
     def input_pullback(kept, left_cot, right_cot, gating_part, weight, upstream):
@@ -734,9 +700,7 @@
     def _():
         hand_over(result, output_stage, output_got, small_sem.at[0], output_sem)
 
-    left_cot = sum_of(
-        ib_left, pair_sem.at[2], None, step_j, ROWS_PARTS[4]
-    )
+    left_cot = sum_of(ib_left, pair_sem.at[2], None, step_j)
     right_cot = sum_of(ib_right, pair_sem.at[3], own_i, step_i)
     second_cot = input_pullback(
         in_kept, left_cot, right_cot, gating_part, in_in_turned, upstream32[...]
@@ -774,9 +738,7 @@
     gating = out_kept[6]
     gating_cot = second_cot * out_kept[9] * gating * (1.0 - gating)
     gating_part = dot(gating_cot.astype(BF16), out_in_turned[4 * WIDTH :, :])
-    flat[...] = sum_of(
-        ob_left, pair_sem.at[6], own_j, step_j, ROWS_PARTS[5]
-    )
+    flat[...] = sum_of(ob_left, pair_sem.at[6], own_j, step_j)
     left_cot = jnp.concatenate(
         [flat[pl.ds(j, BLOCK, stride=BLOCK), :] for j in range(BLOCK)], axis=0
     )
@@ -788,76 +750,73 @@
     @pl.when(h == 0)
     def _():
         hand_over(gradient, gradient_stage, gradient_got, small_sem.at[1], gradient_sem)
-        flat[...] = gradient
-        for j in range(BLOCK):
-            final_cot[at, j] = flat[pl.ds(j, BLOCK, stride=BLOCK), :].astype(BF16)
+
+    def stack(r, value):
+        g, q = r // 4, r % 4
+        stacked[g * BLOCK : (g + 1) * BLOCK, q * WIDTH : (q + 1) * WIDTH] = value.astype(BF16)
+
+    flat[...] = gradient
+
+    @pl.when(h == 0)
+    def _():
+        for r in range(BLOCK):
+            stack(r, flat[pl.ds(r, BLOCK, stride=BLOCK), :])
 
     @pl.when(h == 1)
     def _():
-        final_cot[at] = blocked(gradient)
-
-    def final_chip(n):
-        return chip_at(n, b)
-
-    def final_step(k):
-        return along_rows(at, k)
-
-    send_same(final_cot, final_sem, final_chip, final_step, send_sem.at[26])
-
-    def final_half(part, total):
-        def stack_step(k, carry):
-            slot = final_step(4 * part + k)
-
-            @pl.when(slot != at)
-            def _():
-                wait_for(final_cot.at[slot], final_sem.at[slot])
-
+        for r in range(BLOCK):
+            stack(r, flat[pl.ds(r * BLOCK, BLOCK), :])
+
+    for x8 in range(HIDDEN // 8):
+        chunk = dot(
+            stacked[...], turned_weight[:, x8 * 8 * WIDTH : (x8 + 1) * 8 * WIDTH]
+        ).astype(BF16)
+        for piece in range(8):
+            start = (8 * x8 + piece) * BLOCK
             for g in range(4):
-                rows = pl.ds(pl.multiple_of(g * 64 + k * BLOCK, BLOCK), BLOCK)
-                for q in range(4):
-                    stacked[rows, q * WIDTH : (q + 1) * WIDTH] = final_cot[slot, 4 * g + q]
-            return carry
-
-        lax.fori_loop(0, 4, stack_step, 0)
-
-        def table_step(x8, carry):
-            begin = pl.multiple_of(x8 * 8 * WIDTH, 8 * WIDTH)
-            chunk = dot(stacked[...], turned_weight[:, pl.ds(begin, 8 * WIDTH)]).astype(BF16)
-            for piece in range(8):
-                start = pl.multiple_of((8 * x8 + piece) * BLOCK, BLOCK)
-                for g in range(4):
-                    for k in range(4):
-                        row = g * 64 + k * BLOCK
-                        grad_table[k, pl.ds(start, BLOCK), g * WIDTH : (g + 1) * WIDTH] = chunk[
-                            row : row + BLOCK, piece * WIDTH : (piece + 1) * WIDTH
-                        ]
-            return carry
-
-        lax.fori_loop(0, HIDDEN // 8, table_step, 0)
-        sequences = []
-        for k in range(4):
-            slot = final_step(4 * part + k)
-            for piece in range(2):
-                wait_for(msa_rows.at[slot, pl.ds(piece * 64, 64)], rows_sem.at[slot, piece])
-            sequences.append(msa_rows[slot])
-        return total + dot(
-            jnp.concatenate(sequences, axis=1),
-            grad_table[...].reshape(4 * BLOCK * HIDDEN, BLOCK * HIDDEN),
-        )
-
-    total = lax.fori_loop(0, 2, final_half, jnp.zeros((128, BLOCK * HIDDEN), F32))
-    msa_cot_own[...] = (total * (1.0 / SEQUENCES)).astype(BF16)
-    remote(
-        msa_cot_own.at[pl.ds(pl.multiple_of(other * 64, 64), 64)],
-        msa_cot_got,
-        send_sem.at[27],
-        small_sem.at[2],
-        (a, b),
-        other,
-    ).start()
-    msa_cots[other] = msa_cot_own[pl.ds(pl.multiple_of(h * 64, 64), 64), :]
-    wait_for(msa_cot_got, small_sem.at[2])
-    msa_cots[h] = msa_cot_got[...]
+                grad_table[start : start + BLOCK, g * WIDTH : (g + 1) * WIDTH] = chunk[
+                    g * BLOCK : (g + 1) * BLOCK, piece * WIDTH : (piece + 1) * WIDTH
+                ]
+
+    def cot_step(step, carry):
+        chips = [along_rows(a, GRID - 1 - 2 * step - n) for n in range(2)]
+        sequences = jnp.concatenate(
+            [
+                msa_relayed[pl.ds(2 * chip, 2)].reshape(2 * 64, BLOCK * HIDDEN)
+                for chip in chips
+            ],
+            axis=0,
+        )
+        sums = dot(sequences, grad_table[...]).astype(BF16)
+        for n, chip in enumerate(chips):
+            for core in range(2):
+                start = (2 * n + core) * 64
+                slot = 2 * chip + core
+                cot_parts[slot] = sums[start : start + 64]
+                target = cot_got.at[h, a]
+
+                @pl.when(slot == row)
+                def _():
+                    pltpu.make_async_copy(cot_parts.at[slot], target, cot_sem.at[h, a]).start()
+
+                @pl.when(slot != row)
+                def _():
+                    remote(
+                        cot_parts.at[slot], target, send_sem.at[26], cot_sem.at[h, a], (chip, b), core
+                    ).start()
+
+        return carry
+
+    lax.fori_loop(0, 4, cot_step, 0)
+    for core in range(2):
+
+        def cot_sum(k, total, core=core):
+            n = along_rows(a, k)
+            wait_for(cot_got.at[core, n], cot_sem.at[core, n])
+            return total + cot_got[core, n].astype(F32)
+
+        total = lax.fori_loop(0, GRID, cot_sum, jnp.zeros((64, BLOCK * HIDDEN), F32))
+        msa_cots[1 - core] = (total * (1.0 / SEQUENCES)).astype(BF16)
 
     cots = jnp.concatenate(
         [
@@ -909,19 +868,17 @@
         for slot in range(4):
             wait_for(relay_left.at[pl.ds(0, 32)], relay_send_sem.at[slot])
 
-    msa_sent(right_dj, msa_right, 0, send_sem.at[2])
-    msa_sent(left_ic, msa_left, 1, send_sem.at[3])
+    msa_sent(right_jd, msa_direct, 0, send_sem.at[2])
+    msa_sent(left_ic, msa_direct, 1, send_sem.at[3])
     block_sent(0, pair_input)
     block_sent(1, cotangent)
-    msa_sent(relay_left, msa_left, 0, send_sem.at[8])
-    msa_sent(relay_right, msa_right, 1, send_sem.at[9])
-    for number in (10, 13, 14, 16, 26):
+    msa_sent(relay_left, msa_relayed, 0, send_sem.at[8])
+    msa_sent(relay_right, msa_relayed, 1, send_sem.at[9])
+    for number in (10, 13, 14, 16):
         wait_for(o_left.at[pl.ds(0, 7)], send_sem.at[number])
     for number in (11, 12, 15, 17):
         wait_for(o_left, send_sem.at[number])
-    msa_sent(left_ci, msa_left, 0, send_sem.at[21])
-    msa_sent(right_dj, msa_left, 1, send_sem.at[24])
-    wait_for(msa_cot_got, send_sem.at[27])
+    wait_for(cot_parts.at[pl.ds(0, 15)], send_sem.at[26])
 
     @pl.when(h == 0)
     def _():
@@ -972,20 +929,19 @@
             shares,
             shares,
             shares,
+            shares,
             block,
             block,
             shares,
             shares,
             all_sequences,
             all_sequences,
-            pltpu.VMEM((GRID, 128, BLOCK * HIDDEN), BF16),
             gathered,
             gathered,
             block,
             gathered,
             gathered,
             block,
-            gathered,
             gathered,
             gathered,
             gathered,
@@ -1011,11 +967,11 @@
             pltpu.VMEM((9, BLOCK * BLOCK, WIDTH), F32),
             flat,
             flat,
-            pltpu.VMEM((2 * WIDTH, 4 * WIDTH), BF16),
-            pltpu.VMEM((4, BLOCK * HIDDEN, BLOCK * HIDDEN), BF16),
+            pltpu.VMEM((64, 4 * WIDTH), BF16),
+            pltpu.VMEM((BLOCK * HIDDEN, BLOCK * HIDDEN), BF16),
             pltpu.VMEM((2, 64, BLOCK * HIDDEN), BF16),
-            pltpu.VMEM((128, BLOCK * HIDDEN), BF16),
-            shares,
+            all_sequences,
+            pltpu.VMEM((2, GRID, 64, BLOCK * HIDDEN), BF16),
             pltpu.VMEM((2, 8, BLOCK, WIDTH), BF16),
             half_block,
             pltpu.VMEM((2, 8, BLOCK, WIDTH), F32),
@@ -1024,10 +980,9 @@
             dma((4,)),
             dma((2, 2)),
             dma((2, 2 * GRID)),
-            dma((GRID, 2)),
             dma((8, GRID)),
-            dma((GRID,)),
-            dma((3,)),
+            dma((2, GRID)),
+            dma((2,)),
             dma((28,)),
             dma((2,)),
             dma((2,)),

time: 98.6 us -> 94.3 us (0.956)
  Pallas kernels: 97.8 us -> 93.5 us
    pallas_call x1, Pallas kernels: 95.7 us -> 91.4 us  [pair_updates(): pl.pallas_call(pair_kernel, out_shape=(jax.ShapeDtypeStruct((8, BLOCK, WI...]
where the time goes in v5:
time: 94.3 us; the launch traced here: 94.1 us
  Pallas kernels  93.5 us (99%)
    pallas_call x1, Pallas kernels, pair_updates(): pl.pallas_call(pair_kernel, out_shape=(jax.ShapeDtypeStruct((8, BLOCK, WI...  91.4 us
    pallas_call x1, Pallas kernels, body(): pl.pallas_call(hand_out_kernel, out_shape=tuple((jax.ShapeDtypeStruct(one...  2.07 us

profile of v5, /device:TPU:1, one launch (start us, length us, event | category | flops | bytes accessed | tf_op | source)
XLA Modules:
  0.0 94.1 jit_solution(2755618438019247011)
XLA Ops:
  0.6 91.4 %pair_updates.1 = (bf16[8,16,128]{2,1,0:T(8,128)(2,1)}, f32[8,16,128]{2,1,0:T(8,128)}, f32[1024,256]{1,0:T(8,128)}) custom-call(bf16[1024,256]{1,0:T(8,128)(2,1)} %bitcast.3, bf16[64,256]{1,0:T(8,128)(2,1)} %bitcast.4, bf16[8,16,128]{2,1,0:T(8,128)(2,1)} %pair_input.1, bf16[8,16,128]{2,1,0:T(8,128)(2,1)} %cotangent.1, bf16[1024,128]{1,0:T(8,128)(2,1)} %outer_weight_hbm.1, ...), custom_call_target="tpu_custom_call" | custom-call | tf_op jit(solution)/shard_map/pair_updates/pallas_call | solution.py:908
  92.1 2.1 %hand_out.1 = (bf16[8,16,128]{2,1,0:T(8,128)(2,1)}, f32[8,16,128]{2,1,0:T(8,128)}, f32[1024,256]{1,0:T(8,128)}) custom-call(bf16[8,16,128]{2,1,0:T(8,128)(2,1)} %get-tuple-element.9.refs_0_, f32[8,16,128]{2,1,0:T(8,128)} %get-tuple-element.10.refs_1_, f32[1024,256]{1,0:T(8,128)} %get-tuple-element.11.refs_2_), custom_call_target="tpu_custom_call" | custom-call | tf_op jit(solution)/shard_map/hand_out/pallas_call | solution.py:1052

commit v6 on v5

--- a/solution.py
+++ b/solution.py
@@ -56,7 +56,8 @@
     in_out_weight_hbm,
     pair_output,
     pair_gradient,
-    alignment_gradient,
+    alignment_first,
+    alignment_second,
     homolog,
     factor_weight,
     outer_weight,
@@ -66,7 +67,6 @@
     in_out_weight,
     normed_msa,
     msa_scale,
-    alignment,
     spread_factor,
     left_ic,
     left_ci,
@@ -129,7 +129,6 @@
     output_sem,
     gradient_sem,
     input_sem,
-    alignment_sem,
 ):
     row, col = lax.axis_index("row"), lax.axis_index("col")
     a, h, b = row // 2, row % 2, col
@@ -446,7 +445,7 @@
                     axis=0,
                 )
             )
-        picked = (jnp.concatenate(columns, axis=1) * (1.0 / SEQUENCES)).astype(BF16)
+        picked = jnp.concatenate(columns, axis=1).astype(BF16)
         weight = table_weight[pl.ds(pl.multiple_of(d8 * 8 * WIDTH, 8 * WIDTH), 8 * WIDTH), :]
         return total + dot(picked, weight)
 
@@ -458,7 +457,7 @@
         wait_for(cot_block.at[pl.ds(part * 8, 8)], block_sem.at[1, part])
     for r in range(BLOCK):
         start = ((r % 4) * 4 + r // 4) * BLOCK
-        flat[pl.ds(r * BLOCK, BLOCK), :] = projected[start : start + BLOCK]
+        flat[pl.ds(r * BLOCK, BLOCK), :] = projected[start : start + BLOCK] * (1.0 / SEQUENCES)
 
     def add_rows(i, value):
         first[pl.ds(i * BLOCK, BLOCK), :] = (
@@ -478,35 +477,31 @@
     def send_same(dst, sems, chips, steps, send):
         own = steps(0)
 
-        def step(k, carry):
+        def step(k):
             chip = chips(steps(GRID - k))
             remote(dst.at[own], dst.at[own], send, sems.at[own], chip, h).start()
-            return carry
-
-        lax.fori_loop(1, GRID, step, 0)
+
+        for k in range(1, GRID):
+            step(k)
 
     def send_other(src, dst, sems, chips, steps, send):
         own = steps(0)
 
-        def step(k, carry):
+        def step(k):
             chip = chips(steps(GRID - 1 - k))
             remote(src, dst.at[own], send, sems.at[own], chip, other).start()
-            return carry
-
-        lax.fori_loop(0, GRID, step, 0)
+
+        for k in range(GRID):
+            step(k)
 
     def block_product(totals, left, by_column, right):
-        def inner(group, totals):
-            totals = list(totals)
-            for u in range(4):
-                t = group * 4 + u
-                across = right(t)
-                for p in range(BLOCK):
-                    one = left[t, pl.ds(p, 1), :] if by_column else left[p, pl.ds(t, 1), :]
-                    totals[p] = totals[p] + one * across
-            return tuple(totals)
-
-        return lax.fori_loop(0, BLOCK // 4, inner, totals)
+        totals = list(totals)
+        for t in range(BLOCK):
+            across = right(t)
+            for p in range(BLOCK):
+                one = left[t, pl.ds(p, 1), :] if by_column else left[p, pl.ds(t, 1), :]
+                totals[p] = totals[p] + one * across
+        return tuple(totals)
 
     def no_totals():
         return tuple(jnp.zeros((BLOCK, WIDTH), F32) for _ in range(BLOCK))
@@ -838,19 +833,8 @@
                 msa_scale[rows, :1],
                 normed_cots[g * 64 : (g + 1) * 64],
             )
-            for part in range(2):
-                alignment[part][rows, :] = value[:, part * WIDTH : (part + 1) * WIDTH]
-    alignment_copies = [
-        pltpu.make_async_copy(
-            alignment[part],
-            alignment_gradient.at[:, pl.ds(part * WIDTH, WIDTH)],
-            alignment_sem.at[part],
-        )
-        for part in range(2)
-    ]
-    for copy in alignment_copies:
-        copy.start()
-
+            alignment_first[rows, :] = value[:, :WIDTH]
+            alignment_second[rows, :] = value[:, WIDTH:]
     @pl.when(keeps_first)
     def _():
         pair_output[...] = output_stage[0]
@@ -890,9 +874,6 @@
             wait_for(output_got, output_sem.at[0])
             wait_for(gradient_got, gradient_sem.at[0])
 
-    for copy in alignment_copies:
-        copy.wait()
-
 
 def pair_updates(homolog, factor_weight, pair_input, cotangent, weights):
     gathered = pltpu.VMEM((GRID, BLOCK, BLOCK, WIDTH), BF16)
@@ -903,17 +884,14 @@
     half_block = pltpu.VMEM((8, BLOCK, WIDTH), BF16)
     wide_block = pltpu.VMEM((BLOCK, BLOCK, WIDTH), F32)
     half_wide = pltpu.VMEM((8, BLOCK, WIDTH), F32)
+    whole_side = pltpu.VMEM((64 * BLOCK, WIDTH), F32)
     dma = pltpu.SemaphoreType.DMA
     vmem = pl.BlockSpec(memory_space=pltpu.VMEM)
     return pl.pallas_call(
         pair_kernel,
-        out_shape=(
-            jax.ShapeDtypeStruct((8, BLOCK, WIDTH), BF16),
-            jax.ShapeDtypeStruct((8, BLOCK, WIDTH), F32),
-            jax.ShapeDtypeStruct((64 * BLOCK, 2 * WIDTH), F32),
-        ),
+        out_shape=(half_block, half_wide, whole_side, whole_side),
         in_specs=[pl.BlockSpec(memory_space=pl.ANY)] * 9,
-        out_specs=(vmem, vmem, pl.BlockSpec(memory_space=pl.ANY)),
+        out_specs=(vmem,) * 4,
         scratch_shapes=[
             pltpu.VMEM((64 * BLOCK, 2 * WIDTH), BF16),
             pltpu.VMEM((2 * HIDDEN, 2 * WIDTH), BF16),
@@ -924,7 +902,6 @@
             pltpu.VMEM((WIDTH, WIDTH), BF16),
             [pltpu.VMEM((64 * BLOCK, WIDTH), F32)] * 2,
             pltpu.VMEM((64 * BLOCK, WIDTH), F32),
-            [pltpu.VMEM((64 * BLOCK, WIDTH), F32)] * 2,
             pltpu.VMEM((8 * WIDTH, 2 * WIDTH), BF16),
             shares,
             shares,
@@ -987,37 +964,38 @@
             dma((2,)),
             dma((2,)),
             dma((7,)),
-            dma((2,)),
         ],
         compiler_params=pltpu.CompilerParams(
-            collective_id=1, has_side_effects=True, vmem_limit_bytes=62 << 20
+            collective_id=1, has_side_effects=True, vmem_limit_bytes=60 << 20
         ),
         name="pair_updates",
     )(homolog, factor_weight, pair_input, cotangent, *weights)
 
 
-def hand_out_kernel(*refs):
-    sources, targets, held = refs[:3], refs[3:6], refs[6:9]
-    read_sem, write_sem = refs[9:]
-    reads, writes = [], []
-    for src, dst, buffer in zip(sources, targets, held):
-        parts = 4 if src.shape[0] > 8 else 1
-        rows = src.shape[0] // parts
-        for part in range(parts):
-            some = pl.ds(part * rows, rows)
-            number = len(reads)
-            reads.append(
-                pltpu.make_async_copy(src.at[some], buffer.at[some], read_sem.at[number])
-            )
-            writes.append(
-                pltpu.make_async_copy(buffer.at[some], dst.at[some], write_sem.at[number])
-            )
-    for copy in reads:
+def hand_out_kernel(
+    pair_output,
+    pair_gradient,
+    alignment_first,
+    alignment_second,
+    pair_output_out,
+    pair_gradient_out,
+    alignment_gradient,
+    copy_sem,
+):
+    rows = alignment_first.shape[0] // 4
+    pairs = [(pair_output, pair_output_out), (pair_gradient, pair_gradient_out)]
+    for part in range(4):
+        some = pl.ds(part * rows, rows)
+        for side, held in enumerate((alignment_first, alignment_second)):
+            target = alignment_gradient.at[some, pl.ds(side * WIDTH, WIDTH)]
+            pairs.append((held.at[some], target))
+    copies = [
+        pltpu.make_async_copy(src, dst, copy_sem.at[number])
+        for number, (src, dst) in enumerate(pairs)
+    ]
+    for copy in copies:
         copy.start()
-    for read, write in zip(reads, writes):
-        read.wait()
-        write.start()
-    for copy in writes:
+    for copy in copies:
         copy.wait()
 
 
@@ -1051,12 +1029,15 @@
     anywhere = pl.BlockSpec(memory_space=pl.ANY)
     pair_output, pair_gradient, alignment_gradient = pl.pallas_call(
         hand_out_kernel,
-        out_shape=tuple(jax.ShapeDtypeStruct(one.shape, one.dtype) for one in results),
-        in_specs=[anywhere] * 3,
+        out_shape=(
+            jax.ShapeDtypeStruct(pair_input.shape, BF16),
+            jax.ShapeDtypeStruct(pair_input.shape, F32),
+            jax.ShapeDtypeStruct(homolog.shape, F32),
+        ),
+        in_specs=[pl.BlockSpec(memory_space=pltpu.VMEM)] * 4,
         out_specs=(anywhere,) * 3,
-        scratch_shapes=[pltpu.VMEM(one.shape, one.dtype) for one in results]
-        + [pltpu.SemaphoreType.DMA((6,))] * 2,
-        compiler_params=pltpu.CompilerParams(vmem_limit_bytes=62 << 20),
+        scratch_shapes=[pltpu.SemaphoreType.DMA((10,))],
+        compiler_params=pltpu.CompilerParams(vmem_limit_bytes=16 << 20),
         name="hand_out",
     )(*results)
     return pair_output, pair_gradient, alignment_gradient.reshape(sequences, residues, depth)

time: 94.3 us -> 90.8 us (0.963)
  Pallas kernels: 93.5 us -> 90 us
    pallas_call x2, Pallas kernels: 93.5 us -> 90 us  [the longest x1 88.9 us: pair_updates(): pl.pallas_call(pair_kernel, out_shape=(half_block, half_wide, whole_side,...]
where the time goes in v6:
time: 90.8 us; the launch traced here: 90.6 us
  Pallas kernels  90 us (99%)
    pallas_call x1, Pallas kernels, pair_updates(): pl.pallas_call(pair_kernel, out_shape=(half_block, half_wide, whole_side,...  88.9 us

profile of v6, /device:TPU:1, one launch (start us, length us, event | category | flops | bytes accessed | tf_op | source)
XLA Modules:
  0.0 90.6 jit_solution(9712418467322977952)
XLA Ops:
  0.6 88.9 %pair_updates.1 = (bf16[8,16,128]{2,1,0:T(8,128)(2,1)S(1)}, f32[8,16,128]{2,1,0:T(8,128)S(1)}, f32[1024,128]{1,0:T(8,128)S(1)}, f32[1024,128]{1,0:T(8,128)S(1)}) custom-call(bf16[1024,256]{1,0:T(8,128)(2,1)} %bitcast.3, bf16[64,256]{1,0:T(8,128)(2,1)} %bitcast.4, bf16[8,16,128]{2,1,0:T(8,128)(2,1)} %pair_input.1, bf16[8,16,128]{2,1,0:T(8,128)(2,1)} %cotangent.1, ...), custom_call_target="tpu_custom_call" | custom-call | tf_op jit(solution)/shard_map/pair_updates/pallas_call | solution.py:890
  89.5 1.1 %hand_out.1 = (bf16[8,16,128]{2,1,0:T(8,128)(2,1)}, f32[8,16,128]{2,1,0:T(8,128)}, f32[1024,256]{1,0:T(8,128)}) custom-call(bf16[8,16,128]{2,1,0:T(8,128)(2,1)S(1)} %get-tuple-element.10.pair_output, f32[8,16,128]{2,1,0:T(8,128)S(1)} %get-tuple-element.11.pair_gradient, f32[1024,128]{1,0:T(8,128)S(1)} %get-tuple-element.12.alignment_first, ...), custom_call_target="tpu_custom_call" | custom-call | tf_op jit(solution)/shard_map/hand_out/pallas_call | solution.py:1030

commit v7 on v6

--- a/solution.py
+++ b/solution.py
@@ -102,6 +102,7 @@
     in_out_turned,
     outer32,
     wide,
+    wide_too,
     cot_wide,
     cot_turned,
     flat,
@@ -190,33 +191,6 @@
     def wait_for(ref, sem):
         pltpu.make_async_copy(ref, ref, sem).wait()
 
-    barrier = pltpu.get_barrier_semaphore()
-
-    def greet(chip, core):
-        pl.semaphore_signal(
-            barrier, inc=1, device_id=(2 * chip[0] + core, chip[1]), device_id_type=MESH
-        )
-
-    def greet_step(k, carry):
-        for core in range(2):
-            greet(column(along_rows(a, GRID - k)), core)
-            greet(line(along_columns(b, GRID - k)), core)
-        return carry
-
-    @pl.when(jnp.logical_not(relay_stays))
-    def _():
-        greet((source_row, at), h)
-
-    @pl.when(h == 1)
-    def _():
-        greet((b, at), 0)
-
-    @pl.when(jnp.logical_and(h == 1, jnp.logical_not(stays)))
-    def _():
-        greet((b, at), 1)
-
-    lax.fori_loop(1, GRID, greet_step, 0)
-    greet((a, b), other)
     inputs = (
         (homolog_hbm, homolog),
         (factor_weight_hbm, factor_weight),
@@ -232,6 +206,34 @@
     ]
     for copy in copies:
         copy.start()
+
+    barrier = pltpu.get_barrier_semaphore()
+
+    def greet(chip, core):
+        pl.semaphore_signal(
+            barrier, inc=1, device_id=(2 * chip[0] + core, chip[1]), device_id_type=MESH
+        )
+
+    def greet_step(k, carry):
+        for core in range(2):
+            greet(column(along_rows(a, GRID - k)), core)
+            greet(line(along_columns(b, GRID - k)), core)
+        return carry
+
+    @pl.when(jnp.logical_not(relay_stays))
+    def _():
+        greet((source_row, at), h)
+
+    @pl.when(h == 1)
+    def _():
+        greet((b, at), 0)
+
+    @pl.when(jnp.logical_and(h == 1, jnp.logical_not(stays)))
+    def _():
+        greet((b, at), 1)
+
+    lax.fori_loop(1, GRID, greet_step, 0)
+    greet((a, b), other)
     copies[0].wait()
     copies[1].wait()
 
@@ -659,8 +661,8 @@
         send_part(
             left_parts, n, ib_left, own_j, pair_sem.at[2], row_chip, other, send_sem.at[12]
         )
-        wide[...] = i_left[n].astype(F32)
-        totals = block_product(no_totals(), wide, False, lambda t: cot_wide[t])
+        wide_too[...] = i_left[n].astype(F32)
+        totals = block_product(no_totals(), wide_too, False, lambda t: cot_wide[t])
 
         @pl.when(n != own_i)
         def _():
@@ -773,7 +775,7 @@
                     g * BLOCK : (g + 1) * BLOCK, piece * WIDTH : (piece + 1) * WIDTH
                 ]
 
-    def cot_step(step, carry):
+    def cot_step(step):
         chips = [along_rows(a, GRID - 1 - 2 * step - n) for n in range(2)]
         sequences = jnp.concatenate(
             [
@@ -800,9 +802,8 @@
                         cot_parts.at[slot], target, send_sem.at[26], cot_sem.at[h, a], (chip, b), core
                     ).start()
 
-        return carry
-
-    lax.fori_loop(0, 4, cot_step, 0)
+    for step in range(4):
+        cot_step(step)
     for core in range(2):
 
         def cot_sum(k, total, core=core):
@@ -939,6 +940,7 @@
             wide_block,
             wide_block,
             wide_block,
+            wide_block,
             flat,
             pltpu.VMEM((10, BLOCK * BLOCK, WIDTH), F32),
             pltpu.VMEM((9, BLOCK * BLOCK, WIDTH), F32),

time: 90.8 us -> 90 us (level)
  no operation moved by 1% of the time
where the time goes in v7:
time: 90 us; the launch traced here: 89.9 us
  Pallas kernels  89.2 us (99%)
    pallas_call x1, Pallas kernels, pair_updates(): pl.pallas_call(pair_kernel, out_shape=(half_block, half_wide, whole_side,...  88.2 us

profile of v7, /device:TPU:1, one launch (start us, length us, event | category | flops | bytes accessed | tf_op | source)
XLA Modules:
  0.0 89.9 jit_solution(1778220869554200985)
XLA Ops:
  0.6 88.2 %pair_updates.1 = (bf16[8,16,128]{2,1,0:T(8,128)(2,1)S(1)}, f32[8,16,128]{2,1,0:T(8,128)S(1)}, f32[1024,128]{1,0:T(8,128)S(1)}, f32[1024,128]{1,0:T(8,128)S(1)}) custom-call(bf16[1024,256]{1,0:T(8,128)(2,1)} %bitcast.3, bf16[64,256]{1,0:T(8,128)(2,1)} %bitcast.4, bf16[8,16,128]{2,1,0:T(8,128)(2,1)} %pair_input.1, bf16[8,16,128]{2,1,0:T(8,128)(2,1)} %cotangent.1, ...), custom_call_target="tpu_custom_call" | custom-call | tf_op jit(solution)/shard_map/pair_updates/pallas_call | solution.py:891
  88.8 1.1 %hand_out.1 = (bf16[8,16,128]{2,1,0:T(8,128)(2,1)}, f32[8,16,128]{2,1,0:T(8,128)}, f32[1024,256]{1,0:T(8,128)}) custom-call(bf16[8,16,128]{2,1,0:T(8,128)(2,1)S(1)} %get-tuple-element.10.pair_output, f32[8,16,128]{2,1,0:T(8,128)S(1)} %get-tuple-element.11.pair_gradient, f32[1024,128]{1,0:T(8,128)S(1)} %get-tuple-element.12.alignment_first, ...), custom_call_target="tpu_custom_call" | custom-call | tf_op jit(solution)/shard_map/hand_out/pallas_call | solution.py:1032

commit v8 on v7

--- a/solution.py
+++ b/solution.py
@@ -373,7 +373,7 @@
             src, msa_relayed, msa_sem.at[0], relay_slot, line_step, kind, send_sem.at[8 + kind], half
         )
 
-    wide_weight[...] = outer_weight[...].astype(F32)
+    wide_weight[: HIDDEN * HIDDEN, :] = outer_weight[...].astype(F32)
     spread_weight[...] = jnp.zeros(spread_weight.shape, BF16)
 
     def weight_step(n, carry):
@@ -928,7 +928,7 @@
             gathered,
             gathered,
             gathered,
-            pltpu.VMEM((HIDDEN * HIDDEN, WIDTH), F32),
+            pltpu.VMEM((HIDDEN * (HIDDEN + 1), WIDTH), F32),
             pltpu.VMEM((HIDDEN * WIDTH, WIDTH), BF16),
             pltpu.VMEM((HIDDEN * WIDTH, 4 * WIDTH), BF16),
             pltpu.VMEM((4 * WIDTH, HIDDEN * WIDTH), BF16),

time: 90 us -> 90 us (level)
  no operation moved by 1% of the time
where the time goes in v8:
time: 90 us; the launch traced here: 89.9 us
  Pallas kernels  89.2 us (99%)
    pallas_call x1, Pallas kernels, pair_updates(): pl.pallas_call(pair_kernel, out_shape=(half_block, half_wide, whole_side,...  88.2 us

profile of v8, /device:TPU:1, one launch (start us, length us, event | category | flops | bytes accessed | tf_op | source)
XLA Modules:
  0.0 89.9 jit_solution(7604683249291388393)
XLA Ops:
  0.6 88.2 %pair_updates.1 = (bf16[8,16,128]{2,1,0:T(8,128)(2,1)S(1)}, f32[8,16,128]{2,1,0:T(8,128)S(1)}, f32[1024,128]{1,0:T(8,128)S(1)}, f32[1024,128]{1,0:T(8,128)S(1)}) custom-call(bf16[1024,256]{1,0:T(8,128)(2,1)} %bitcast.3, bf16[64,256]{1,0:T(8,128)(2,1)} %bitcast.4, bf16[8,16,128]{2,1,0:T(8,128)(2,1)} %pair_input.1, bf16[8,16,128]{2,1,0:T(8,128)(2,1)} %cotangent.1, ...), custom_call_target="tpu_custom_call" | custom-call | tf_op jit(solution)/shard_map/pair_updates/pallas_call | solution.py:891
  88.8 1.1 %hand_out.1 = (bf16[8,16,128]{2,1,0:T(8,128)(2,1)}, f32[8,16,128]{2,1,0:T(8,128)}, f32[1024,256]{1,0:T(8,128)}) custom-call(bf16[8,16,128]{2,1,0:T(8,128)(2,1)S(1)} %get-tuple-element.10.pair_output, f32[8,16,128]{2,1,0:T(8,128)S(1)} %get-tuple-element.11.pair_gradient, f32[1024,128]{1,0:T(8,128)S(1)} %get-tuple-element.12.alignment_first, ...), custom_call_target="tpu_custom_call" | custom-call | tf_op jit(solution)/shard_map/hand_out/pallas_call | solution.py:1032

commit v9 on v8

--- a/solution.py
+++ b/solution.py
@@ -411,8 +411,10 @@
     ):
         turned_one[...] = weight[...].T
 
+    own_four = source_row // 2
+
     def outer_step(k, carry):
-        n = (b // 2 + k) % 4
+        n = (own_four // 2 + k // 2) % 2 * 2 + (own_four % 2 + k % 2) % 2
 
         def msa_wait(part, carry):
             slot = 4 * n + part
@@ -776,7 +778,8 @@
                 ]
 
     def cot_step(step):
-        chips = [along_rows(a, GRID - 1 - 2 * step - n) for n in range(2)]
+        places = [2 * step + n for n in range(2)]
+        chips = [along_rows(a, (GRID - 1 - place) * other + place * h) for place in places]
         sequences = jnp.concatenate(
             [
                 msa_relayed[pl.ds(2 * chip, 2)].reshape(2 * 64, BLOCK * HIDDEN)

time: 90 us -> 90.2 us (level)
  no operation moved by 1% of the time
where the time goes in v9:
time: 90.2 us; the launch traced here: 90.1 us
  Pallas kernels  89.4 us (99%)
    pallas_call x1, Pallas kernels, pair_updates(): pl.pallas_call(pair_kernel, out_shape=(half_block, half_wide, whole_side,...  88.4 us

profile of v9, /device:TPU:1, one launch (start us, length us, event | category | flops | bytes accessed | tf_op | source)
XLA Modules:
  0.0 90.1 jit_solution(13136054050086788422)
XLA Ops:
  0.6 88.4 %pair_updates.1 = (bf16[8,16,128]{2,1,0:T(8,128)(2,1)S(1)}, f32[8,16,128]{2,1,0:T(8,128)S(1)}, f32[1024,128]{1,0:T(8,128)S(1)}, f32[1024,128]{1,0:T(8,128)S(1)}) custom-call(bf16[1024,256]{1,0:T(8,128)(2,1)} %bitcast.3, bf16[64,256]{1,0:T(8,128)(2,1)} %bitcast.4, bf16[8,16,128]{2,1,0:T(8,128)(2,1)} %pair_input.1, bf16[8,16,128]{2,1,0:T(8,128)(2,1)} %cotangent.1, ...), custom_call_target="tpu_custom_call" | custom-call | tf_op jit(solution)/shard_map/pair_updates/pallas_call | solution.py:894
  89.0 1.1 %hand_out.1 = (bf16[8,16,128]{2,1,0:T(8,128)(2,1)}, f32[8,16,128]{2,1,0:T(8,128)}, f32[1024,256]{1,0:T(8,128)}) custom-call(bf16[8,16,128]{2,1,0:T(8,128)(2,1)S(1)} %get-tuple-element.10.pair_output, f32[8,16,128]{2,1,0:T(8,128)S(1)} %get-tuple-element.11.pair_gradient, f32[1024,128]{1,0:T(8,128)S(1)} %get-tuple-element.12.alignment_first, ...), custom_call_target="tpu_custom_call" | custom-call | tf_op jit(solution)/shard_map/hand_out/pallas_call | solution.py:1035
